TPU v7x, 128 devices: a whole 4x4x4 slice. The times are simulated.
128 devices in a mesh: attn: 2 (over core), expert: 64 (over z, x, y).
Axes of the slice: x: 4, y: 4, z: 4, core: 2. Of those that a mesh axis runs over, the one named last changes fastest.
Arguments:
- queries: bfloat16 [1024, 36864], P(('attn', 'expert')), may hold values from -200 to 200, as said below
- new_latent: bfloat16 [1024, 576], P(('attn', 'expert')), may hold values from -6 to 6
- latent_cache: bfloat16 [2048, 36864], P(('attn', 'expert')), may hold values from -6 to 6
- block_table: int32 [128, 16], P(('attn', 'expert')), may hold values from 0 to 15, each once within a row
- lengths: int32 [128, 8], P(('attn', 'expert')), may hold values from 1 to 128, 576 in all within a row
- value_up: bfloat16 [64, 512, 128], P('expert'), may hold values from -0.25 to 0.25
- out_proj: bfloat16 [8192, 3584], P('expert'), may hold values from -0.0625 to 0.0625
- norm_gain: float32 [3584], replicated, may hold values from 0.1 to 1.9
- expert_ids: int32 [1024, 8], P(('attn', 'expert')), may hold values from 0 to 127, all different within a row; in each aligned block of 8 rows (0 to 7, 8 to 15, ...) at most 2 rows name the same one
- affinity: float32 [1024, 8], P(('attn', 'expert')), may hold values from 0.02 to 1
- gate_weight: bfloat16 [128, 3584, 1024], P('expert', None, 'attn'), may hold values from -0.09375 to 0.09375
- up_weight: bfloat16 [128, 3584, 1024], P('expert', None, 'attn'), may hold values from -0.09375 to 0.09375
- down_weight: bfloat16 [128, 1024, 3584], P('expert', 'attn'), may hold values from -0.1875 to 0.1875
Outputs:
- normed: bfloat16 [1024, 3584], P(('attn', 'expert'))
- expert_out: bfloat16 [1024, 3584], P(('attn', 'expert'))
Inputs may be any that keep to these rules, and one draw needn't show every extreme that they name: Absorbed queries; some heads of some tokens may carry large scales. `block_table`: each row lists every page of its device's pool once; sequence s of the device owns entries s * 2 to (s + 1) * 2 - 1, in position order. `lengths`: on each device the longest sequence holds exactly 128 cached entries. `expert_ids`: A token names 8 different experts; among the 8 tokens of one device no expert is named by more than 2 tokens, a bound that some block reaches.
All inputs are finite; a program needn't handle non-finite values.
Results may differ from a plain program's by a relative error of at most 0.022.
Values may be sent and summed in bfloat16 or wider, within the bound.
No kernel may reach another device: no remote copies, remote signals or barrier semaphores. Data moves between devices by JAX's collectives and lax.ppermute only.
A program may use at most 128 MiB of HBM per device.

v0:
```python
import jax
import jax.numpy as jnp
from jax import lax
from jax.sharding import PartitionSpec as P

SCORE_SCALE = 192.0 ** (-0.5)
ROUTED_SCALE = 2.5
EPSILON = 1e-06


def attend_rows(query_rows, fresh_latent, key_rows, live_count, kv_width):
    scores = (
        jnp.einsum("she,sje->shj", query_rows, key_rows, preferred_element_type=jnp.float32)
        * SCORE_SCALE
    )
    own_score = (
        jnp.einsum("she,se->sh", query_rows, fresh_latent, preferred_element_type=jnp.float32)
        * SCORE_SCALE
    )
    positions = jnp.arange(key_rows.shape[1], dtype=jnp.int32)
    live_mask = positions[None, None, :] < live_count[:, None, None]
    scores = jnp.where(live_mask, scores, -jnp.inf)
    highest = jnp.maximum(jnp.max(scores, axis=2), own_score)
    raised = jnp.exp(scores - highest[:, :, None])
    own_raised = jnp.exp(own_score - highest)
    denominator = jnp.sum(raised, axis=2) + own_raised
    weights = (raised / denominator[:, :, None]).astype(jnp.bfloat16)
    own_weight = (own_raised / denominator).astype(jnp.bfloat16)
    latent = jnp.einsum(
        "shj,sjc->shc", weights, key_rows[:, :, :kv_width], preferred_element_type=jnp.float32
    )
    latent = latent + own_weight.astype(jnp.float32)[:, :, None] * fresh_latent[
        :, None, :kv_width
    ].astype(jnp.float32)
    return latent.astype(jnp.bfloat16)


def expert_rows(arrived_rows, gate_weight, up_weight, down_weight):
    gate_proj = jnp.einsum(
        "secd,edf->secf", arrived_rows, gate_weight, preferred_element_type=jnp.float32
    )
    up_proj = jnp.einsum(
        "secd,edf->secf", arrived_rows, up_weight, preferred_element_type=jnp.float32
    )
    hidden = (jax.nn.silu(gate_proj) * up_proj).astype(jnp.bfloat16)
    return jnp.einsum("secf,efd->secd", hidden, down_weight, preferred_element_type=jnp.float32)


def shards(
    queries,
    new_latent,
    latent_cache,
    block_table,
    lengths,
    value_up,
    out_proj,
    norm_gain,
    expert_ids,
    affinity,
    gate_weight,
    up_weight,
    down_weight,
):
    seq_count, entry_width = new_latent.shape
    head_count = queries.shape[1] // entry_width
    kv_width = value_up.shape[1]
    pool_pages = latent_cache.shape[0]
    context = pool_pages // seq_count * (latent_cache.shape[1] // entry_width)
    key_rows = jnp.take(latent_cache, block_table.reshape(-1), axis=0).reshape(
        seq_count, context, entry_width
    )
    query_rows = queries.reshape(seq_count, head_count, entry_width)
    latent = attend_rows(query_rows, new_latent, key_rows, lengths.reshape(-1), kv_width)
    arrived = lax.all_to_all(latent, "expert", split_axis=1, concat_axis=0, tiled=True)
    values = jnp.einsum(
        "rhc,hcv->rhv", arrived, value_up, preferred_element_type=jnp.float32
    ).astype(jnp.bfloat16)
    values = values.reshape(values.shape[0], values.shape[1] * values.shape[2])
    attn_out = lax.psum_scatter(
        jnp.dot(values, out_proj, preferred_element_type=jnp.float32),
        "expert",
        scatter_dimension=0,
        tiled=True,
    )
    mean_square = jnp.mean(attn_out * attn_out, axis=1, keepdims=True)
    normed = (attn_out * lax.rsqrt(mean_square + EPSILON) * norm_gain).astype(jnp.bfloat16)
    chip_count = lax.axis_size("expert")
    copies = lax.axis_size("attn")
    local_experts = gate_weight.shape[0]
    expert_count = chip_count * local_experts
    top_count = expert_ids.shape[1]
    capacity = max(2, 2 * seq_count * top_count // expert_count)
    model_width = normed.shape[1]
    pair_ids = expert_ids.reshape(-1)
    onehot = (pair_ids[:, None] == jnp.arange(expert_count, dtype=jnp.int32)[None, :]).astype(
        jnp.int32
    )
    slot_rank = jnp.sum((jnp.cumsum(onehot, axis=0) - 1) * onehot, axis=1)
    slot_index = pair_ids * capacity + slot_rank
    slot_table = slot_index.reshape(seq_count, top_count)
    slot_numbers = jnp.arange(expert_count * capacity, dtype=jnp.int32)
    placement = jnp.any(slot_table[None, :, :] == slot_numbers[:, None, None], axis=2).astype(
        jnp.bfloat16
    )
    outgoing = jnp.dot(placement, normed, preferred_element_type=jnp.float32).astype(jnp.bfloat16)
    outgoing = outgoing.reshape(chip_count, local_experts, capacity, model_width)
    doubled = jnp.concatenate([outgoing] * copies, axis=0)
    received = lax.all_to_all(doubled, ("attn", "expert"), split_axis=0, concat_axis=0, tiled=True)
    partial_value = expert_rows(received, gate_weight, up_weight, down_weight)
    returned = lax.all_to_all(
        partial_value.astype(jnp.bfloat16),
        ("attn", "expert"),
        split_axis=0,
        concat_axis=0,
        tiled=True,
    ).astype(partial_value.dtype)
    returned = returned.reshape(copies, chip_count, local_experts, capacity, model_width)
    expert_back = jnp.sum(returned, axis=0).astype(jnp.bfloat16)
    returned_rows = expert_back.reshape(expert_count * capacity, model_width)
    picked = jnp.take(returned_rows, slot_index, axis=0).reshape(seq_count, top_count, model_width)
    route_weight = affinity / jnp.sum(affinity, axis=1, keepdims=True) * ROUTED_SCALE
    expert_out = jnp.sum(route_weight[:, :, None] * picked.astype(jnp.float32), axis=1).astype(
        jnp.bfloat16
    )
    return (normed, expert_out)


def solution(mesh):
    placed = (
        P(("attn", "expert"), None),
        P(("attn", "expert"), None),
        P(("attn", "expert"), None),
        P(("attn", "expert"), None),
        P(("attn", "expert"), None),
        P("expert", None, None),
        P("expert", None),
        P(),
        P(("attn", "expert"), None),
        P(("attn", "expert"), None),
        P("expert", None, "attn"),
        P("expert", None, "attn"),
        P("expert", "attn", None),
    )
    return jax.shard_map(
        shards,
        mesh=mesh,
        in_specs=placed,
        out_specs=(P(("attn", "expert"), None), P(("attn", "expert"), None)),
        check_vma=False,
    )
```

profile of v0, /device:TPU:1, one launch (start us, length us, event | category | flops | bytes accessed | tf_op | source)
XLA Modules:
  0.0 562.8 jit_solution(7105561419328449737)
XLA Ops:
  7.2 0.0 copy-start
  7.2 0.0 reduce-scatter.2.cloned.1.call-start
  7.2 0.7 fusion.52
  8.0 0.5 copy-done
  8.5 2.3 gather_fusion
  10.8 2.7 gather.13
  13.5 0.5 broadcast.153
  14.0 0.0 copy-done.8
  14.0 0.7 reduce.4
  14.7 0.1 reshape.165
  14.8 0.1 broadcast_in_dim.48
  14.8 0.1 broadcast_in_dim.49
  14.9 1.9 reshape.167
  16.8 0.0 copy-done.9
  16.8 0.1 iota_compare_fusion.2
  16.9 0.0 copy-done.7
  16.9 0.2 broadcast_select_fusion
  17.1 0.3 fusion.48
  17.4 0.7 fusion.56
  18.2 0.0 copy-start.1
  18.2 0.3 fusion.41
  18.5 0.4 fusion.34
  18.9 0.3 copy.30
  19.2 23.7 %all_to_all.25 = bf16[8,64,512]{2,0,1:T(8,128)(2,1)S(1)} all-to-all(bf16[8,64,512]{2,0,1:T(8,128)(2,1)S(1)} %copy.30), channel_id=1, replica_groups=mesh['attn'=2,'expert'=64] {'expert'}, dimensions={1} | all-to-all | bytes 1048576 | tf_op jit(solution)/shard_map/all_to_all | solution.py:74
  42.9 0.0 copy-done.3
  42.9 0.0 copy-done.1
  42.9 4.5 fusion.37
  47.4 0.0 reduce-scatter.2.cloned.1.call-update
  47.4 0.7 copy-done.4
  48.0 0.1 reshape.170
  48.1 0.1 fusion.47
  48.2 0.1 reduce_window_sum.11
  48.3 0.2 select_reduce_fusion
  48.5 0.1 reduce_sum.62
  48.6 0.1 fusion.46
  48.7 314.2 %reduce-scatter.2.cloned.1.call-done = f32[8,3584]{1,0:T(8,128)} async-done(((f32[512,3584]{1,0:T(8,128)}), f32[8,3584]{1,0:T(8,128)}) %reduce-scatter.2.cloned.1.call-update) | async-done | bytes 114704 | tf_op jit(solution)/shard_map/reduce_scatter | solution.py:79
  362.9 1.0 multiply_reduce_fusion.1
  363.9 0.0 copy-done.5
  364.0 1.0 multiply_convert_fusion
  364.9 0.0 copy-start.2
  365.0 0.7 convolution_convert_fusion
  365.6 1.7 reshape.171
  367.3 6.8 %pad_maximum_fusion = bf16[128,2,2,3584]{3,2,1,0:T(2,128)(2,1)S(1)} fusion(bf16[64,2,2,3584]{3,2,1,0:T(2,128)(2,1)} %reshape.171), kind=kLoop, calls=%fused_computation.11 | loop fusion | flops 1835008 | bytes 5505024 | tf_op jit(solution)/shard_map/concatenate | solution.py:107
  374.1 0.0 copy-done.2
  374.1 0.0 slice-start.2
  374.1 97.1 %all_to_all.26 = bf16[128,2,2,3584]{3,2,1,0:T(2,128)(2,1)S(1)} all-to-all(bf16[128,2,2,3584]{3,2,1,0:T(2,128)(2,1)S(1)} %pad_maximum_fusion), channel_id=1, replica_groups=mesh['attn'=2,'expert'=64] {'attn','expert'}, dimensions={0} | all-to-all | bytes 7340032 | tf_op jit(solution)/shard_map/all_to_all | solution.py:108
  471.2 5.3 fusion.14
  476.5 0.0 slice-done.2
  476.5 0.0 slice-start.1
  476.5 2.2 fusion.29
  478.7 0.0 slice-done
  478.7 0.0 slice-done.1
  478.8 2.1 fusion.9
  480.8 5.6 copy.33
  486.5 8.4 %all-to-all-start.2 = ((bf16[128,2,2,3584]{3,2,1,0:T(2,128)(2,1)}), bf16[128,2,2,3584]{3,2,1,0:T(2,128)(2,1)}, u32[]{:S(2)}, u32[]{:S(2)}) async-start(bf16[128,2,2,3584]{3,2,1,0:T(2,128)(2,1)} %copy.33), calls=%async_computation.3 | async-start | bytes 7340032 | tf_op jit(solution)/shard_map/all_to_all | solution.py:110
  494.8 0.1 mul.110
  494.9 0.0 copy-done.6
  494.9 0.1 reduce_sum.60
  495.0 0.1 divide_multiply_fusion
  495.1 45.8 %all-to-all-done.2 = bf16[128,2,2,3584]{3,2,1,0:T(2,128)(2,1)} async-done(((bf16[128,2,2,3584]{3,2,1,0:T(2,128)(2,1)}), bf16[128,2,2,3584]{3,2,1,0:T(2,128)(2,1)}, u32[]{:S(2)}, u32[]{:S(2)}) %all-to-all-start.2) | async-done | bytes 3670048 | tf_op jit(solution)/shard_map/all_to_all | solution.py:110
  540.9 9.2 %reduce = bf16[64,2,2,3584]{3,2,1,0:T(2,128)(2,1)} reduce(bf16[2,64,2,2,3584]{4,3,2,1,0:T(2,128)(2,1)} %bitcast.20, bf16[]{:T(256)} %constant.70), dimensions={0}, to_apply=%region_8.9.clone | reduce | flops 917504 | bytes 5505026 | tf_op jit(solution)/shard_map/reduce_sum | solution.py:118
  550.1 4.1 convert_element_type.68
  554.2 0.8 gather_fusion.1
  555.0 1.0 multiply_reduce_fusion
  (22 shorter events, 0.1 us)
Async XLA Ops:
  7.2 1.3 copy-start
  7.2 355.7 %reduce-scatter.2.cloned.1.call-start = ((), (), s32[]{:S(2)}) async-start(), calls=%async_computation.4 | async-start | bytes 7454720 | tf_op jit(solution)/shard_map/reduce_scatter | solution.py:79
  8.5 5.5 copy-start.8
  10.8 6.0 %copy-start.9 = (s32[1,8]{1,0:T(1,128)S(1)}, s32[1,8]{1,0:T(1,128)}, u32[]{:S(2)}) copy-start(s32[1,8]{1,0:T(1,128)} %param.17) | copy-start | bytes 100
  10.8 6.1 %copy-start.7 = (bf16[8,576]{1,0:T(8,128)(2,1)S(1)}, bf16[8,576]{1,0:T(8,128)(2,1)}, u32[]{:S(2)}) copy-start(bf16[8,576]{1,0:T(8,128)(2,1)} %param.14) | copy-start | bytes 27652
  17.4 25.4 %copy-start.3 = (bf16[1,512,128]{2,1,0:T(8,128)(2,1)S(1)}, bf16[1,512,128]{2,1,0:T(8,128)(2,1)}, u32[]{:S(2)}) copy-start(bf16[1,512,128]{2,1,0:T(8,128)(2,1)} %param.18) | copy-start | bytes 393220
  18.2 24.7 %copy-start.1 = (bf16[128,3584]{1,0:T(8,128)(2,1)S(1)}, bf16[128,3584]{1,0:T(8,128)(2,1)}, u32[]{:S(2)}) copy-start(bf16[128,3584]{1,0:T(8,128)(2,1)} %param.19) | copy-start | bytes 2752516
  47.4 0.7 copy-start.4
  47.4 316.6 %copy-start.5 = (f32[3584]{0:T(1024)S(1)}, f32[3584]{0:T(1024)}, u32[]{:S(2)}) copy-start(f32[3584]{0:T(1024)} %param.20) | copy-start | bytes 43012
  364.9 9.2 %copy-start.2 = (bf16[8,3584]{1,0:T(8,128)(2,1)}, bf16[8,3584]{1,0:T(8,128)(2,1)S(1)}, u32[]{:S(2)}) copy-start(bf16[8,3584]{1,0:T(8,128)(2,1)S(1)} %multiply_convert_fusion) | copy-start | bytes 172036
  374.1 102.4 %slice-start.2 = ((s8[7340032]{0:T(1024)(128)(4,1)}), s8[4194304]{0:T(1024)(128)(4,1)S(1)}, s32[]{:S(2)}) async-start(s8[7340032]{0:T(1024)(128)(4,1)} %bitcast.82), calls=%async_computation.7 | async-start | bytes 8388608
  471.2 5.3 slice-start.3
  471.2 7.5 %slice-start = ((s8[7340032]{0:T(1024)(128)(4,1)}), s8[4194304]{0:T(1024)(128)(4,1)S(1)}, s32[]{:S(2)}) async-start(s8[7340032]{0:T(1024)(128)(4,1)} %bitcast.77), calls=%async_computation.5 | async-start | bytes 8388608
  476.5 2.2 slice-start.1
  486.5 8.5 %copy-start.6 = (f32[8,8]{1,0:T(8,128)S(1)}, f32[8,8]{1,0:T(8,128)}, u32[]{:S(2)}) copy-start(f32[8,8]{1,0:T(8,128)} %param.22) | copy-start | bytes 772
  486.5 54.5 %all-to-all-start.2 = ((bf16[128,2,2,3584]{3,2,1,0:T(2,128)(2,1)}), bf16[128,2,2,3584]{3,2,1,0:T(2,128)(2,1)}, u32[]{:S(2)}, u32[]{:S(2)}) async-start(bf16[128,2,2,3584]{3,2,1,0:T(2,128)(2,1)} %copy.33), calls=%async_computation.3 | async-start | bytes 7340032 | tf_op jit(solution)/shard_map/all_to_all | solution.py:110
Sparse Core Ops, SparseCore 0:
  47.5 315.3 reduce-scatter.1
where the time goes:
time: 564 us; the launch traced here: 563 us
  waiting for transfers between devices  360 us (64%)
  blocking collectives  121 us (21%)
  other arithmetic  21.7 us (4%)
  local copies, waits for them, and re-layouts  21.5 us (4%)
  matrix products  16.1 us (3%)
  between operations  14.3 us (3%)
  starting transfers between devices  8.39 us (1%)
    reduce_scatter x1, waiting for transfers between devices, shards(): lax.psum_scatter(jnp.dot(values, out_proj, preferred_element_type=jnp.flo...  314 us
    all_to_all x1, blocking collectives, shards(): lax.all_to_all(doubled, ('attn', 'expert'), split_axis=0, concat_axis=0,...  97.1 us
    all_to_all x1, waiting for transfers between devices, shards(): lax.all_to_all(partial_value.astype(jnp.bfloat16), ('attn', 'expert'), sp...  45.8 us
    all_to_all x1, blocking collectives, shards(): lax.all_to_all(latent, 'expert', split_axis=1, concat_axis=0, tiled=True)  23.7 us
  transfers between devices with their start and end apart: 2, of which 2 were waited for; matrix products, arithmetic and copies ran while one was open for 0% of the time, Pallas kernels for 0%

commit v1 on v0

v1 whole, which is shorter than its diff:
```python
import jax
import jax.numpy as jnp
from jax import lax
from jax.sharding import Mesh, PartitionSpec as P

SCORE_SCALE = 192.0 ** (-0.5)
ROUTED_SCALE = 2.5
EPSILON = 1e-06
SIDE = 4
CHIPS = ("z", "x", "y")
SWAP = [(0, 1), (1, 0)]


def attend_rows(query_rows, fresh_latent, key_rows, live_count, kv_width):
    scores = (
        jnp.einsum("she,sje->shj", query_rows, key_rows, preferred_element_type=jnp.float32)
        * SCORE_SCALE
    )
    own_score = (
        jnp.einsum("she,se->sh", query_rows, fresh_latent, preferred_element_type=jnp.float32)
        * SCORE_SCALE
    )
    positions = jnp.arange(key_rows.shape[1], dtype=jnp.int32)
    live_mask = positions[None, None, :] < live_count[:, None, None]
    scores = jnp.where(live_mask, scores, -jnp.inf)
    highest = jnp.maximum(jnp.max(scores, axis=2), own_score)
    raised = jnp.exp(scores - highest[:, :, None])
    own_raised = jnp.exp(own_score - highest)
    denominator = jnp.sum(raised, axis=2) + own_raised
    weights = (raised / denominator[:, :, None]).astype(jnp.bfloat16)
    own_weight = (own_raised / denominator).astype(jnp.bfloat16)
    latent = jnp.einsum(
        "shj,sjc->shc", weights, key_rows[:, :, :kv_width], preferred_element_type=jnp.float32
    )
    latent = latent + own_weight.astype(jnp.float32)[:, :, None] * fresh_latent[
        :, None, :kv_width
    ].astype(jnp.float32)
    return latent.astype(jnp.bfloat16)


def along_y(array, step):
    return lax.ppermute(array, "y", [(i, (i + step) % SIDE) for i in range(SIDE)])


def other_core(array):
    return lax.ppermute(array, "core", SWAP)


def expert_rows(arrived_rows, gate_weight, up_weight, down_weight):
    gate_proj = jnp.einsum(
        "secd,edf->secf", arrived_rows, gate_weight, preferred_element_type=jnp.float32
    )
    up_proj = jnp.einsum(
        "secd,edf->secf", arrived_rows, up_weight, preferred_element_type=jnp.float32
    )
    hidden = (jax.nn.silu(gate_proj) * up_proj).astype(jnp.bfloat16)
    return jnp.einsum("secf,efd->secd", hidden, down_weight, preferred_element_type=jnp.float32)


def shards(
    queries,
    new_latent,
    latent_cache,
    block_table,
    lengths,
    value_up,
    out_proj,
    norm_gain,
    expert_ids,
    affinity,
    gate_weight,
    up_weight,
    down_weight,
):
    seq_count, entry_width = new_latent.shape
    head_count = queries.shape[1] // entry_width
    kv_width = value_up.shape[1]
    pool_pages = latent_cache.shape[0]
    context = pool_pages // seq_count * (latent_cache.shape[1] // entry_width)
    model_width = out_proj.shape[1]
    half = model_width // 2
    core = lax.axis_index("core")
    place_y = lax.axis_index("y")
    planes = head_count // SIDE

    part = lax.dynamic_slice_in_dim(out_proj, core * half, half, 1)
    mine = [along_y(part, k) for k in range(1, SIDE)]
    theirs = [other_core(m) for m in mine]
    ups = [value_up[0]] + [along_y(value_up[0], k) for k in range(1, SIDE)]

    key_rows = jnp.take(latent_cache, block_table.reshape(-1), axis=0).reshape(
        seq_count, context, entry_width
    )
    query_rows = queries.reshape(seq_count, head_count, entry_width)
    latent = attend_rows(query_rows, new_latent, key_rows, lengths.reshape(-1), kv_width)
    outbound = jnp.transpose(latent, (1, 0, 2)).reshape(planes, SIDE * seq_count, kv_width)
    arrived = lax.all_to_all(outbound, ("z", "x"), split_axis=0, concat_axis=0, tiled=True)
    arrived = arrived.reshape(planes, SIDE, seq_count, kv_width)
    total = jnp.zeros((planes * seq_count, model_width), jnp.float32)
    for k in range(SIDE):
        rows = lax.dynamic_index_in_dim(
            arrived, lax.rem(place_y - k + SIDE, SIDE), 1, keepdims=False
        ).reshape(planes * seq_count, kv_width)
        values = jnp.dot(rows, ups[k], preferred_element_type=jnp.float32).astype(jnp.bfloat16)
        if k == 0:
            weight = out_proj
        else:
            first = jnp.where(core == 0, mine[k - 1], theirs[k - 1])
            second = jnp.where(core == 0, theirs[k - 1], mine[k - 1])
            weight = jnp.concatenate([first, second], axis=1)
        total = total + jnp.dot(values, weight, preferred_element_type=jnp.float32)
    partial = total.astype(jnp.bfloat16).reshape(planes, seq_count, model_width)
    collected = lax.all_to_all(partial, ("z", "x"), split_axis=0, concat_axis=0, tiled=True)
    attn_out = jnp.sum(collected.astype(jnp.float32), axis=0)
    mean_square = jnp.mean(attn_out * attn_out, axis=1, keepdims=True)
    normed = (attn_out * lax.rsqrt(mean_square + EPSILON) * norm_gain).astype(jnp.bfloat16)

    chip_count = SIDE**3
    local_experts = gate_weight.shape[0]
    expert_count = chip_count * local_experts
    top_count = expert_ids.shape[1]
    capacity = max(2, 2 * seq_count * top_count // expert_count)
    pair_ids = expert_ids.reshape(-1)
    onehot = (pair_ids[:, None] == jnp.arange(expert_count, dtype=jnp.int32)[None, :]).astype(
        jnp.int32
    )
    slot_rank = jnp.sum((jnp.cumsum(onehot, axis=0) - 1) * onehot, axis=1)
    slot_index = pair_ids * capacity + slot_rank
    slot_table = slot_index.reshape(seq_count, top_count)
    slot_numbers = jnp.arange(expert_count * capacity, dtype=jnp.int32)
    placement = jnp.any(slot_table[None, :, :] == slot_numbers[:, None, None], axis=2).astype(
        jnp.bfloat16
    )
    outgoing = jnp.dot(placement, normed, preferred_element_type=jnp.float32).astype(jnp.bfloat16)
    outgoing = outgoing.reshape(chip_count, local_experts * capacity, model_width)
    received = lax.all_to_all(outgoing, CHIPS, split_axis=0, concat_axis=0, tiled=True)
    both = jnp.concatenate([received, other_core(received)], axis=0)
    both = both.reshape(2 * chip_count, local_experts, capacity, model_width)
    partial_value = expert_rows(both, gate_weight, up_weight, down_weight)
    partial_value = partial_value.reshape(2, chip_count, local_experts * capacity, model_width)
    beside = other_core(partial_value[1].astype(jnp.bfloat16))
    reply = (partial_value[0] + beside.astype(jnp.float32)).astype(jnp.bfloat16)
    returned = lax.all_to_all(reply, CHIPS, split_axis=0, concat_axis=0, tiled=True)
    returned_rows = returned.reshape(expert_count * capacity, model_width)
    picked = jnp.take(returned_rows, slot_index, axis=0).reshape(seq_count, top_count, model_width)
    route_weight = affinity / jnp.sum(affinity, axis=1, keepdims=True) * ROUTED_SCALE
    expert_out = jnp.sum(route_weight[:, :, None] * picked.astype(jnp.float32), axis=1).astype(
        jnp.bfloat16
    )
    return (normed, expert_out)


def solution(mesh):
    grid = Mesh(mesh.devices.reshape(2, SIDE, SIDE, SIDE), ("core",) + CHIPS)
    rows = P(("core",) + CHIPS, None)
    placed = (
        rows,
        rows,
        rows,
        rows,
        rows,
        P(CHIPS, None, None),
        P(CHIPS, None),
        P(),
        rows,
        rows,
        P(CHIPS, None, "core"),
        P(CHIPS, None, "core"),
        P(CHIPS, "core", None),
    )
    return jax.shard_map(
        shards, mesh=grid, in_specs=placed, out_specs=(rows, rows), check_vma=False
    )
```

time: 564 us -> 187 us (0.33)
  waiting for transfers between devices: 360 us -> 48.5 us
  blocking collectives: 121 us -> 34.4 us
  starting transfers between devices: 8.39 us -> 45.5 us
  between operations: 14.3 us -> 1.07 us
  other arithmetic: 21.7 us -> 15.7 us
    reduce_scatter x1 -> x0, waiting for transfers between devices: 314 us -> none  [shards(): lax.psum_scatter(jnp.dot(values, out_proj, preferred_element_type=jnp.flo...]
    all_to_all x2 -> x1, blocking collectives: 121 us -> 34.4 us  [shards(): lax.all_to_all(outgoing, CHIPS, split_axis=0, concat_axis=0, tiled=True)]
    ppermute x0 -> x11, starting transfers between devices: none -> 25.5 us  [the longest x5 14.8 us: other_core(): return lax.ppermute(array, 'core', SWAP)]
    all_to_all x1 -> x3, starting transfers between devices: 8.35 us -> 20 us  [the longest x1 7.59 us: shards(): lax.all_to_all(outbound, ('z', 'x'), split_axis=0, concat_axis=0, tiled=T...]
    reduce_sum x1, other arithmetic: 9.19 us -> 0.12 us  [shards(): attn_out = jnp.sum(collected.astype(jnp.float32), axis=0)]
    convert_element_type x2 -> x1, local copies, waits for them, and re-layouts: 9.66 us -> 1.42 us  [shards(): beside = other_core(partial_value[1].astype(jnp.bfloat16))]
    ppermute x0 -> x11, waiting for transfers between devices: none -> 6.59 us  [the longest x5 6.58 us: other_core(): return lax.ppermute(array, 'core', SWAP)]
    all_to_all x1 -> x3, waiting for transfers between devices: 45.8 us -> 41.9 us  [the longest x1 25 us: shards(): lax.all_to_all(reply, CHIPS, split_axis=0, concat_axis=0, tiled=True)]
  transfers between devices with their start and end apart: 2 -> 14, of which waited for: 2 -> 5; matrix products, arithmetic and copies ran while one was open for 0% -> 13% of each run, Pallas kernels for 0% -> 0%
where the time goes in v1:
time: 187 us; the launch traced here: 185 us
  waiting for transfers between devices  48.5 us (26%)
  starting transfers between devices  45.5 us (24%)
  blocking collectives  34.4 us (18%)
  local copies, waits for them, and re-layouts  20.4 us (11%)
  matrix products  19.2 us (10%)
  other arithmetic  15.7 us (8%)
    all_to_all x1, blocking collectives, shards(): lax.all_to_all(outgoing, CHIPS, split_axis=0, concat_axis=0, tiled=True)  34.4 us
    all_to_all x1, waiting for transfers between devices, shards(): lax.all_to_all(reply, CHIPS, split_axis=0, concat_axis=0, tiled=True)  25 us
    ppermute x5, starting transfers between devices, other_core(): return lax.ppermute(array, 'core', SWAP)  14.8 us
    all_to_all x1, waiting for transfers between devices, shards(): lax.all_to_all(partial, ('z', 'x'), split_axis=0, concat_axis=0, tiled=True)  14.2 us
    ppermute x6, starting transfers between devices, along_y(): lax.ppermute(array, 'y', [(i, (i + step) % SIDE) for i in range(SIDE)])  10.7 us
    dot_general x4, matrix products, shards(): total = total + jnp.dot(values, weight, preferred_element_type=jnp.float32)  9.56 us
    all_to_all x1, starting transfers between devices, shards(): lax.all_to_all(outbound, ('z', 'x'), split_axis=0, concat_axis=0, tiled=T...  7.59 us
    ppermute x5, waiting for transfers between devices, other_core(): return lax.ppermute(array, 'core', SWAP)  6.58 us
  transfers between devices with their start and end apart: 14, of which 5 were waited for; matrix products, arithmetic and copies ran while one was open for 13% of the time, Pallas kernels for 0%

profile of v1, /device:TPU:1, one launch (start us, length us, event | category | flops | bytes accessed | tf_op | source)
XLA Modules:
  0.0 184.8 jit_solution(9825726144627224024)
XLA Ops:
  0.7 1.1 constant_dynamic-slice_fusion
  1.8 2.2 %collective-permute-start.1 = (bf16[128,1792]{1,0:T(8,128)(2,1)S(1)}, bf16[128,1792]{1,0:T(8,128)(2,1)}, u32[]{:S(2)}, u32[]{:S(2)}) collective-permute-start(bf16[128,1792]{1,0:T(8,128)(2,1)S(1)} %constant_dynamic-slice_fusion), channel_id=1, source_target_pairs={{0,1},{1,2},{2,3},{3,0},{4,5},{5,6},{6,7},{7,4},{8,9},{9,10},{10,1... | collective-permute-start | bytes 1376264 | tf_op jit(solution)/shard_map/ppermute | solution.py:42
  4.0 0.7 fusion.70
  4.7 2.4 %gather_fusion = bf16[16,36864]{1,0:T(8,128)(2,1)} fusion(bf16[16,36864]{1,0:T(8,128)(2,1)S(1)} %copy-done, s32[1024]{0:T(1024)S(1)} %pad_clamp_fusion.1), kind=kCustom, calls=%fused_computation | custom fusion | bytes 2359360 | tf_op jit(solution)/shard_map/jit(_take)/gather | solution.py:91
  7.0 2.7 %gather.13 = bf16[8,128,576]{2,1,0:T(8,128)(2,1)S(1)} reshape(bf16[16,36864]{1,0:T(8,128)(2,1)} %gather_fusion) | data formatting | bytes 2359296 | tf_op jit(solution)/shard_map/jit(_take)/gather | solution.py:91
  9.8 0.5 broadcast.161
  10.3 0.7 reduce.3
  10.9 0.1 reshape.183
  11.1 0.1 broadcast_in_dim.49
  11.2 0.8 reshape.185
  12.1 0.2 broadcast_select_fusion
  12.4 0.3 fusion.57
  12.7 0.7 fusion.80
  13.4 0.3 fusion.36
  13.8 0.4 fusion.20
  14.2 1.1 copy.28
  15.2 7.6 %all-to-all-start = ((bf16[16,32,512]{2,1,0:T(8,128)(2,1)}), bf16[16,32,512]{2,1,0:T(8,128)(2,1)S(1)}, u32[]{:S(2)}, u32[]{:S(2)}) async-start(bf16[16,32,512]{2,1,0:T(8,128)(2,1)} %bitcast.11), calls=%async_computation | async-start | bytes 1048576 | tf_op jit(solution)/shard_map/all_to_all | solution.py:97
  22.8 1.5 collective-permute-start.7
  24.4 1.6 collective-permute-start.4
  26.0 1.8 collective-permute-start.2
  27.8 0.4 collective-permute-start
  28.2 2.3 %collective-permute-start.6 = (bf16[512,128]{1,0:T(8,128)(2,1)S(1)}, bf16[512,128]{1,0:T(8,128)(2,1)}, u32[]{:S(2)}, u32[]{:S(2)}) collective-permute-start(bf16[512,128]{1,0:T(8,128)(2,1)S(1)} %bitcast.120), channel_id=1, source_target_pairs={{0,3},{1,0},{2,1},{3,2},{4,7},{5,4},{6,5},{7,6},{8,11},{9,8},{10,9... | collective-permute-start | bytes 393224 | tf_op jit(solution)/shard_map/ppermute | solution.py:42
  30.5 2.7 %all-to-all-done = bf16[16,32,512]{2,1,0:T(8,128)(2,1)S(1)} async-done(((bf16[16,32,512]{2,1,0:T(8,128)(2,1)}), bf16[16,32,512]{2,1,0:T(8,128)(2,1)S(1)}, u32[]{:S(2)}, u32[]{:S(2)}) %all-to-all-start) | async-done | bytes 524320 | tf_op jit(solution)/shard_map/all_to_all | solution.py:97
  33.2 1.7 fusion.23
  34.9 2.7 %collective-permute-start.3 = (bf16[512,128]{1,0:T(8,128)(2,1)S(1)}, bf16[512,128]{1,0:T(8,128)(2,1)}, u32[]{:S(2)}, u32[]{:S(2)}) collective-permute-start(bf16[512,128]{1,0:T(8,128)(2,1)S(1)} %bitcast.121), channel_id=1, source_target_pairs={{0,2},{1,3},{2,0},{3,1},{4,6},{5,7},{6,4},{7,5},{8,10},{9,11},{10,... | collective-permute-start | bytes 393224 | tf_op jit(solution)/shard_map/ppermute | solution.py:42
  37.6 9.3 %collective-permute-start.8 = (bf16[128,1792]{1,0:T(8,128)(2,1)}, bf16[128,1792]{1,0:T(8,128)(2,1)S(1)}, u32[]{:S(2)}, u32[]{:S(2)}) collective-permute-start(bf16[128,1792]{1,0:T(8,128)(2,1)} %collective-permute-done.7), channel_id=1, source_target_pairs={{0,64},{64,0},{1,65},{65,1},{2,66},{66,2},{3,67},{67,3},{4,68},{68... | collective-permute-start | bytes 1376264 | tf_op jit(solution)/shard_map/ppermute | solution.py:46
  47.0 0.1 collective-permute-start.5
  47.1 2.2 %broadcast_select_fusion.6 = (bf16[128,1792]{1,0:T(8,128)(2,1)}, bf16[128,1792]{1,0:T(8,128)(2,1)}) fusion(bf16[128,1792]{1,0:T(8,128)(2,1)} %collective-permute-done.1, bf16[128,1792]{1,0:T(8,128)(2,1)} %collective-permute-done.2, pred[]{:T(512)S(6)} %eq.14), kind=kLoop, calls=%fused_computation.54 | loop fusion | flops 458752 | bytes 1835009 | tf_op jit(solution)/shard_map/jit(_where)/select_n | solution.py:108
  49.2 2.0 %broadcast_select_fusion.2 = (bf16[128,1792]{1,0:T(8,128)(2,1)}, bf16[128,1792]{1,0:T(8,128)(2,1)}) fusion(bf16[128,1792]{1,0:T(8,128)(2,1)} %collective-permute-done.7, bf16[128,1792]{1,0:T(8,128)(2,1)S(1)} %collective-permute-done.8, pred[]{:T(512)S(6)} %eq.14), kind=kLoop, calls=%fused_computation.50 | loop fusion | flops 458752 | bytes 1835009 | tf_op jit(solution)/shard_map/jit(_where)/select_n | solution.py:108
  51.3 1.1 broadcast_select_fusion.4
  52.4 3.0 %convolution_add_fusion.1 = f32[128,3584]{1,0:T(8,128)} fusion(f32[128,3584]{1,0:T(8,128)S(1)} %fusion.23, bf16[512,128]{1,0:T(8,128)(2,1)} %collective-permute-done, bf16[128,1792]{1,0:T(8,128)(2,1)} %get-tuple-element.7, bf16[128,1792]{1,0:T(8,128)(2,1)} %get-tuple-element.6, bf16[16,4,8,512]{3,2,1,0:T(8,128)(2,1)S(1)} %bitcast.116, s32[]{:T(128)S(6)} %select_n.101), kind=kOutput, calls=%fused_computation.12 | convolution fusion | flops 136527872 | bytes 4849668 | tf_op jit(solution)/shard_map/dot_general | solution.py:111
  55.4 1.8 fusion.24
  57.2 3.1 %fusion.11 = bf16[16,8,3584]{2,1,0:T(8,128)(2,1)} fusion(f32[128,3584]{1,0:T(8,128)S(1)} %fusion.24, f32[128,3584]{1,0:T(8,128)} %convolution_add_fusion.1, bf16[512,128]{1,0:T(8,128)(2,1)} %collective-permute-done.3, bf16[128,1792]{1,0:T(8,128)(2,1)S(1)} %get-tuple-element.5, bf16[128,1792]{1,0:T(8,128)(2,1)S(1)} %get-tuple-element.4, ...), kind=kOutput, calls=%fused_computation.14 | convolution fusion | flops 137445376 | bytes 5767172 | tf_op jit(solution)/shard_map/dot_general | solution.py:111
  60.2 6.4 %all-to-all-start.1 = ((bf16[16,8,3584]{2,1,0:T(8,128)(2,1)}), bf16[16,8,3584]{2,1,0:T(8,128)(2,1)S(1)}, u32[]{:S(2)}, u32[]{:S(2)}) async-start(bf16[16,8,3584]{2,1,0:T(8,128)(2,1)} %fusion.11), calls=%async_computation.1 | async-start | bytes 1835008 | tf_op jit(solution)/shard_map/all_to_all | solution.py:113
  66.9 0.1 reduce_window_sum.11
  67.0 0.2 select_reduce_fusion
  67.2 0.1 fusion.55
  67.3 14.2 %all-to-all-done.1 = bf16[16,8,3584]{2,1,0:T(8,128)(2,1)S(1)} async-done(((bf16[16,8,3584]{2,1,0:T(8,128)(2,1)}), bf16[16,8,3584]{2,1,0:T(8,128)(2,1)S(1)}, u32[]{:S(2)}, u32[]{:S(2)}) %all-to-all-start.1) | async-done | bytes 917536 | tf_op jit(solution)/shard_map/all_to_all | solution.py:113
  81.6 0.1 convert_reduce_fusion
  81.7 0.1 multiply_reduce_fusion.1
  81.8 0.1 multiply_convert_fusion.2
  81.9 2.0 %convolution_convert_fusion = bf16[256,3584]{1,0:T(8,128)(2,1)} fusion(pred[256,8]{0,1:T(8,128)(4,1)S(1)} %fusion.55, bf16[8,3584]{1,0:T(8,128)(2,1)S(1)} %multiply_convert_fusion.2), kind=kOutput, calls=%fused_computation.9 | convolution fusion | flops 15597568 | bytes 1894400 | tf_op jit(solution)/shard_map/dot_general | solution.py:134
  83.9 3.1 %reshape.194 = bf16[64,4,3584]{2,1,0:T(4,128)(2,1)S(1)} reshape(bf16[256,3584]{1,0:T(8,128)(2,1)} %convolution_convert_fusion) | data formatting | bytes 3670016 | tf_op jit(solution)/shard_map/reshape | solution.py:135
  87.1 34.4 %all_to_all.20 = bf16[64,4,3584]{2,1,0:T(4,128)(2,1)S(1)} all-to-all(bf16[64,4,3584]{2,1,0:T(4,128)(2,1)S(1)} %reshape.194), channel_id=1, replica_groups=mesh['core'=2,'z'=4,'x'=4,'y'=4] {'z','x','y'}, dimensions={0} | all-to-all | bytes 3670016 | tf_op jit(solution)/shard_map/all_to_all | solution.py:136
  121.5 2.9 %collective-permute-start.9 = (bf16[64,4,3584]{2,1,0:T(4,128)(2,1)S(1)}, bf16[64,4,3584]{2,1,0:T(4,128)(2,1)S(1)}, u32[]{:S(2)}, u32[]{:S(2)}) collective-permute-start(bf16[64,4,3584]{2,1,0:T(4,128)(2,1)S(1)} %all_to_all.20), channel_id=1, source_target_pairs={{0,64},{64,0},{1,65},{65,1},{2,66},{66,2},{3,67},{67,3},{4,68},{68... | collective-permute-start | bytes 5505032 | tf_op jit(solution)/shard_map/ppermute | solution.py:46
  124.4 3.4 %collective-permute-done.9 = bf16[64,4,3584]{2,1,0:T(4,128)(2,1)S(1)} collective-permute-done((bf16[64,4,3584]{2,1,0:T(4,128)(2,1)S(1)}, bf16[64,4,3584]{2,1,0:T(4,128)(2,1)S(1)}, u32[]{:S(2)}, u32[]{:S(2)}) %collective-permute-start.9) | collective-permute-done | bytes 1835040 | tf_op jit(solution)/shard_map/ppermute | solution.py:46
  127.8 2.4 %pad_maximum_fusion = bf16[128,4,3584]{2,1,0:T(4,128)(2,1)S(1)} fusion(bf16[64,4,3584]{2,1,0:T(4,128)(2,1)S(1)} %collective-permute-done.9, bf16[64,4,3584]{2,1,0:T(4,128)(2,1)S(1)} %all_to_all.20), kind=kLoop, calls=%fused_computation.16 | loop fusion | flops 1835008 | bytes 7340032 | tf_op jit(solution)/shard_map/concatenate | solution.py:137
  130.2 0.6 copy.29
  130.9 2.0 %fusion.13 = f32[128,2,2,512]{3,0,2,1:T(8,128)S(1)} fusion(bf16[128,2,2,3584]{3,0,2,1:T(8,128)(2,1)S(1)} %bitcast.113, bf16[2,3584,512]{2,1,0:T(8,128)(2,1)S(1)} %bitcast.127), kind=kOutput, calls=%fused_computation.20 | convolution fusion | flops 1879048192 | bytes 12058624 | tf_op jit(solution)/shard_map/secd,edf->secf/dot_general | solution.py:50
  132.9 1.8 slice-done.5
  134.7 2.0 %fusion.16 = f32[128,2,2,512]{3,0,2,1:T(8,128)S(1)} fusion(bf16[128,2,2,3584]{3,0,2,1:T(8,128)(2,1)S(1)} %bitcast.114, bf16[2,3584,512]{2,1,0:T(8,128)(2,1)S(1)} %bitcast.129), kind=kOutput, calls=%fused_computation.21 | convolution fusion | flops 1879048192 | bytes 12058624 | tf_op jit(solution)/shard_map/secd,edf->secf/dot_general | solution.py:53
  136.8 2.2 %fusion.6 = f32[128,2,2,3584]{3,0,2,1:T(8,128)S(1)} fusion(bf16[2,512,3584]{2,1,0:T(8,128)(2,1)S(1)} %bitcast.112, f32[128,2,2,512]{3,0,2,1:T(8,128)S(1)} %fusion.16, f32[128,2,2,512]{3,0,2,1:T(8,128)S(1)} %fusion.13), kind=kOutput, calls=%fused_computation.8 | convolution fusion | flops 1880621056 | bytes 16777216 | tf_op jit(solution)/shard_map/secf,efd->secd/dot_general | solution.py:57
  139.0 0.2 slice.30
  139.2 1.4 copy.30
  140.6 0.7 collective-permute-start.10
  141.3 0.2 slice.24
  141.5 3.2 %collective-permute-done.10 = bf16[64,4,3584]{2,1,0:T(4,128)(2,1)S(1)} collective-permute-done((bf16[64,4,3584]{2,1,0:T(4,128)(2,1)S(1)}, bf16[64,4,3584]{2,1,0:T(4,128)(2,1)S(1)}, u32[]{:S(2)}, u32[]{:S(2)}) %collective-permute-start.10) | collective-permute-done | bytes 1835040 | tf_op jit(solution)/shard_map/ppermute | solution.py:46
  144.7 4.1 %fusion.12 = bf16[64,4,3584]{2,1,0:T(4,128)(2,1)} fusion(f32[64,4,3584]{2,0,1:T(8,128)S(1)} %bitcast.109, bf16[64,4,3584]{2,1,0:T(4,128)(2,1)S(1)} %collective-permute-done.10), kind=kLoop, calls=%fused_computation.18 | loop fusion | flops 2752512 | bytes 7340032 | tf_op jit(solution)/shard_map/convert_element_type | solution.py:142
  148.7 5.9 %all-to-all-start.3 = ((bf16[64,4,3584]{2,1,0:T(4,128)(2,1)}), bf16[64,4,3584]{2,1,0:T(4,128)(2,1)}, u32[]{:S(2)}, u32[]{:S(2)}) async-start(bf16[64,4,3584]{2,1,0:T(4,128)(2,1)} %fusion.12), calls=%async_computation.3 | async-start | bytes 3670016 | tf_op jit(solution)/shard_map/all_to_all | solution.py:143
  154.8 0.1 reduce_sum.64
  155.0 25.0 %all-to-all-done.3 = bf16[64,4,3584]{2,1,0:T(4,128)(2,1)} async-done(((bf16[64,4,3584]{2,1,0:T(4,128)(2,1)}), bf16[64,4,3584]{2,1,0:T(4,128)(2,1)}, u32[]{:S(2)}, u32[]{:S(2)}) %all-to-all-start.3) | async-done | bytes 1835040 | tf_op jit(solution)/shard_map/all_to_all | solution.py:143
  179.9 3.0 %reshape.196 = bf16[256,3584]{1,0:T(8,128)(2,1)S(1)} reshape(bf16[64,4,3584]{2,1,0:T(4,128)(2,1)} %all-to-all-done.3) | data formatting | bytes 3670016 | tf_op jit(solution)/shard_map/reshape | solution.py:144
  183.0 0.8 gather_fusion.1
  183.8 1.0 multiply_reduce_fusion
  (65 shorter events, 0.7 us)
Async XLA Ops:
  0.6 4.0 %copy-start = (bf16[16,36864]{1,0:T(8,128)(2,1)S(1)}, bf16[16,36864]{1,0:T(8,128)(2,1)}, u32[]{:S(2)}) copy-start(bf16[16,36864]{1,0:T(8,128)(2,1)} %param.15) | copy-start | bytes 3538948
  1.8 24.2 %collective-permute-start.1 = (bf16[128,1792]{1,0:T(8,128)(2,1)S(1)}, bf16[128,1792]{1,0:T(8,128)(2,1)}, u32[]{:S(2)}, u32[]{:S(2)}) collective-permute-start(bf16[128,1792]{1,0:T(8,128)(2,1)S(1)} %constant_dynamic-slice_fusion), channel_id=1, source_target_pairs={{0,1},{1,2},{2,3},{3,0},{4,5},{5,6},{6,7},{7,4},{8,9},{9,10},{10,1... | collective-permute-start | bytes 1376264 | tf_op jit(solution)/shard_map/ppermute | solution.py:42
  7.0 3.2 %copy-start.10 = (s32[1,16]{1,0:T(1,128)S(1)}, s32[1,16]{1,0:T(1,128)}, u32[]{:S(2)}) copy-start(s32[1,16]{1,0:T(1,128)} %param.16) | copy-start | bytes 196
  7.0 4.2 %copy-start.2 = (bf16[8,36864]{1,0:T(8,128)(2,1)S(1)}, bf16[8,36864]{1,0:T(8,128)(2,1)}, u32[]{:S(2)}) copy-start(bf16[8,36864]{1,0:T(8,128)(2,1)} %param.13) | copy-start | bytes 1769476
  7.0 5.0 %copy-start.11 = (s32[1,8]{1,0:T(1,128)S(1)}, s32[1,8]{1,0:T(1,128)}, u32[]{:S(2)}) copy-start(s32[1,8]{1,0:T(1,128)} %param.17) | copy-start | bytes 100
  11.2 1.2 copy-start.9
  13.8 14.1 %copy-start.5 = (bf16[1,512,128]{2,1,0:T(8,128)(2,1)S(1)}, bf16[1,512,128]{2,1,0:T(8,128)(2,1)}, u32[]{:S(2)}) copy-start(bf16[1,512,128]{2,1,0:T(8,128)(2,1)} %param.18) | copy-start | bytes 393220
  15.2 18.0 %all-to-all-start = ((bf16[16,32,512]{2,1,0:T(8,128)(2,1)}), bf16[16,32,512]{2,1,0:T(8,128)(2,1)S(1)}, u32[]{:S(2)}, u32[]{:S(2)}) async-start(bf16[16,32,512]{2,1,0:T(8,128)(2,1)} %bitcast.11), calls=%async_computation | async-start | bytes 1048576 | tf_op jit(solution)/shard_map/all_to_all | solution.py:97
  22.8 12.1 %collective-permute-start.7 = (bf16[128,1792]{1,0:T(8,128)(2,1)S(1)}, bf16[128,1792]{1,0:T(8,128)(2,1)}, u32[]{:S(2)}, u32[]{:S(2)}) collective-permute-start(bf16[128,1792]{1,0:T(8,128)(2,1)S(1)} %constant_dynamic-slice_fusion), channel_id=1, source_target_pairs={{0,3},{1,0},{2,1},{3,2},{4,7},{5,4},{6,5},{7,6},{8,11},{9,8},{10,9... | collective-permute-start | bytes 1376264 | tf_op jit(solution)/shard_map/ppermute | solution.py:42
  24.4 13.3 %collective-permute-start.4 = (bf16[128,1792]{1,0:T(8,128)(2,1)S(1)}, bf16[128,1792]{1,0:T(8,128)(2,1)S(1)}, u32[]{:S(2)}, u32[]{:S(2)}) collective-permute-start(bf16[128,1792]{1,0:T(8,128)(2,1)S(1)} %constant_dynamic-slice_fusion), channel_id=1, source_target_pairs={{0,2},{1,3},{2,0},{3,1},{4,6},{5,7},{6,4},{7,5},{8,10},{9,11},{10,... | collective-permute-start | bytes 1376264 | tf_op jit(solution)/shard_map/ppermute | solution.py:42
  26.0 21.0 %collective-permute-start.2 = (bf16[128,1792]{1,0:T(8,128)(2,1)}, bf16[128,1792]{1,0:T(8,128)(2,1)}, u32[]{:S(2)}, u32[]{:S(2)}) collective-permute-start(bf16[128,1792]{1,0:T(8,128)(2,1)} %collective-permute-done.1), channel_id=1, source_target_pairs={{0,64},{64,0},{1,65},{65,1},{2,66},{66,2},{3,67},{67,3},{4,68},{68... | collective-permute-start | bytes 1376264 | tf_op jit(solution)/shard_map/ppermute | solution.py:46
  27.8 24.5 %collective-permute-start = (bf16[512,128]{1,0:T(8,128)(2,1)S(1)}, bf16[512,128]{1,0:T(8,128)(2,1)}, u32[]{:S(2)}, u32[]{:S(2)}) collective-permute-start(bf16[512,128]{1,0:T(8,128)(2,1)S(1)} %bitcast.119), channel_id=1, source_target_pairs={{0,1},{1,2},{2,3},{3,0},{4,5},{5,6},{6,7},{7,4},{8,9},{9,10},{10,1... | collective-permute-start | bytes 393224 | tf_op jit(solution)/shard_map/ppermute | solution.py:42
  28.2 27.2 %collective-permute-start.6 = (bf16[512,128]{1,0:T(8,128)(2,1)S(1)}, bf16[512,128]{1,0:T(8,128)(2,1)}, u32[]{:S(2)}, u32[]{:S(2)}) collective-permute-start(bf16[512,128]{1,0:T(8,128)(2,1)S(1)} %bitcast.120), channel_id=1, source_target_pairs={{0,3},{1,0},{2,1},{3,2},{4,7},{5,4},{6,5},{7,6},{8,11},{9,8},{10,9... | collective-permute-start | bytes 393224 | tf_op jit(solution)/shard_map/ppermute | solution.py:42
  34.9 22.2 %collective-permute-start.3 = (bf16[512,128]{1,0:T(8,128)(2,1)S(1)}, bf16[512,128]{1,0:T(8,128)(2,1)}, u32[]{:S(2)}, u32[]{:S(2)}) collective-permute-start(bf16[512,128]{1,0:T(8,128)(2,1)S(1)} %bitcast.121), channel_id=1, source_target_pairs={{0,2},{1,3},{2,0},{3,1},{4,6},{5,7},{6,4},{7,5},{8,10},{9,11},{10,... | collective-permute-start | bytes 393224 | tf_op jit(solution)/shard_map/ppermute | solution.py:42
  37.6 13.6 %copy-start.3 = (bf16[128,1792]{1,0:T(8,128)(2,1)}, bf16[128,1792]{1,0:T(8,128)(2,1)S(1)}, u32[]{:S(2)}) copy-start(bf16[128,1792]{1,0:T(8,128)(2,1)S(1)} %collective-permute-done.4) | copy-start | bytes 1376260
  37.6 11.6 %collective-permute-start.8 = (bf16[128,1792]{1,0:T(8,128)(2,1)}, bf16[128,1792]{1,0:T(8,128)(2,1)S(1)}, u32[]{:S(2)}, u32[]{:S(2)}) collective-permute-start(bf16[128,1792]{1,0:T(8,128)(2,1)} %collective-permute-done.7), channel_id=1, source_target_pairs={{0,64},{64,0},{1,65},{65,1},{2,66},{66,2},{3,67},{67,3},{4,68},{68... | collective-permute-start | bytes 1376264 | tf_op jit(solution)/shard_map/ppermute | solution.py:46
  47.0 4.3 %collective-permute-start.5 = (bf16[128,1792]{1,0:T(8,128)(2,1)S(1)}, bf16[128,1792]{1,0:T(8,128)(2,1)S(1)}, u32[]{:S(2)}, u32[]{:S(2)}) collective-permute-start(bf16[128,1792]{1,0:T(8,128)(2,1)S(1)} %collective-permute-done.4), channel_id=1, source_target_pairs={{0,64},{64,0},{1,65},{65,1},{2,66},{66,2},{3,67},{67,3},{4,68},{68... | collective-permute-start | bytes 1376264 | tf_op jit(solution)/shard_map/ppermute | solution.py:46
  60.2 6.5 %copy-start.6 = (s32[8,8]{1,0:T(8,128)S(1)}, s32[8,8]{1,0:T(8,128)}, u32[]{:S(2)}) copy-start(s32[8,8]{1,0:T(8,128)} %param.21) | copy-start | bytes 772
  60.2 21.6 %copy-start.7 = (f32[3584]{0:T(1024)S(1)}, f32[3584]{0:T(1024)}, u32[]{:S(2)}) copy-start(f32[3584]{0:T(1024)} %param.20) | copy-start | bytes 43012
  60.2 21.3 %all-to-all-start.1 = ((bf16[16,8,3584]{2,1,0:T(8,128)(2,1)}), bf16[16,8,3584]{2,1,0:T(8,128)(2,1)S(1)}, u32[]{:S(2)}, u32[]{:S(2)}) async-start(bf16[16,8,3584]{2,1,0:T(8,128)(2,1)} %fusion.11), calls=%async_computation.1 | async-start | bytes 1835008 | tf_op jit(solution)/shard_map/all_to_all | solution.py:113
  81.9 5.1 %copy-start.4 = (bf16[8,3584]{1,0:T(8,128)(2,1)}, bf16[8,3584]{1,0:T(8,128)(2,1)S(1)}, u32[]{:S(2)}) copy-start(bf16[8,3584]{1,0:T(8,128)(2,1)S(1)} %multiply_convert_fusion.2) | copy-start | bytes 172036
  87.0 43.8 %slice-start.2 = ((s8[7340032]{0:T(1024)(128)(4,1)}), s8[4194304]{0:T(1024)(128)(4,1)S(1)}, s32[]{:S(2)}) async-start(s8[7340032]{0:T(1024)(128)(4,1)} %bitcast.126), calls=%async_computation.6 | async-start | bytes 8388608
  121.5 9.3 %slice-start.3 = ((s8[7340032]{0:T(1024)(128)(4,1)}), s8[3145728]{0:T(1024)(128)(4,1)S(1)}, s32[]{:S(2)}) async-start(s8[7340032]{0:T(1024)(128)(4,1)} %bitcast.126), calls=%async_computation.7 | async-start | bytes 6291456
  121.5 6.3 %collective-permute-start.9 = (bf16[64,4,3584]{2,1,0:T(4,128)(2,1)S(1)}, bf16[64,4,3584]{2,1,0:T(4,128)(2,1)S(1)}, u32[]{:S(2)}, u32[]{:S(2)}) collective-permute-start(bf16[64,4,3584]{2,1,0:T(4,128)(2,1)S(1)} %all_to_all.20), channel_id=1, source_target_pairs={{0,64},{64,0},{1,65},{65,1},{2,66},{66,2},{3,67},{67,3},{4,68},{68... | collective-permute-start | bytes 5505032 | tf_op jit(solution)/shard_map/ppermute | solution.py:46
  130.2 2.8 %slice-start.4 = ((s8[7340032]{0:T(1024)(128)(4,1)}), s8[4194304]{0:T(1024)(128)(4,1)S(1)}, s32[]{:S(2)}) async-start(s8[7340032]{0:T(1024)(128)(4,1)} %bitcast.128), calls=%async_computation.8 | async-start | bytes 8388608
  130.2 6.6 %slice-start = ((s8[7340032]{0:T(1024)(128)(4,1)}), s8[4194304]{0:T(1024)(128)(4,1)S(1)}, s32[]{:S(2)}) async-start(s8[7340032]{0:T(1024)(128)(4,1)} %bitcast.111), calls=%async_computation.4 | async-start | bytes 8388608
  130.9 3.9 %slice-start.5 = ((s8[7340032]{0:T(1024)(128)(4,1)}), s8[3145728]{0:T(1024)(128)(4,1)S(1)}, s32[]{:S(2)}) async-start(s8[7340032]{0:T(1024)(128)(4,1)} %bitcast.128), calls=%async_computation.9 | async-start | bytes 6291456
  130.9 5.9 %slice-start.1 = ((s8[7340032]{0:T(1024)(128)(4,1)}), s8[3145728]{0:T(1024)(128)(4,1)S(1)}, s32[]{:S(2)}) async-start(s8[7340032]{0:T(1024)(128)(4,1)} %bitcast.111), calls=%async_computation.5 | async-start | bytes 6291456
  140.6 4.1 %collective-permute-start.10 = (bf16[64,4,3584]{2,1,0:T(4,128)(2,1)S(1)}, bf16[64,4,3584]{2,1,0:T(4,128)(2,1)S(1)}, u32[]{:S(2)}, u32[]{:S(2)}) collective-permute-start(bf16[64,4,3584]{2,1,0:T(4,128)(2,1)S(1)} %copy.30), channel_id=1, source_target_pairs={{0,64},{64,0},{1,65},{65,1},{2,66},{66,2},{3,67},{67,3},{4,68},{68... | collective-permute-start | bytes 5505032 | tf_op jit(solution)/shard_map/ppermute | solution.py:46
  148.7 6.0 %copy-start.8 = (f32[8,8]{1,0:T(8,128)S(1)}, f32[8,8]{1,0:T(8,128)}, u32[]{:S(2)}) copy-start(f32[8,8]{1,0:T(8,128)} %param.22) | copy-start | bytes 772
  148.7 31.2 %all-to-all-start.3 = ((bf16[64,4,3584]{2,1,0:T(4,128)(2,1)}), bf16[64,4,3584]{2,1,0:T(4,128)(2,1)}, u32[]{:S(2)}, u32[]{:S(2)}) async-start(bf16[64,4,3584]{2,1,0:T(4,128)(2,1)} %fusion.12), calls=%async_computation.3 | async-start | bytes 3670016 | tf_op jit(solution)/shard_map/all_to_all | solution.py:143
  179.9 4.9 %copy-start.1 = (bf16[16,36864]{1,0:T(8,128)(2,1)S(1)}, bf16[16,36864]{1,0:T(8,128)(2,1)}, u32[]{:S(2)}) copy-start(bf16[16,36864]{1,0:T(8,128)(2,1)} %param.15) | copy-start | bytes 3538948

commit v2 on v1

v2 whole, which is shorter than its diff:
```python
import jax
import jax.numpy as jnp
from jax import lax
from jax.experimental import pallas as pl
from jax.experimental.pallas import tpu as pltpu
from jax.sharding import Mesh, PartitionSpec as P

SCORE_SCALE = 192.0 ** (-0.5)
ROUTED_SCALE = 2.5
EPSILON = 1e-06
SIDE = 4
CHIPS = ("z", "x", "y")
SWAP = [(0, 1), (1, 0)]
F32 = jnp.float32
BF16 = jnp.bfloat16
MIB = 1 << 20
SMEM = pl.BlockSpec(memory_space=pltpu.SMEM)
VMEM = pl.BlockSpec(memory_space=pltpu.VMEM)
HBM = pl.BlockSpec(memory_space=pltpu.HBM)


def dot_nt(a, b):
    return lax.dot_general(a, b, (((1,), (1,)), ((), ())), preferred_element_type=F32)


def dot(a, b):
    return jnp.dot(a, b, preferred_element_type=F32)


def attend_kernel(
    table_hbm, length_hbm, query_hbm, fresh_hbm, cache_hbm, out_ref,
    table_ref, length_ref, query_ref, fresh_ref, cache_ref, key_ref, sems,
):
    moves = (
        (cache_hbm, cache_ref),
        (query_hbm, query_ref),
        (table_hbm, table_ref),
        (length_hbm, length_ref),
        (fresh_hbm, fresh_ref),
    )
    copies = [pltpu.make_async_copy(a, b, sems.at[i]) for i, (a, b) in enumerate(moves)]
    for copy in copies:
        copy.start()
    seq_count, entry = fresh_ref.shape
    pages = cache_ref.shape[0]
    pairs = cache_ref.shape[1] // (2 * entry)
    wide = entry + 64
    kv_width = out_ref.shape[1]
    spots = pairs * pages
    copies[0].wait()
    for r in range(pairs):
        at = 2 * entry * r
        key_ref[0, r * pages : (r + 1) * pages, :] = cache_ref[:, at : at + wide]
        key_ref[1, r * pages : (r + 1) * pages, :] = cache_ref[:, at + entry - 64 : at + 2 * entry]
    even_keys, odd_keys = key_ref[0], key_ref[1]

    for copy in copies[1:]:
        copy.wait()
    sequence = lax.broadcasted_iota(jnp.int32, (seq_count, spots), 0)
    lane = lax.broadcasted_iota(jnp.int32, (seq_count, spots), 1)
    page, entry_at = lane % pages, 2 * (lane // pages)
    first = jnp.zeros((seq_count, spots), jnp.int32)
    second, live = first, first
    for s in range(seq_count):
        here = sequence == s
        first = jnp.where(here, table_ref[0, 2 * s], first)
        second = jnp.where(here, table_ref[0, 2 * s + 1], second)
        live = jnp.where(here, length_ref[0, s], live)

    def bias_of(position):
        inside = ((page == first) & (position < live)) | (
            (page == second) & (position + 2 * pairs < live)
        )
        return jnp.where(inside, 0.0, -jnp.inf).astype(F32)

    even_bias, odd_bias = bias_of(entry_at), bias_of(entry_at + 1)
    fresh = jnp.concatenate(
        [fresh_ref[...].astype(F32), jnp.zeros((seq_count, wide - entry), F32)], axis=1
    )
    group = 8
    for g in range(query_ref.shape[1] // (2 * entry) // group):
        base = 2 * entry * group * g
        evens = [
            query_ref[:, base + 2 * entry * i : base + 2 * entry * i + wide].astype(F32)
            for i in range(group)
        ]
        odds = [
            query_ref[:, base + 2 * entry * (i + 1) - wide : base + 2 * entry * (i + 1)].astype(F32)
            for i in range(group)
        ]
        rows = group * seq_count
        column = lax.broadcasted_iota(jnp.int32, (rows, wide), 1)
        even_low = jnp.where(column < entry, jnp.concatenate(evens, axis=0), 0.0)
        odd_high = jnp.where(column >= 64, jnp.concatenate(odds, axis=0), 0.0)
        even_high = pltpu.roll(even_low, 64, 1)
        odd_low = pltpu.roll(odd_high, entry, 1)
        low = jnp.concatenate([even_low, odd_low], axis=0)
        high = jnp.concatenate([even_high, odd_high], axis=0)
        heads = 2 * group
        own = jnp.sum(
            low.reshape(heads, seq_count, wide) * fresh[None], axis=2, keepdims=True
        ) * SCORE_SCALE
        even_scores = (dot_nt(low.astype(BF16), even_keys) * SCORE_SCALE).reshape(
            heads, seq_count, spots
        ) + even_bias[None]
        odd_scores = (dot_nt(high.astype(BF16), odd_keys) * SCORE_SCALE).reshape(
            heads, seq_count, spots
        ) + odd_bias[None]
        top = jnp.maximum(
            jnp.max(jnp.maximum(even_scores, odd_scores), axis=2, keepdims=True), own
        )
        even_raised = jnp.exp(even_scores - top)
        odd_raised = jnp.exp(odd_scores - top)
        own_raised = jnp.exp(own - top)
        scale = 1.0 / (
            jnp.sum(even_raised + odd_raised, axis=2, keepdims=True) + own_raised
        )
        even_weights = (even_raised * scale).astype(BF16).reshape(2 * rows, spots)
        odd_weights = (odd_raised * scale).astype(BF16).reshape(2 * rows, spots)
        own_weight = (own_raised * scale).astype(BF16).astype(F32)
        even_part = dot(even_weights, even_keys)[:, :kv_width]
        odd_part = pltpu.roll(dot(odd_weights, odd_keys), entry, 1)[:, :kv_width]
        own_part = (own_weight * fresh[None, :, :kv_width]).reshape(2 * rows, kv_width)
        latent = even_part + odd_part + own_part
        for i in range(group):
            two = jnp.concatenate(
                [
                    latent[i * seq_count : (i + 1) * seq_count],
                    latent[rows + i * seq_count : rows + (i + 1) * seq_count],
                ],
                axis=0,
            )
            at = 2 * seq_count * (group * g + i)
            out_ref[at : at + 2 * seq_count, :] = two.astype(BF16)


def attend(block_table, lengths, queries, new_latent, latent_cache, kv_width):
    seq_count, entry = new_latent.shape
    head_count = queries.shape[1] // entry
    pages, page_width = latent_cache.shape
    spots = pages * page_width // (2 * entry)
    return pl.pallas_call(
        attend_kernel,
        out_shape=jax.ShapeDtypeStruct((head_count * seq_count, kv_width), BF16),
        in_specs=[HBM] * 5,
        out_specs=VMEM,
        scratch_shapes=[
            pltpu.SMEM(block_table.shape, jnp.int32),
            pltpu.SMEM(lengths.shape, jnp.int32),
            pltpu.VMEM(queries.shape, BF16),
            pltpu.VMEM(new_latent.shape, BF16),
            pltpu.VMEM(latent_cache.shape, BF16),
            pltpu.VMEM((2, spots, entry + 64), BF16),
            pltpu.SemaphoreType.DMA((5,)),
        ],
        compiler_params=pltpu.CompilerParams(vmem_limit_bytes=60 * MIB),
        cost_estimate=pl.CostEstimate(
            flops=1_400_000_000, bytes_accessed=2_400_000, transcendentals=600_000
        ),
        name="attend",
    )(block_table, lengths, queries, new_latent, latent_cache)


def prepare_kernel(
    out_proj, value_up, ids_hbm, affinity_hbm, top, bottom, routes, ids, affinity, sems
):
    core = lax.axis_index("core")
    head_rows, half = out_proj.shape[0], out_proj.shape[1] // 2
    at = pl.ds(pl.multiple_of(core * half, 128), half)
    middle = head_rows // 2
    moves = [(ids_hbm, ids), (affinity_hbm, affinity)]
    for i, part in enumerate((top, bottom)):
        moves.append((out_proj.at[pl.ds(i * middle, middle), at], part.at[:, :half]))
        for b in range(value_up.shape[1] // head_rows):
            rows = pl.ds(b * head_rows + i * middle, middle)
            columns = pl.ds(half + b * head_rows, head_rows)
            moves.append((value_up.at[0, rows], part.at[:, columns]))
    copies = [pltpu.make_async_copy(a, b, sems.at[i]) for i, (a, b) in enumerate(moves)]
    for copy in copies:
        copy.start()
    for copy in copies[:2]:
        copy.wait()
    rows, top_count = ids.shape
    rest = jnp.zeros((rows, routes.shape[1] - 2 * top_count), F32)
    routes[...] = jnp.concatenate([ids[...].astype(F32), affinity[...], rest], axis=1)
    for copy in copies[2:]:
        copy.wait()


def prepare(out_proj, value_up, expert_ids, affinity):
    head_rows, width = out_proj.shape
    return pl.pallas_call(
        prepare_kernel,
        out_shape=(
            jax.ShapeDtypeStruct((head_rows // 2, width // 2 + value_up.shape[1]), BF16),
            jax.ShapeDtypeStruct((head_rows // 2, width // 2 + value_up.shape[1]), BF16),
            jax.ShapeDtypeStruct((expert_ids.shape[0], 128), F32),
        ),
        in_specs=[HBM] * 4,
        out_specs=(VMEM, VMEM, VMEM),
        scratch_shapes=[
            pltpu.VMEM(expert_ids.shape, jnp.int32),
            pltpu.VMEM(affinity.shape, F32),
            pltpu.SemaphoreType.DMA((4 + 2 * (value_up.shape[1] // head_rows),)),
        ],
        compiler_params=pltpu.CompilerParams(vmem_limit_bytes=60 * MIB),
        cost_estimate=pl.CostEstimate(flops=0, bytes_accessed=1_200_000, transcendentals=0),
        name="prepare",
    )(out_proj, value_up, expert_ids, affinity)


def route_kernel(own_ref, far_ref, place_ref, mix_ref):
    core = lax.axis_index("core")
    seq_count = own_ref.shape[0]
    tokens, top_count = 2 * seq_count, 8
    columns = place_ref.shape[1]
    routes = jnp.concatenate([own_ref[...], far_ref[...]], axis=0)
    affinity = routes[:, top_count : 2 * top_count]
    share = affinity / jnp.sum(affinity, axis=1, keepdims=True) * ROUTED_SCALE
    experts = routes.shape[1]
    expert = lax.broadcasted_iota(jnp.int32, (tokens, experts), 1).astype(F32)
    chosen = jnp.zeros((tokens, experts), F32)
    shares = jnp.zeros((tokens, experts), F32)
    for k in range(top_count):
        hit = expert == routes[:, k : k + 1]
        chosen = jnp.where(hit, 1.0, chosen)
        shares = jnp.where(hit, share[:, k : k + 1], shares)
    row = lax.broadcasted_iota(jnp.int32, (tokens, tokens), 0)
    column = lax.broadcasted_iota(jnp.int32, (tokens, tokens), 1)
    earlier = ((column < row) & (column // seq_count == row // seq_count)).astype(F32)
    rank = dot(earlier.astype(BF16), chosen.astype(BF16))
    token = lax.broadcasted_iota(jnp.int32, (tokens, experts), 0)
    slot = (rank + jnp.where(token < seq_count, 1.0, 3.0)) * chosen
    named = lax.broadcasted_iota(jnp.int32, (experts, columns), 0)
    at = lax.broadcasted_iota(jnp.int32, (experts, columns), 1)
    spread = (named == at // 8 * 2 + core).astype(F32).astype(BF16)
    high = shares.astype(BF16)
    low = (shares - high.astype(F32)).astype(BF16)
    at = lax.broadcasted_iota(jnp.int32, (tokens, columns), 1)
    filled = dot(slot.astype(BF16), spread) == (at % 4 + 1).astype(F32)
    high = jnp.where(filled, dot(high, spread), 0.0)
    low = jnp.where(filled, dot(low, spread), 0.0)
    placed = filled.astype(F32)
    first = at % 8 < 4

    def by_half(table):
        return [jnp.where(first, table, 0.0), jnp.where(first, 0.0, table)]

    place_ref[...] = jnp.concatenate(by_half(placed), axis=0).astype(BF16)
    mix_ref[...] = jnp.concatenate(by_half(high) + by_half(low), axis=0).astype(BF16)


def route(own, far, chips):
    tokens = 2 * own.shape[0]
    return pl.pallas_call(
        route_kernel,
        out_shape=(
            jax.ShapeDtypeStruct((2 * tokens, chips * 8), BF16),
            jax.ShapeDtypeStruct((4 * tokens, chips * 8), BF16),
        ),
        in_specs=[VMEM] * 2,
        out_specs=(VMEM, VMEM),
        compiler_params=pltpu.CompilerParams(vmem_limit_bytes=8 * MIB),
        cost_estimate=pl.CostEstimate(
            flops=20_000_000, bytes_accessed=120_000, transcendentals=0
        ),
        name="route",
    )(own, far)


def value_kernel(arrived_ref, *refs):
    *piece_refs, out_ref = refs
    place_y = lax.axis_index("y")
    rows, kv_width = arrived_ref.shape
    tokens = rows // SIDE
    head_rows = 2 * piece_refs[0].shape[0]
    half = piece_refs[0].shape[1] - kv_width
    to = lax.broadcasted_iota(jnp.int32, (tokens, rows), 0)
    source = lax.broadcasted_iota(jnp.int32, (tokens, rows), 1)
    plane, seq = to // 8, to % 8
    arrived = arrived_ref[...]
    ups = [
        jnp.concatenate([piece_refs[2 * k][:, half:], piece_refs[2 * k + 1][:, half:]], axis=0)
        for k in range(SIDE)
    ]
    for k, up in enumerate(ups):
        head = lax.rem(place_y - k + SIDE, SIDE)
        pick = (source == plane * (SIDE * 8) + head * 8 + seq).astype(F32)
        latent = dot(pick.astype(BF16), arrived).astype(BF16)
        total = jnp.zeros((tokens, head_rows), F32)
        for at in range(0, kv_width, head_rows):
            total = total + dot(latent[:, at : at + head_rows], up[:, at : at + head_rows])
        out_ref[:, k * head_rows : (k + 1) * head_rows] = total.astype(BF16)


def find_values(arrived, pieces):
    rows = arrived.shape[0]
    return pl.pallas_call(
        value_kernel,
        out_shape=jax.ShapeDtypeStruct((rows // SIDE, 2 * SIDE * pieces[0].shape[0]), BF16),
        in_specs=[VMEM] * 9,
        out_specs=VMEM,
        compiler_params=pltpu.CompilerParams(vmem_limit_bytes=12 * MIB),
        cost_estimate=pl.CostEstimate(
            flops=350_000_000, bytes_accessed=3_200_000, transcendentals=0
        ),
        name="find_values",
    )(arrived, *pieces)


def project_kernel(own_values, far_values, *refs):
    *piece_refs, out_ref = refs
    rows, width = own_values.shape
    head_rows = 2 * piece_refs[0].shape[0]
    half = out_ref.shape[1]
    to = lax.broadcasted_iota(jnp.int32, (2 * rows, rows), 0)
    source = lax.broadcasted_iota(jnp.int32, (2 * rows, rows), 1)
    same = source == to // 16 * 8 + to % 8
    near = (same & (to % 16 < 8)).astype(F32).astype(BF16)
    far = (same & (to % 16 >= 8)).astype(F32).astype(BF16)
    values = (dot(near, own_values[...]) + dot(far, far_values[...])).astype(BF16)
    step = 256
    for at in range(0, half, step):
        total = jnp.zeros((2 * rows, step), F32)
        columns = slice(at, at + step)
        for k in range(SIDE):
            part = jnp.concatenate(
                [piece_refs[2 * k][:, columns], piece_refs[2 * k + 1][:, columns]], axis=0
            )
            total = total + dot(values[:, k * head_rows : (k + 1) * head_rows], part)
        out_ref[:, at : at + step] = total.astype(BF16)


def project(own_values, far_values, pieces, half):
    return pl.pallas_call(
        project_kernel,
        out_shape=jax.ShapeDtypeStruct((2 * own_values.shape[0], half), BF16),
        in_specs=[VMEM] * 10,
        out_specs=VMEM,
        compiler_params=pltpu.CompilerParams(vmem_limit_bytes=12 * MIB),
        cost_estimate=pl.CostEstimate(
            flops=600_000_000, bytes_accessed=3_000_000, transcendentals=0
        ),
        name="project",
    )(own_values, far_values, *pieces)


def expert_kernel(
    rows_ref, gate_ref, up_ref, down_ref, gate_far, up_far, down_far, out_ref,
    gate_buf, up_buf, down_buf, wide_ref, total_ref, sems,
):
    core = lax.axis_index("core")
    blocks, width, block = gate_buf.shape
    half = width // 2
    count = total_ref.shape[0]

    def copies(i):
        near = i < blocks // 2
        at = pl.ds((i % (blocks // 2)) * block, block)
        gate, up, down = (gate_ref, up_ref, down_ref) if near else (gate_far, up_far, down_far)
        return (
            pltpu.make_async_copy(gate.at[core, :, at], gate_buf.at[i], sems.at[0, i]),
            pltpu.make_async_copy(up.at[core, :, at], up_buf.at[i], sems.at[1, i]),
            pltpu.make_async_copy(down.at[core, at, :], down_buf.at[i], sems.at[2, i]),
        )

    started = [copies(i) for i in range(blocks)]
    for three in started:
        for copy in three:
            copy.start()

    to = lax.broadcasted_iota(jnp.int32, (count, 2 * count), 0)
    source = lax.broadcasted_iota(jnp.int32, (count, 2 * count), 1)
    step = 256
    for side in range(2):
        pick = (source == to // 4 * 8 + to % 4 + 4 * side).astype(F32).astype(BF16)
        for at in range(0, half, step):
            wide_ref[:, side * half + at : side * half + at + step] = dot(
                pick, rows_ref[:, at : at + step]
            ).astype(BF16)

    for i in range(blocks):
        started[i][0].wait()
        started[i][1].wait()
        gate = dot(wide_ref[...], gate_buf[i])
        up = dot(wide_ref[...], up_buf[i])
        hidden = (gate / (1.0 + jnp.exp(-gate)) * up).astype(BF16)
        started[i][2].wait()
        for at in range(0, width, 2 * step):
            part = dot(hidden, down_buf[i, :, at : at + 2 * step])
            if i == 0:
                total_ref[:, at : at + 2 * step] = part
            else:
                total_ref[:, at : at + 2 * step] += part

    to = lax.broadcasted_iota(jnp.int32, (2 * count, count), 0)
    source = lax.broadcasted_iota(jnp.int32, (2 * count, count), 1)
    first = (to % 8 < 4) & (source == to // 8 * 4 + to % 4)
    second = (to % 8 >= 4) & (source == to // 8 * 4 + to % 4)
    first = first.astype(F32).astype(BF16)
    second = second.astype(F32).astype(BF16)
    for at in range(0, half, step):
        out_ref[:, at : at + step] = (
            dot(first, total_ref[:, at : at + step].astype(BF16))
            + dot(second, total_ref[:, half + at : half + at + step].astype(BF16))
        ).astype(BF16)


def run_expert(rows, near, far):
    width = near[2].shape[2]
    hidden = near[2].shape[1]
    block = 256
    blocks = 2 * hidden // block
    count = rows.shape[0] // 2
    return pl.pallas_call(
        expert_kernel,
        out_shape=jax.ShapeDtypeStruct(rows.shape, BF16),
        in_specs=[VMEM] + [HBM] * 6,
        out_specs=VMEM,
        scratch_shapes=[
            pltpu.VMEM((blocks, width, block), BF16),
            pltpu.VMEM((blocks, width, block), BF16),
            pltpu.VMEM((blocks, block, width), BF16),
            pltpu.VMEM((count, width), BF16),
            pltpu.VMEM((count, width), F32),
            pltpu.SemaphoreType.DMA((3, blocks)),
        ],
        compiler_params=pltpu.CompilerParams(vmem_limit_bytes=57 * MIB),
        cost_estimate=pl.CostEstimate(
            flops=7_500_000_000, bytes_accessed=26_000_000, transcendentals=300_000
        ),
        name="expert",
    )(rows, *near, *far)


def along_y(array, step):
    return lax.ppermute(array, "y", [(i, (i + step) % SIDE) for i in range(SIDE)])


def other_core(array):
    return lax.ppermute(array, "core", SWAP)


def shards(
    queries,
    new_latent,
    latent_cache,
    block_table,
    lengths,
    value_up,
    out_proj,
    norm_gain,
    expert_ids,
    affinity,
    gate_weight,
    up_weight,
    down_weight,
):
    seq_count = new_latent.shape[0]
    kv_width = value_up.shape[1]
    head_rows, model_width = out_proj.shape
    half = model_width // 2
    core = lax.axis_index("core")
    planes = SIDE * SIDE
    chips = SIDE**3

    top, bottom, routes = prepare(out_proj, value_up, expert_ids, affinity)
    one_top, three_bottom = along_y(top, 1), along_y(bottom, -1)
    far_routes = other_core(routes)

    latent = attend(block_table, lengths, queries, new_latent, latent_cache, kv_width)
    outbound = latent.reshape(planes, SIDE * seq_count, kv_width)
    outbound, one_top, three_bottom, far_routes = lax.optimization_barrier(
        (outbound, one_top, three_bottom, far_routes)
    )
    two_top, two_bottom = along_y(one_top, 1), along_y(three_bottom, -1)
    one_bottom, three_top = along_y(bottom, 1), along_y(top, -1)
    pieces = (top, bottom, one_top, one_bottom, two_top, two_bottom, three_top, three_bottom)
    arrived = lax.all_to_all(outbound, ("z", "x"), split_axis=0, concat_axis=0, tiled=True)
    arrived = arrived.reshape(planes * SIDE * seq_count, kv_width)
    placement, mixing = route(routes, far_routes, chips)
    arrived, placement, mixing = lax.optimization_barrier((arrived, placement, mixing))

    own_values = find_values(arrived, pieces)
    partial = project(own_values, other_core(own_values), pieces, half)
    partial, gate_weight = lax.optimization_barrier((partial, gate_weight))
    far_gate = other_core(gate_weight)
    partial = partial.reshape(planes, 2 * seq_count, half)
    collected = lax.all_to_all(partial, ("z", "x"), split_axis=0, concat_axis=0, tiled=True)
    mine = jnp.sum(collected.astype(F32), axis=0)
    theirs = other_core(mine)
    theirs = jnp.concatenate([theirs[seq_count:], theirs[:seq_count]], axis=0)
    attn_out = jnp.where(
        core == 0,
        jnp.concatenate([mine, theirs], axis=1),
        jnp.concatenate([theirs, mine], axis=1),
    )
    attn_out, up_weight, down_weight = lax.optimization_barrier(
        (attn_out, up_weight, down_weight)
    )
    far_weights = (far_gate, other_core(up_weight), other_core(down_weight))
    weights = (gate_weight, up_weight, down_weight)
    mean_square = jnp.mean(attn_out * attn_out, axis=1, keepdims=True)
    both = (attn_out * lax.rsqrt(mean_square + EPSILON) * norm_gain).astype(BF16)
    normed = both[:seq_count]
    both = jnp.concatenate([both[:, :half], both[:, half:]], axis=0)
    outgoing = lax.dot_general(
        placement, both, (((0,), (0,)), ((), ())), preferred_element_type=F32
    )
    outgoing = outgoing.astype(BF16).reshape(chips, 8, half)
    received = lax.all_to_all(outgoing, CHIPS, split_axis=0, concat_axis=0, tiled=True)
    reply = run_expert(received.reshape(chips * 8, half), weights, far_weights)
    returned = lax.all_to_all(
        reply.reshape(chips, 8, half), CHIPS, split_axis=0, concat_axis=0, tiled=True
    )
    mixed = dot(mixing, returned.reshape(chips * 8, half))
    mixed = mixed[: 4 * seq_count] + mixed[4 * seq_count :]
    mixed = mixed.reshape(2, 2, seq_count, half)
    mixed = jnp.transpose(mixed, (1, 2, 0, 3)).reshape(2, seq_count, model_width)
    expert_out = (mixed[0] + other_core(mixed[1])).astype(BF16)
    return (normed, expert_out)


def solution(mesh):
    grid = Mesh(mesh.devices.reshape(2, SIDE, SIDE, SIDE), ("core",) + CHIPS)
    rows = P(("core",) + CHIPS, None)
    placed = (
        rows,
        rows,
        rows,
        rows,
        rows,
        P(CHIPS, None, None),
        P(CHIPS, None),
        P(),
        rows,
        rows,
        P(CHIPS, None, "core"),
        P(CHIPS, None, "core"),
        P(CHIPS, "core", None),
    )
    return jax.shard_map(
        shards, mesh=grid, in_specs=placed, out_specs=(rows, rows), check_vma=False
    )
```

time: 187 us -> 150 us (0.80)
  blocking collectives: 34.4 us -> 82.5 us
  waiting for transfers between devices: 48.5 us -> 12.9 us
  Pallas kernels: 0 us -> 24.1 us
  local copies, waits for them, and re-layouts: 20.4 us -> 0.68 us
  starting transfers between devices: 45.5 us -> 26 us
  matrix products: 19.2 us -> 1.1 us
  other arithmetic: 15.7 us -> 1.05 us
    all_to_all x0 -> x2, blocking collectives: none -> 52 us  [the longest x1 30.4 us: shards(): lax.all_to_all(reply.reshape(chips, 8, half), CHIPS, split_axis=0, concat...]
    all_to_all x2 -> x0, waiting for transfers between devices: 39.2 us -> none  [the longest x1 25 us: shards(): lax.all_to_all(reply, CHIPS, split_axis=0, concat_axis=0, tiled=True)]
    pallas_call x0 -> x6, Pallas kernels: none -> 24.1 us  [the longest x1 13 us: run_expert(): pl.pallas_call(expert_kernel, out_shape=jax.ShapeDtypeStruct(rows.shape,...]
    dot_general x11 -> x2, matrix products: 19.2 us -> 1.1 us  [the longest x1 0.66 us: shards(): lax.dot_general(placement, both, (((0,), (0,)), ((), ())), preferred_elem...]
    all_to_all x2 -> x0, starting transfers between devices: 12.4 us -> none  [the longest x1 6.44 us: shards(): lax.all_to_all(partial, ('z', 'x'), split_axis=0, concat_axis=0, tiled=True)]
    reshape x5 -> x0, local copies, waits for them, and re-layouts: 7.12 us -> none  [the longest x1 3.12 us: shards(): outgoing.reshape(chip_count, local_experts * capacity, model_width)]
    select_n x6 -> x1, other arithmetic: 6.17 us -> 0.02 us  [shards(): jnp.where(core == 0, jnp.concatenate([mine, theirs], axis=1), jnp.concate...]
    gather x3 -> x0, local copies, waits for them, and re-layouts: 5.9 us -> none  [the longest x2 5.08 us: shards(): jnp.take(latent_cache, block_table.reshape(-1), axis=0)]
  transfers between devices with their start and end apart: 14 -> 14, of which waited for: 5 -> 5; matrix products, arithmetic and copies ran while one was open for 13% -> 1% of each run, Pallas kernels for 0% -> 4%
where the time goes in v2:
time: 150 us; the launch traced here: 149 us
  blocking collectives  82.5 us (55%)
  starting transfers between devices  26 us (17%)
  Pallas kernels  24.1 us (16%)
  waiting for transfers between devices  12.9 us (9%)
    all_to_all x1, blocking collectives, shards(): lax.all_to_all(outgoing, CHIPS, split_axis=0, concat_axis=0, tiled=True)  30.6 us
    all_to_all x1, blocking collectives, shards(): lax.all_to_all(reply.reshape(chips, 8, half), CHIPS, split_axis=0, concat...  30.4 us
    all_to_all x1, blocking collectives, shards(): lax.all_to_all(partial, ('z', 'x'), split_axis=0, concat_axis=0, tiled=True)  21.6 us
    pallas_call x1, Pallas kernels, run_expert(): pl.pallas_call(expert_kernel, out_shape=jax.ShapeDtypeStruct(rows.shape,...  13 us
    ppermute x7, starting transfers between devices, other_core(): return lax.ppermute(array, 'core', SWAP)  10.1 us
    ppermute x6, starting transfers between devices, along_y(): lax.ppermute(array, 'y', [(i, (i + step) % SIDE) for i in range(SIDE)])  8.22 us
    all_to_all x1, starting transfers between devices, shards(): lax.all_to_all(outbound, ('z', 'x'), split_axis=0, concat_axis=0, tiled=T...  7.7 us
    pallas_call x1, Pallas kernels, attend(): pl.pallas_call(attend_kernel, out_shape=jax.ShapeDtypeStruct((head_count...  6.25 us
  transfers between devices with their start and end apart: 14, of which 5 were waited for; matrix products, arithmetic and copies ran while one was open for 1% of the time, Pallas kernels for 4%

profile of v2, /device:TPU:1, one launch (start us, length us, event | category | flops | bytes accessed | tf_op | source)
XLA Modules:
  0.0 149.2 jit_solution(15086980783941058135)
XLA Ops:
  0.6 2.1 %prepare.1 = (bf16[64,2304]{1,0:T(8,128)(2,1)}, bf16[64,2304]{1,0:T(8,128)(2,1)}, f32[8,128]{1,0:T(8,128)}) custom-call(bf16[128,3584]{1,0:T(8,128)(2,1)} %out_proj.1, bf16[1,512,128]{2,1,0:T(8,128)(2,1)} %value_up.1, s32[8,8]{1,0:T(8,128)} %ids_hbm.1, f32[8,8]{1,0:T(8,128)} %affinity_hbm.1), custom_call_target="tpu_custom_call" | custom-call | bytes 1200000 | tf_op jit(solution)/shard_map/prepare/pallas_call | solution.py:192
  2.7 2.2 %collective-permute-start = (bf16[64,2304]{1,0:T(8,128)(2,1)}, bf16[64,2304]{1,0:T(8,128)(2,1)S(1)}, u32[]{:S(2)}, u32[]{:S(2)}) collective-permute-start(bf16[64,2304]{1,0:T(8,128)(2,1)} %get-tuple-element.19.refs_0_), channel_id=1, source_target_pairs={{0,1},{1,2},{2,3},{3,0},{4,5},{5,6},{6,7},{7,4},{8,9},{9,10},{10,1... | collective-permute-start | bytes 884744 | tf_op jit(solution)/shard_map/ppermute | solution.py:437
  4.9 1.5 %collective-permute-start.1 = (bf16[64,2304]{1,0:T(8,128)(2,1)}, bf16[64,2304]{1,0:T(8,128)(2,1)S(1)}, u32[]{:S(2)}, u32[]{:S(2)}) collective-permute-start(bf16[64,2304]{1,0:T(8,128)(2,1)} %get-tuple-element.20.refs_1_), channel_id=1, source_target_pairs={{0,3},{1,0},{2,1},{3,2},{4,7},{5,4},{6,5},{7,6},{8,11},{9,8},{10,9... | collective-permute-start | bytes 884744 | tf_op jit(solution)/shard_map/ppermute | solution.py:437
  6.4 0.0 copy-start
  6.5 0.0 copy-start.1
  6.5 0.0 copy-start.2
  6.5 1.0 collective-permute-start.2
  7.5 6.2 %attend.1 = bf16[512,512]{1,0:T(8,128)(2,1)} custom-call(s32[1,16]{1,0:T(1,128)} %table_hbm.1, s32[1,8]{1,0:T(1,128)} %length_hbm.1, bf16[8,36864]{1,0:T(8,128)(2,1)} %query_hbm.1, bf16[8,576]{1,0:T(8,128)(2,1)} %fresh_hbm.1, bf16[16,36864]{1,0:T(8,128)(2,1)} %cache_hbm.1), custom_call_target="tpu_custom_call" | custom-call | flops 1400000000 | bytes 2400000 | tf_op jit(solution)/shard_map/attend/pallas_call | solution.py:142
  13.7 0.0 collective-permute-done.2.far_ref
  13.7 0.0 collective-permute-done.refs_2_
  13.7 0.0 collective-permute-done.1.refs_7_
  13.8 7.7 %all-to-all-start = ((bf16[16,32,512]{2,1,0:T(8,128)(2,1)}), bf16[16,32,512]{2,1,0:T(8,128)(2,1)S(1)}, u32[]{:S(2)}, u32[]{:S(2)}) async-start(bf16[16,32,512]{2,1,0:T(8,128)(2,1)} %bitcast.22), calls=%async_computation | async-start | bytes 1048576 | tf_op jit(solution)/shard_map/all_to_all | solution.py:479
  21.5 0.0 copy-done
  21.5 1.8 %collective-permute-start.6 = (bf16[64,2304]{1,0:T(8,128)(2,1)S(1)}, bf16[64,2304]{1,0:T(8,128)(2,1)S(1)}, u32[]{:S(2)}, u32[]{:S(2)}) collective-permute-start(bf16[64,2304]{1,0:T(8,128)(2,1)S(1)} %copy-done), channel_id=1, source_target_pairs={{0,3},{1,0},{2,1},{3,2},{4,7},{5,4},{6,5},{7,6},{8,11},{9,8},{10,9... | collective-permute-start | bytes 884744 | tf_op jit(solution)/shard_map/ppermute | solution.py:437
  23.3 0.0 copy-done.1
  23.3 0.0 collective-permute-start.3
  23.3 0.0 collective-permute-start.4
  23.3 2.7 %collective-permute-start.5 = (bf16[64,2304]{1,0:T(8,128)(2,1)S(1)}, bf16[64,2304]{1,0:T(8,128)(2,1)S(1)}, u32[]{:S(2)}, u32[]{:S(2)}) collective-permute-start(bf16[64,2304]{1,0:T(8,128)(2,1)S(1)} %collective-permute-done.1.refs_7_), channel_id=1, source_target_pairs={{0,3},{1,0},{2,1},{3,2},{4,7},{5,4},{6,5},{7,6},{8,11},{9,8},{10,9... | collective-permute-start | bytes 884744 | tf_op jit(solution)/shard_map/ppermute | solution.py:437
  26.0 0.0 copy-done.2
  26.0 0.4 route.1
  26.4 5.7 %all-to-all-done = bf16[16,32,512]{2,1,0:T(8,128)(2,1)S(1)} async-done(((bf16[16,32,512]{2,1,0:T(8,128)(2,1)}), bf16[16,32,512]{2,1,0:T(8,128)(2,1)S(1)}, u32[]{:S(2)}, u32[]{:S(2)}) %all-to-all-start) | async-done | bytes 524320 | tf_op jit(solution)/shard_map/all_to_all | solution.py:479
  32.0 0.0 collective-permute-done.6.refs_6_
  32.0 0.0 collective-permute-done.3.refs_3_
  32.0 5.0 %collective-permute-done.4.refs_4_ = bf16[64,2304]{1,0:T(8,128)(2,1)S(1)} collective-permute-done((bf16[64,2304]{1,0:T(8,128)(2,1)S(1)}, bf16[64,2304]{1,0:T(8,128)(2,1)S(1)}, u32[]{:S(2)}, u32[]{:S(2)}) %collective-permute-start.4) | collective-permute-done | bytes 294944 | tf_op jit(solution)/shard_map/ppermute | solution.py:437
  37.0 0.0 collective-permute-done.5.refs_5_
  37.0 0.9 find_values.1.own_values
  37.9 3.3 %collective-permute-start.7 = (bf16[128,512]{1,0:T(8,128)(2,1)S(1)}, bf16[128,512]{1,0:T(8,128)(2,1)S(1)}, u32[]{:S(2)}, u32[]{:S(2)}) collective-permute-start(bf16[128,512]{1,0:T(8,128)(2,1)S(1)} %find_values.1.own_values), channel_id=1, source_target_pairs={{0,64},{64,0},{1,65},{65,1},{2,66},{66,2},{3,67},{67,3},{4,68},{68... | collective-permute-start | bytes 393224 | tf_op jit(solution)/shard_map/ppermute | solution.py:441
  41.2 1.0 collective-permute-done.7.far_values
  42.2 1.5 project.1
  43.6 0.0 copy-start.3
  43.6 21.6 %all_to_all.20 = bf16[16,16,1792]{2,1,0:T(8,128)(2,1)S(1)} all-to-all(bf16[16,16,1792]{2,1,0:T(8,128)(2,1)S(1)} %bitcast.17), channel_id=1, replica_groups=mesh['core'=2,'z'=4,'x'=4,'y'=4] {'z','x'}, dimensions={0} | all-to-all | bytes 1835008 | tf_op jit(solution)/shard_map/all_to_all | solution.py:489
  65.3 0.1 convert_reduce_fusion
  65.4 1.6 %collective-permute-start.8 = (f32[16,1792]{1,0:T(8,128)S(1)}, f32[16,1792]{1,0:T(8,128)S(1)}, u32[]{:S(2)}, u32[]{:S(2)}) collective-permute-start(f32[16,1792]{1,0:T(8,128)S(1)} %convert_reduce_fusion), channel_id=1, source_target_pairs={{0,64},{64,0},{1,65},{65,1},{2,66},{66,2},{3,67},{67,3},{4,68},{68... | collective-permute-start | bytes 344072 | tf_op jit(solution)/shard_map/ppermute | solution.py:441
  67.0 0.1 collective-permute-start.9
  67.1 0.9 collective-permute-done.8
  68.0 0.4 collective-permute-start.10
  68.5 0.2 collective-permute-start.11
  68.6 0.1 multiply_reduce_fusion
  68.8 0.0 copy-done.3
  68.8 0.1 multiply_convert_fusion
  68.9 0.7 fusion
  69.5 30.6 %all_to_all.21 = bf16[64,8,1792]{2,1,0:T(8,128)(2,1)} all-to-all(bf16[64,8,1792]{2,1,0:T(8,128)(2,1)S(1)} %fusion), channel_id=1, replica_groups=mesh['core'=2,'z'=4,'x'=4,'y'=4] {'z','x','y'}, dimensions={0} | all-to-all | bytes 3670016 | tf_op jit(solution)/shard_map/all_to_all | solution.py:511
  100.1 0.0 collective-permute-done.9.gate_far
  100.1 0.0 collective-permute-done.10.up_far
  100.1 0.0 collective-permute-done.11.down_far
  100.1 13.0 %expert.1 = bf16[512,1792]{1,0:T(8,128)(2,1)} custom-call(bf16[512,1792]{1,0:T(8,128)(2,1)} %bitcast.19, bf16[2,3584,512]{2,1,0:T(8,128)(2,1)} %gate_ref, bf16[2,3584,512]{2,1,0:T(8,128)(2,1)} %up_ref, bf16[2,512,3584]{2,1,0:T(8,128)(2,1)} %down_ref, bf16[2,3584,512]{2,1,0:T(8,128)(2,1)} %collective-permute-done.9.gate_far, ...), custom_call_target="tpu_custom_call" | custom-call | flops 7500000256 | bytes 26000000 | tf_op jit(solution)/shard_map/expert/pallas_call | solution.py:415
  113.1 30.4 %all_to_all.22 = bf16[64,8,1792]{2,1,0:T(8,128)(2,1)S(1)} all-to-all(bf16[64,8,1792]{2,1,0:T(8,128)(2,1)} %bitcast.20), channel_id=1, replica_groups=mesh['core'=2,'z'=4,'x'=4,'y'=4] {'z','x','y'}, dimensions={0} | all-to-all | bytes 3670016 | tf_op jit(solution)/shard_map/all_to_all | solution.py:513
  143.5 0.4 fusion.1
  144.0 3.5 %collective-permute-start.12 = (f32[8,3584]{1,0:T(8,128)S(1)}, f32[8,3584]{1,0:T(8,128)S(1)}, u32[]{:S(2)}, u32[]{:S(2)}) collective-permute-start(f32[8,3584]{1,0:T(8,128)S(1)} %bitcast.24), channel_id=1, source_target_pairs={{0,64},{64,0},{1,65},{65,1},{2,66},{66,2},{3,67},{67,3},{4,68},{68... | collective-permute-start | bytes 344072 | tf_op jit(solution)/shard_map/ppermute | solution.py:441
  147.6 0.6 slice.40
  148.2 0.3 collective-permute-done.12
  148.5 0.6 add_convert_fusion
  (6 shorter events, 0.1 us)
Async XLA Ops:
  2.7 11.0 %collective-permute-start = (bf16[64,2304]{1,0:T(8,128)(2,1)}, bf16[64,2304]{1,0:T(8,128)(2,1)S(1)}, u32[]{:S(2)}, u32[]{:S(2)}) collective-permute-start(bf16[64,2304]{1,0:T(8,128)(2,1)} %get-tuple-element.19.refs_0_), channel_id=1, source_target_pairs={{0,1},{1,2},{2,3},{3,0},{4,5},{5,6},{6,7},{7,4},{8,9},{9,10},{10,1... | collective-permute-start | bytes 884744 | tf_op jit(solution)/shard_map/ppermute | solution.py:437
  4.9 8.8 %collective-permute-start.1 = (bf16[64,2304]{1,0:T(8,128)(2,1)}, bf16[64,2304]{1,0:T(8,128)(2,1)S(1)}, u32[]{:S(2)}, u32[]{:S(2)}) collective-permute-start(bf16[64,2304]{1,0:T(8,128)(2,1)} %get-tuple-element.20.refs_1_), channel_id=1, source_target_pairs={{0,3},{1,0},{2,1},{3,2},{4,7},{5,4},{6,5},{7,6},{8,11},{9,8},{10,9... | collective-permute-start | bytes 884744 | tf_op jit(solution)/shard_map/ppermute | solution.py:437
  6.4 15.0 %copy-start = (bf16[64,2304]{1,0:T(8,128)(2,1)S(1)}, bf16[64,2304]{1,0:T(8,128)(2,1)}, u32[]{:S(2)}) copy-start(bf16[64,2304]{1,0:T(8,128)(2,1)} %get-tuple-element.19.refs_0_) | copy-start | bytes 884740
  6.5 16.8 %copy-start.1 = (bf16[64,2304]{1,0:T(8,128)(2,1)S(1)}, bf16[64,2304]{1,0:T(8,128)(2,1)}, u32[]{:S(2)}) copy-start(bf16[64,2304]{1,0:T(8,128)(2,1)} %get-tuple-element.20.refs_1_) | copy-start | bytes 884740
  6.5 19.5 %copy-start.2 = (f32[8,128]{1,0:T(8,128)S(1)}, f32[8,128]{1,0:T(8,128)}, u32[]{:S(2)}) copy-start(f32[8,128]{1,0:T(8,128)} %get-tuple-element.21.own_ref) | copy-start | bytes 12292
  6.5 7.3 %collective-permute-start.2 = (f32[8,128]{1,0:T(8,128)}, f32[8,128]{1,0:T(8,128)S(1)}, u32[]{:S(2)}, u32[]{:S(2)}) collective-permute-start(f32[8,128]{1,0:T(8,128)} %get-tuple-element.21.own_ref), channel_id=1, source_target_pairs={{0,64},{64,0},{1,65},{65,1},{2,66},{66,2},{3,67},{67,3},{4,68},{68... | collective-permute-start | bytes 12296 | tf_op jit(solution)/shard_map/ppermute | solution.py:441
  13.8 18.3 %all-to-all-start = ((bf16[16,32,512]{2,1,0:T(8,128)(2,1)}), bf16[16,32,512]{2,1,0:T(8,128)(2,1)S(1)}, u32[]{:S(2)}, u32[]{:S(2)}) async-start(bf16[16,32,512]{2,1,0:T(8,128)(2,1)} %bitcast.22), calls=%async_computation | async-start | bytes 1048576 | tf_op jit(solution)/shard_map/all_to_all | solution.py:479
  21.5 10.6 %collective-permute-start.6 = (bf16[64,2304]{1,0:T(8,128)(2,1)S(1)}, bf16[64,2304]{1,0:T(8,128)(2,1)S(1)}, u32[]{:S(2)}, u32[]{:S(2)}) collective-permute-start(bf16[64,2304]{1,0:T(8,128)(2,1)S(1)} %copy-done), channel_id=1, source_target_pairs={{0,3},{1,0},{2,1},{3,2},{4,7},{5,4},{6,5},{7,6},{8,11},{9,8},{10,9... | collective-permute-start | bytes 884744 | tf_op jit(solution)/shard_map/ppermute | solution.py:437
  23.3 8.8 %collective-permute-start.3 = (bf16[64,2304]{1,0:T(8,128)(2,1)S(1)}, bf16[64,2304]{1,0:T(8,128)(2,1)S(1)}, u32[]{:S(2)}, u32[]{:S(2)}) collective-permute-start(bf16[64,2304]{1,0:T(8,128)(2,1)S(1)} %copy-done.1), channel_id=1, source_target_pairs={{0,1},{1,2},{2,3},{3,0},{4,5},{5,6},{6,7},{7,4},{8,9},{9,10},{10,1... | collective-permute-start | bytes 884744 | tf_op jit(solution)/shard_map/ppermute | solution.py:437
  23.3 13.8 %collective-permute-start.4 = (bf16[64,2304]{1,0:T(8,128)(2,1)S(1)}, bf16[64,2304]{1,0:T(8,128)(2,1)S(1)}, u32[]{:S(2)}, u32[]{:S(2)}) collective-permute-start(bf16[64,2304]{1,0:T(8,128)(2,1)S(1)} %collective-permute-done.refs_2_), channel_id=1, source_target_pairs={{0,1},{1,2},{2,3},{3,0},{4,5},{5,6},{6,7},{7,4},{8,9},{9,10},{10,1... | collective-permute-start | bytes 884744 | tf_op jit(solution)/shard_map/ppermute | solution.py:437
  23.3 13.8 %collective-permute-start.5 = (bf16[64,2304]{1,0:T(8,128)(2,1)S(1)}, bf16[64,2304]{1,0:T(8,128)(2,1)S(1)}, u32[]{:S(2)}, u32[]{:S(2)}) collective-permute-start(bf16[64,2304]{1,0:T(8,128)(2,1)S(1)} %collective-permute-done.1.refs_7_), channel_id=1, source_target_pairs={{0,3},{1,0},{2,1},{3,2},{4,7},{5,4},{6,5},{7,6},{8,11},{9,8},{10,9... | collective-permute-start | bytes 884744 | tf_op jit(solution)/shard_map/ppermute | solution.py:437
  37.9 4.3 %collective-permute-start.7 = (bf16[128,512]{1,0:T(8,128)(2,1)S(1)}, bf16[128,512]{1,0:T(8,128)(2,1)S(1)}, u32[]{:S(2)}, u32[]{:S(2)}) collective-permute-start(bf16[128,512]{1,0:T(8,128)(2,1)S(1)} %find_values.1.own_values), channel_id=1, source_target_pairs={{0,64},{64,0},{1,65},{65,1},{2,66},{66,2},{3,67},{67,3},{4,68},{68... | collective-permute-start | bytes 393224 | tf_op jit(solution)/shard_map/ppermute | solution.py:441
  43.6 25.1 %copy-start.3 = (f32[3584]{0:T(1024)S(1)}, f32[3584]{0:T(1024)}, u32[]{:S(2)}) copy-start(f32[3584]{0:T(1024)} %param.20) | copy-start | bytes 43012
  65.4 2.6 %collective-permute-start.8 = (f32[16,1792]{1,0:T(8,128)S(1)}, f32[16,1792]{1,0:T(8,128)S(1)}, u32[]{:S(2)}, u32[]{:S(2)}) collective-permute-start(f32[16,1792]{1,0:T(8,128)S(1)} %convert_reduce_fusion), channel_id=1, source_target_pairs={{0,64},{64,0},{1,65},{65,1},{2,66},{66,2},{3,67},{67,3},{4,68},{68... | collective-permute-start | bytes 344072 | tf_op jit(solution)/shard_map/ppermute | solution.py:441
  67.0 33.1 %collective-permute-start.9 = (bf16[2,3584,512]{2,1,0:T(8,128)(2,1)}, bf16[2,3584,512]{2,1,0:T(8,128)(2,1)}, u32[]{:S(2)}, u32[]{:S(2)}) collective-permute-start(bf16[2,3584,512]{2,1,0:T(8,128)(2,1)} %gate_ref), channel_id=1, source_target_pairs={{0,64},{64,0},{1,65},{65,1},{2,66},{66,2},{3,67},{67,3},{4,68},{68... | collective-permute-start | bytes 22020104 | tf_op jit(solution)/shard_map/ppermute | solution.py:441
  68.0 32.1 %collective-permute-start.10 = (bf16[2,3584,512]{2,1,0:T(8,128)(2,1)}, bf16[2,3584,512]{2,1,0:T(8,128)(2,1)}, u32[]{:S(2)}, u32[]{:S(2)}) collective-permute-start(bf16[2,3584,512]{2,1,0:T(8,128)(2,1)} %up_ref), channel_id=1, source_target_pairs={{0,64},{64,0},{1,65},{65,1},{2,66},{66,2},{3,67},{67,3},{4,68},{68... | collective-permute-start | bytes 22020104 | tf_op jit(solution)/shard_map/ppermute | solution.py:441
  68.5 31.7 %collective-permute-start.11 = (bf16[2,512,3584]{2,1,0:T(8,128)(2,1)}, bf16[2,512,3584]{2,1,0:T(8,128)(2,1)}, u32[]{:S(2)}, u32[]{:S(2)}) collective-permute-start(bf16[2,512,3584]{2,1,0:T(8,128)(2,1)} %down_ref), channel_id=1, source_target_pairs={{0,64},{64,0},{1,65},{65,1},{2,66},{66,2},{3,67},{67,3},{4,68},{68... | collective-permute-start | bytes 22020104 | tf_op jit(solution)/shard_map/ppermute | solution.py:441
  144.0 4.5 %collective-permute-start.12 = (f32[8,3584]{1,0:T(8,128)S(1)}, f32[8,3584]{1,0:T(8,128)S(1)}, u32[]{:S(2)}, u32[]{:S(2)}) collective-permute-start(f32[8,3584]{1,0:T(8,128)S(1)} %bitcast.24), channel_id=1, source_target_pairs={{0,64},{64,0},{1,65},{65,1},{2,66},{66,2},{3,67},{67,3},{4,68},{68... | collective-permute-start | bytes 344072 | tf_op jit(solution)/shard_map/ppermute | solution.py:441

commit v3 on v2

--- a/solution.py
+++ b/solution.py
@@ -161,20 +161,19 @@
     )(block_table, lengths, queries, new_latent, latent_cache)
 
 
-def prepare_kernel(
-    out_proj, value_up, ids_hbm, affinity_hbm, top, bottom, routes, ids, affinity, sems
-):
+def prepare_kernel(out_proj, value_up, ids_hbm, affinity_hbm, piece, routes, ids, affinity, sems):
     core = lax.axis_index("core")
     head_rows, half = out_proj.shape[0], out_proj.shape[1] // 2
     at = pl.ds(pl.multiple_of(core * half, 128), half)
-    middle = head_rows // 2
-    moves = [(ids_hbm, ids), (affinity_hbm, affinity)]
-    for i, part in enumerate((top, bottom)):
-        moves.append((out_proj.at[pl.ds(i * middle, middle), at], part.at[:, :half]))
-        for b in range(value_up.shape[1] // head_rows):
-            rows = pl.ds(b * head_rows + i * middle, middle)
-            columns = pl.ds(half + b * head_rows, head_rows)
-            moves.append((value_up.at[0, rows], part.at[:, columns]))
+    moves = [
+        (ids_hbm, ids),
+        (affinity_hbm, affinity),
+        (out_proj.at[:, at], piece.at[:, :half]),
+    ]
+    for b in range(value_up.shape[1] // head_rows):
+        rows = pl.ds(b * head_rows, head_rows)
+        columns = pl.ds(half + b * head_rows, head_rows)
+        moves.append((value_up.at[0, rows], piece.at[:, columns]))
     copies = [pltpu.make_async_copy(a, b, sems.at[i]) for i, (a, b) in enumerate(moves)]
     for copy in copies:
         copy.start()
@@ -192,16 +191,15 @@
     return pl.pallas_call(
         prepare_kernel,
         out_shape=(
-            jax.ShapeDtypeStruct((head_rows // 2, width // 2 + value_up.shape[1]), BF16),
-            jax.ShapeDtypeStruct((head_rows // 2, width // 2 + value_up.shape[1]), BF16),
+            jax.ShapeDtypeStruct((head_rows, width // 2 + value_up.shape[1]), BF16),
             jax.ShapeDtypeStruct((expert_ids.shape[0], 128), F32),
         ),
         in_specs=[HBM] * 4,
-        out_specs=(VMEM, VMEM, VMEM),
+        out_specs=(VMEM, VMEM),
         scratch_shapes=[
             pltpu.VMEM(expert_ids.shape, jnp.int32),
             pltpu.VMEM(affinity.shape, F32),
-            pltpu.SemaphoreType.DMA((4 + 2 * (value_up.shape[1] // head_rows),)),
+            pltpu.SemaphoreType.DMA((3 + value_up.shape[1] // head_rows,)),
         ],
         compiler_params=pltpu.CompilerParams(vmem_limit_bytes=60 * MIB),
         cost_estimate=pl.CostEstimate(flops=0, bytes_accessed=1_200_000, transcendentals=0),
@@ -273,23 +271,25 @@
     place_y = lax.axis_index("y")
     rows, kv_width = arrived_ref.shape
     tokens = rows // SIDE
-    head_rows = 2 * piece_refs[0].shape[0]
+    head_rows = piece_refs[0].shape[0]
     half = piece_refs[0].shape[1] - kv_width
     to = lax.broadcasted_iota(jnp.int32, (tokens, rows), 0)
     source = lax.broadcasted_iota(jnp.int32, (tokens, rows), 1)
     plane, seq = to // 8, to % 8
     arrived = arrived_ref[...]
-    ups = [
-        jnp.concatenate([piece_refs[2 * k][:, half:], piece_refs[2 * k + 1][:, half:]], axis=0)
-        for k in range(SIDE)
-    ]
-    for k, up in enumerate(ups):
+    own, one, top, bottom, three = piece_refs
+    for k in range(SIDE):
         head = lax.rem(place_y - k + SIDE, SIDE)
         pick = (source == plane * (SIDE * 8) + head * 8 + seq).astype(F32)
         latent = dot(pick.astype(BF16), arrived).astype(BF16)
         total = jnp.zeros((tokens, head_rows), F32)
         for at in range(0, kv_width, head_rows):
-            total = total + dot(latent[:, at : at + head_rows], up[:, at : at + head_rows])
+            columns = slice(half + at, half + at + head_rows)
+            if k == 2:
+                up = jnp.concatenate([top[:, columns], bottom[:, columns]], axis=0)
+            else:
+                up = (own, one, None, three)[k][:, columns]
+            total = total + dot(latent[:, at : at + head_rows], up)
         out_ref[:, k * head_rows : (k + 1) * head_rows] = total.astype(BF16)
 
 
@@ -297,8 +297,8 @@
     rows = arrived.shape[0]
     return pl.pallas_call(
         value_kernel,
-        out_shape=jax.ShapeDtypeStruct((rows // SIDE, 2 * SIDE * pieces[0].shape[0]), BF16),
-        in_specs=[VMEM] * 9,
+        out_shape=jax.ShapeDtypeStruct((rows // SIDE, SIDE * pieces[0].shape[0]), BF16),
+        in_specs=[VMEM] * 6,
         out_specs=VMEM,
         compiler_params=pltpu.CompilerParams(vmem_limit_bytes=12 * MIB),
         cost_estimate=pl.CostEstimate(
@@ -309,9 +309,9 @@
 
 
 def project_kernel(own_values, far_values, *refs):
-    *piece_refs, out_ref = refs
-    rows, width = own_values.shape
-    head_rows = 2 * piece_refs[0].shape[0]
+    own, one, top, bottom, three, out_ref = refs
+    rows = own_values.shape[0]
+    head_rows = own.shape[0]
     half = out_ref.shape[1]
     to = lax.broadcasted_iota(jnp.int32, (2 * rows, rows), 0)
     source = lax.broadcasted_iota(jnp.int32, (2 * rows, rows), 1)
@@ -323,10 +323,8 @@
     for at in range(0, half, step):
         total = jnp.zeros((2 * rows, step), F32)
         columns = slice(at, at + step)
-        for k in range(SIDE):
-            part = jnp.concatenate(
-                [piece_refs[2 * k][:, columns], piece_refs[2 * k + 1][:, columns]], axis=0
-            )
+        two = jnp.concatenate([top[:, columns], bottom[:, columns]], axis=0)
+        for k, part in enumerate((own[:, columns], one[:, columns], two, three[:, columns])):
             total = total + dot(values[:, k * head_rows : (k + 1) * head_rows], part)
         out_ref[:, at : at + step] = total.astype(BF16)
 
@@ -335,7 +333,7 @@
     return pl.pallas_call(
         project_kernel,
         out_shape=jax.ShapeDtypeStruct((2 * own_values.shape[0], half), BF16),
-        in_specs=[VMEM] * 10,
+        in_specs=[VMEM] * 7,
         out_specs=VMEM,
         compiler_params=pltpu.CompilerParams(vmem_limit_bytes=12 * MIB),
         cost_estimate=pl.CostEstimate(
@@ -346,8 +344,8 @@
 
 
 def expert_kernel(
-    rows_ref, gate_ref, up_ref, down_ref, gate_far, up_far, down_far, out_ref,
-    gate_buf, up_buf, down_buf, wide_ref, total_ref, sems,
+    rows_hbm, gate_far, up_far, down_far, gate_near, up_near, down_near, out_hbm,
+    rows_ref, out_ref, gate_buf, up_buf, down_buf, wide_ref, total_ref, sems, edge_sems,
 ):
     core = lax.axis_index("core")
     blocks, width, block = gate_buf.shape
@@ -356,32 +354,56 @@
 
     def copies(i):
         near = i < blocks // 2
+        gate, up, down = (gate_near, up_near, down_near) if near else (gate_far, up_far, down_far)
         at = pl.ds((i % (blocks // 2)) * block, block)
-        gate, up, down = (gate_ref, up_ref, down_ref) if near else (gate_far, up_far, down_far)
         return (
             pltpu.make_async_copy(gate.at[core, :, at], gate_buf.at[i], sems.at[0, i]),
             pltpu.make_async_copy(up.at[core, :, at], up_buf.at[i], sems.at[1, i]),
             pltpu.make_async_copy(down.at[core, at, :], down_buf.at[i], sems.at[2, i]),
         )
 
+    step = 256
+    edges = range(0, half, step)
+
+    def chunk(at):
+        return slice(None), pl.ds(at, step)
+
+    arriving = [
+        pltpu.make_async_copy(rows_hbm.at[chunk(at)], rows_ref.at[chunk(at)], edge_sems.at[0, i])
+        for i, at in enumerate(edges)
+    ]
+    leaving = [
+        pltpu.make_async_copy(out_ref.at[chunk(at)], out_hbm.at[chunk(at)], edge_sems.at[1, i])
+        for i, at in enumerate(edges)
+    ]
+    for copy in arriving:
+        copy.start()
     started = [copies(i) for i in range(blocks)]
-    for three in started:
-        for copy in three:
-            copy.start()
+    started[0][0].start()
+    started[0][1].start()
 
     to = lax.broadcasted_iota(jnp.int32, (count, 2 * count), 0)
     source = lax.broadcasted_iota(jnp.int32, (count, 2 * count), 1)
-    step = 256
-    for side in range(2):
-        pick = (source == to // 4 * 8 + to % 4 + 4 * side).astype(F32).astype(BF16)
-        for at in range(0, half, step):
+    picks = [
+        (source == to // 4 * 8 + to % 4 + 4 * side).astype(F32).astype(BF16) for side in range(2)
+    ]
+    for i, at in enumerate(edges):
+        arriving[i].wait()
+        for side in range(2):
             wide_ref[:, side * half + at : side * half + at + step] = dot(
-                pick, rows_ref[:, at : at + step]
+                picks[side], rows_ref[:, at : at + step]
             ).astype(BF16)
+
+    started[0][2].start()
+    for copy in started[1]:
+        copy.start()
 
     for i in range(blocks):
         started[i][0].wait()
         started[i][1].wait()
+        if i + 2 < blocks:
+            for copy in started[i + 2]:
+                copy.start()
         gate = dot(wide_ref[...], gate_buf[i])
         up = dot(wide_ref[...], up_buf[i])
         hidden = (gate / (1.0 + jnp.exp(-gate)) * up).astype(BF16)
@@ -395,42 +417,45 @@
 
     to = lax.broadcasted_iota(jnp.int32, (2 * count, count), 0)
     source = lax.broadcasted_iota(jnp.int32, (2 * count, count), 1)
-    first = (to % 8 < 4) & (source == to // 8 * 4 + to % 4)
-    second = (to % 8 >= 4) & (source == to // 8 * 4 + to % 4)
-    first = first.astype(F32).astype(BF16)
-    second = second.astype(F32).astype(BF16)
-    for at in range(0, half, step):
+    same = source == to // 8 * 4 + to % 4
+    first = ((to % 8 < 4) & same).astype(F32).astype(BF16)
+    second = ((to % 8 >= 4) & same).astype(F32).astype(BF16)
+    for i, at in enumerate(edges):
         out_ref[:, at : at + step] = (
             dot(first, total_ref[:, at : at + step].astype(BF16))
             + dot(second, total_ref[:, half + at : half + at + step].astype(BF16))
         ).astype(BF16)
+        leaving[i].start()
+    for copy in leaving:
+        copy.wait()
 
 
 def run_expert(rows, near, far):
-    width = near[2].shape[2]
-    hidden = near[2].shape[1]
-    block = 256
+    _, hidden, width = near[2].shape
+    count, block = rows.shape[0] // 2, 256
     blocks = 2 * hidden // block
-    count = rows.shape[0] // 2
     return pl.pallas_call(
         expert_kernel,
         out_shape=jax.ShapeDtypeStruct(rows.shape, BF16),
-        in_specs=[VMEM] + [HBM] * 6,
-        out_specs=VMEM,
+        in_specs=[HBM] * 7,
+        out_specs=HBM,
         scratch_shapes=[
+            pltpu.VMEM(rows.shape, BF16),
+            pltpu.VMEM(rows.shape, BF16),
             pltpu.VMEM((blocks, width, block), BF16),
             pltpu.VMEM((blocks, width, block), BF16),
             pltpu.VMEM((blocks, block, width), BF16),
             pltpu.VMEM((count, width), BF16),
             pltpu.VMEM((count, width), F32),
             pltpu.SemaphoreType.DMA((3, blocks)),
+            pltpu.SemaphoreType.DMA((2, rows.shape[1] // 256)),
         ],
-        compiler_params=pltpu.CompilerParams(vmem_limit_bytes=57 * MIB),
+        compiler_params=pltpu.CompilerParams(vmem_limit_bytes=58 * MIB),
         cost_estimate=pl.CostEstimate(
             flops=7_500_000_000, bytes_accessed=26_000_000, transcendentals=300_000
         ),
         name="expert",
-    )(rows, *near, *far)
+    )(rows, *far, *near)
 
 
 def along_y(array, step):
@@ -464,29 +489,30 @@
     planes = SIDE * SIDE
     chips = SIDE**3
 
-    top, bottom, routes = prepare(out_proj, value_up, expert_ids, affinity)
-    one_top, three_bottom = along_y(top, 1), along_y(bottom, -1)
+    piece, routes = prepare(out_proj, value_up, expert_ids, affinity)
+    one, three = along_y(piece, 1), along_y(piece, -1)
+    middle = head_rows // 2
+    two_top, two_bottom = along_y(one[:middle], 1), along_y(three[middle:], -1)
+    pieces = (piece, one, two_top, two_bottom, three)
+    routes, pieces = lax.optimization_barrier((routes, pieces))
     far_routes = other_core(routes)
 
     latent = attend(block_table, lengths, queries, new_latent, latent_cache, kv_width)
     outbound = latent.reshape(planes, SIDE * seq_count, kv_width)
-    outbound, one_top, three_bottom, far_routes = lax.optimization_barrier(
-        (outbound, one_top, three_bottom, far_routes)
-    )
-    two_top, two_bottom = along_y(one_top, 1), along_y(three_bottom, -1)
-    one_bottom, three_top = along_y(bottom, 1), along_y(top, -1)
-    pieces = (top, bottom, one_top, one_bottom, two_top, two_bottom, three_top, three_bottom)
     arrived = lax.all_to_all(outbound, ("z", "x"), split_axis=0, concat_axis=0, tiled=True)
     arrived = arrived.reshape(planes * SIDE * seq_count, kv_width)
     placement, mixing = route(routes, far_routes, chips)
-    arrived, placement, mixing = lax.optimization_barrier((arrived, placement, mixing))
-
     own_values = find_values(arrived, pieces)
-    partial = project(own_values, other_core(own_values), pieces, half)
+    far_values, placement, mixing = lax.optimization_barrier(
+        (other_core(own_values), placement, mixing)
+    )
+    partial = project(own_values, far_values, pieces, half)
+
     partial, gate_weight = lax.optimization_barrier((partial, gate_weight))
     far_gate = other_core(gate_weight)
     partial = partial.reshape(planes, 2 * seq_count, half)
     collected = lax.all_to_all(partial, ("z", "x"), split_axis=0, concat_axis=0, tiled=True)
+    collected, far_gate = lax.optimization_barrier((collected, far_gate))
     mine = jnp.sum(collected.astype(F32), axis=0)
     theirs = other_core(mine)
     theirs = jnp.concatenate([theirs[seq_count:], theirs[:seq_count]], axis=0)
@@ -498,8 +524,8 @@
     attn_out, up_weight, down_weight = lax.optimization_barrier(
         (attn_out, up_weight, down_weight)
     )
+    weights = (gate_weight, up_weight, down_weight)
     far_weights = (far_gate, other_core(up_weight), other_core(down_weight))
-    weights = (gate_weight, up_weight, down_weight)
     mean_square = jnp.mean(attn_out * attn_out, axis=1, keepdims=True)
     both = (attn_out * lax.rsqrt(mean_square + EPSILON) * norm_gain).astype(BF16)
     normed = both[:seq_count]

time: 150 us -> 144 us (0.960)
  starting transfers between devices: 26 us -> 23.1 us
  waiting for transfers between devices: 12.9 us -> 10.3 us
    all_to_all x1, waiting for transfers between devices: 5.66 us -> 0.01 us  [shards(): lax.all_to_all(outbound, ('z', 'x'), split_axis=0, concat_axis=0, tiled=T...]
    ppermute x6 -> x4, waiting for transfers between devices: 5 us -> 7.89 us  [along_y(): lax.ppermute(array, 'y', [(i, (i + step) % SIDE) for i in range(SIDE)])]
    ppermute x6 -> x4, starting transfers between devices: 8.22 us -> 6.45 us  [along_y(): lax.ppermute(array, 'y', [(i, (i + step) % SIDE) for i in range(SIDE)])]
  transfers between devices with their start and end apart: 14 -> 12, of which waited for: 5 -> 5; matrix products, arithmetic and copies ran while one was open for 1% -> 1% of each run, Pallas kernels for 4% -> 5%
where the time goes in v3:
time: 144 us; the launch traced here: 143 us
  blocking collectives  82.6 us (57%)
  Pallas kernels  23.7 us (16%)
  starting transfers between devices  23.1 us (16%)
  waiting for transfers between devices  10.3 us (7%)
    all_to_all x1, blocking collectives, shards(): lax.all_to_all(outgoing, CHIPS, split_axis=0, concat_axis=0, tiled=True)  30.5 us
    all_to_all x1, blocking collectives, shards(): lax.all_to_all(reply.reshape(chips, 8, half), CHIPS, split_axis=0, concat...  30.4 us
    all_to_all x1, blocking collectives, shards(): lax.all_to_all(partial, ('z', 'x'), split_axis=0, concat_axis=0, tiled=True)  21.7 us
    pallas_call x1, Pallas kernels, run_expert(): pl.pallas_call(expert_kernel, out_shape=jax.ShapeDtypeStruct(rows.shape,...  12.8 us
    ppermute x7, starting transfers between devices, other_core(): return lax.ppermute(array, 'core', SWAP)  8.96 us
    ppermute x4, waiting for transfers between devices, along_y(): lax.ppermute(array, 'y', [(i, (i + step) % SIDE) for i in range(SIDE)])  7.89 us
    all_to_all x1, starting transfers between devices, shards(): lax.all_to_all(outbound, ('z', 'x'), split_axis=0, concat_axis=0, tiled=T...  7.74 us
    ppermute x4, starting transfers between devices, along_y(): lax.ppermute(array, 'y', [(i, (i + step) % SIDE) for i in range(SIDE)])  6.45 us
  transfers between devices with their start and end apart: 12, of which 5 were waited for; matrix products, arithmetic and copies ran while one was open for 1% of the time, Pallas kernels for 5%

profile of v3, /device:TPU:1, one launch (start us, length us, event | category | flops | bytes accessed | tf_op | source)
XLA Modules:
  0.0 143.4 jit_solution(15537931499716701575)
XLA Ops:
  0.6 1.9 %prepare.1 = (bf16[128,2304]{1,0:T(8,128)(2,1)}, f32[8,128]{1,0:T(8,128)}) custom-call(bf16[128,3584]{1,0:T(8,128)(2,1)} %out_proj.1, bf16[1,512,128]{2,1,0:T(8,128)(2,1)} %value_up.1, s32[8,8]{1,0:T(8,128)} %ids_hbm.1, f32[8,8]{1,0:T(8,128)} %affinity_hbm.1), custom_call_target="tpu_custom_call" | custom-call | bytes 1200000 | tf_op jit(solution)/shard_map/prepare/pallas_call | solution.py:191
  2.6 3.6 %collective-permute-start.2 = (bf16[128,2304]{1,0:T(8,128)(2,1)}, bf16[128,2304]{1,0:T(8,128)(2,1)S(1)}, u32[]{:S(2)}, u32[]{:S(2)}) collective-permute-start(bf16[128,2304]{1,0:T(8,128)(2,1)} %get-tuple-element.24.refs_0_), channel_id=1, source_target_pairs={{0,3},{1,0},{2,1},{3,2},{4,7},{5,4},{6,5},{7,6},{8,11},{9,8},{10,9... | collective-permute-start | bytes 1769480 | tf_op jit(solution)/shard_map/ppermute | solution.py:462
  6.2 0.0 collective-permute-start
  6.2 6.2 %attend.1 = bf16[512,512]{1,0:T(8,128)(2,1)} custom-call(s32[1,16]{1,0:T(1,128)} %table_hbm.1, s32[1,8]{1,0:T(1,128)} %length_hbm.1, bf16[8,36864]{1,0:T(8,128)(2,1)} %query_hbm.1, bf16[8,576]{1,0:T(8,128)(2,1)} %fresh_hbm.1, bf16[16,36864]{1,0:T(8,128)(2,1)} %cache_hbm.1), custom_call_target="tpu_custom_call" | custom-call | flops 1400000000 | bytes 2400000 | tf_op jit(solution)/shard_map/attend/pallas_call | solution.py:142
  12.4 0.0 copy-start
  12.5 7.7 %all-to-all-start = ((bf16[16,32,512]{2,1,0:T(8,128)(2,1)}), bf16[16,32,512]{2,1,0:T(8,128)(2,1)S(1)}, u32[]{:S(2)}, u32[]{:S(2)}) async-start(bf16[16,32,512]{2,1,0:T(8,128)(2,1)} %bitcast.22), calls=%async_computation | async-start | bytes 1048576 | tf_op jit(solution)/shard_map/all_to_all | solution.py:502
  20.2 0.0 collective-permute-done.2.refs_4_
  20.2 0.0 copy-start.1
  20.3 2.7 %collective-permute-start.3 = (bf16[64,2304]{1,0:T(8,128)(2,1)S(1)}, bf16[64,2304]{1,0:T(8,128)(2,1)S(1)}, u32[]{:S(2)}, u32[]{:S(2)}) collective-permute-start(bf16[64,2304]{1,0:T(8,128)(2,1)S(1)} %slice.47), channel_id=1, source_target_pairs={{0,3},{1,0},{2,1},{3,2},{4,7},{5,4},{6,5},{7,6},{8,11},{9,8},{10,9... | collective-permute-start | bytes 884744 | tf_op jit(solution)/shard_map/ppermute | solution.py:462
  23.0 0.0 collective-permute-done.refs_1_
  23.0 0.1 collective-permute-start.1
  23.1 4.7 %collective-permute-done.3.refs_3_ = bf16[64,2304]{1,0:T(8,128)(2,1)S(1)} collective-permute-done((bf16[64,2304]{1,0:T(8,128)(2,1)S(1)}, bf16[64,2304]{1,0:T(8,128)(2,1)S(1)}, u32[]{:S(2)}, u32[]{:S(2)}) %collective-permute-start.3) | collective-permute-done | bytes 294944 | tf_op jit(solution)/shard_map/ppermute | solution.py:462
  27.8 3.2 %collective-permute-done.1.refs_2_ = bf16[64,2304]{1,0:T(8,128)(2,1)S(1)} collective-permute-done((bf16[64,2304]{1,0:T(8,128)(2,1)S(1)}, bf16[64,2304]{1,0:T(8,128)(2,1)S(1)}, u32[]{:S(2)}, u32[]{:S(2)}) %collective-permute-start.1) | collective-permute-done | bytes 294944 | tf_op jit(solution)/shard_map/ppermute | solution.py:462
  31.0 0.0 all-to-all-done
  31.0 0.0 copy-done
  31.0 0.9 find_values.1.own_values
  31.9 2.8 %collective-permute-start.4 = (bf16[128,512]{1,0:T(8,128)(2,1)S(1)}, bf16[128,512]{1,0:T(8,128)(2,1)S(1)}, u32[]{:S(2)}, u32[]{:S(2)}) collective-permute-start(bf16[128,512]{1,0:T(8,128)(2,1)S(1)} %find_values.1.own_values), channel_id=1, source_target_pairs={{0,64},{64,0},{1,65},{65,1},{2,66},{66,2},{3,67},{67,3},{4,68},{68... | collective-permute-start | bytes 393224 | tf_op jit(solution)/shard_map/ppermute | solution.py:466
  34.7 0.0 copy-done.1
  34.7 0.1 collective-permute-start.5
  34.8 1.1 collective-permute-done.5.far_ref
  35.9 0.4 route.1
  36.3 0.0 collective-permute-done.4.far_values
  36.3 1.5 %project.1 = bf16[256,1792]{1,0:T(8,128)(2,1)S(1)} custom-call(bf16[128,512]{1,0:T(8,128)(2,1)S(1)} %find_values.1.own_values, bf16[128,512]{1,0:T(8,128)(2,1)S(1)} %collective-permute-done.4.far_values, bf16[128,2304]{1,0:T(8,128)(2,1)S(1)} %copy-done, bf16[128,2304]{1,0:T(8,128)(2,1)S(1)} %collective-permute-done.refs_1_, ...), custom_call_target="tpu_custom_call" | custom-call | flops 600000000 | bytes 3000000 | tf_op jit(solution)/shard_map/project/pallas_call | solution.py:333
  37.7 0.3 collective-permute-start.6
  38.0 0.0 copy-start.2
  38.0 21.7 %all_to_all.20 = bf16[16,16,1792]{2,1,0:T(8,128)(2,1)S(1)} all-to-all(bf16[16,16,1792]{2,1,0:T(8,128)(2,1)S(1)} %bitcast.17), channel_id=1, replica_groups=mesh['core'=2,'z'=4,'x'=4,'y'=4] {'z','x'}, dimensions={0} | all-to-all | bytes 1835008 | tf_op jit(solution)/shard_map/all_to_all | solution.py:514
  59.7 0.0 collective-permute-done.6.gate_far
  59.7 0.1 convert_reduce_fusion
  59.8 1.7 %collective-permute-start.7 = (f32[16,1792]{1,0:T(8,128)S(1)}, f32[16,1792]{1,0:T(8,128)S(1)}, u32[]{:S(2)}, u32[]{:S(2)}) collective-permute-start(f32[16,1792]{1,0:T(8,128)S(1)} %convert_reduce_fusion), channel_id=1, source_target_pairs={{0,64},{64,0},{1,65},{65,1},{2,66},{66,2},{3,67},{67,3},{4,68},{68... | collective-permute-start | bytes 344072 | tf_op jit(solution)/shard_map/ppermute | solution.py:466
  61.5 1.0 collective-permute-done.7
  62.5 0.4 collective-permute-start.8
  63.0 0.2 collective-permute-start.9
  63.1 0.1 multiply_reduce_fusion
  63.3 0.0 copy-done.2
  63.3 0.1 multiply_convert_fusion
  63.4 0.7 fusion
  64.0 30.5 %all_to_all.21 = bf16[64,8,1792]{2,1,0:T(8,128)(2,1)} all-to-all(bf16[64,8,1792]{2,1,0:T(8,128)(2,1)S(1)} %fusion), channel_id=1, replica_groups=mesh['core'=2,'z'=4,'x'=4,'y'=4] {'z','x','y'}, dimensions={0} | all-to-all | bytes 3670016 | tf_op jit(solution)/shard_map/all_to_all | solution.py:537
  94.6 0.0 collective-permute-done.8.up_far
  94.6 0.0 collective-permute-done.9.down_far
  94.6 12.8 %expert.1 = bf16[512,1792]{1,0:T(8,128)(2,1)} custom-call(bf16[512,1792]{1,0:T(8,128)(2,1)} %bitcast.19, bf16[2,3584,512]{2,1,0:T(8,128)(2,1)} %collective-permute-done.6.gate_far, bf16[2,3584,512]{2,1,0:T(8,128)(2,1)} %collective-permute-done.8.up_far, bf16[2,512,3584]{2,1,0:T(8,128)(2,1)} %collective-permute-done.9.down_far, ...), custom_call_target="tpu_custom_call" | custom-call | flops 7500000256 | bytes 26000000 | tf_op jit(solution)/shard_map/expert/pallas_call | solution.py:437
  107.4 30.4 %all_to_all.22 = bf16[64,8,1792]{2,1,0:T(8,128)(2,1)S(1)} all-to-all(bf16[64,8,1792]{2,1,0:T(8,128)(2,1)} %bitcast.20), channel_id=1, replica_groups=mesh['core'=2,'z'=4,'x'=4,'y'=4] {'z','x','y'}, dimensions={0} | all-to-all | bytes 3670016 | tf_op jit(solution)/shard_map/all_to_all | solution.py:539
  137.8 0.4 fusion.1
  138.3 3.5 %collective-permute-start.10 = (f32[8,3584]{1,0:T(8,128)S(1)}, f32[8,3584]{1,0:T(8,128)S(1)}, u32[]{:S(2)}, u32[]{:S(2)}) collective-permute-start(f32[8,3584]{1,0:T(8,128)S(1)} %bitcast.24), channel_id=1, source_target_pairs={{0,64},{64,0},{1,65},{65,1},{2,66},{66,2},{3,67},{67,3},{4,68},{68... | collective-permute-start | bytes 344072 | tf_op jit(solution)/shard_map/ppermute | solution.py:466
  141.8 0.6 slice.50
  142.5 0.3 collective-permute-done.10
  142.8 0.6 add_convert_fusion
  (8 shorter events, 0.1 us)
Async XLA Ops:
  2.6 17.6 %collective-permute-start.2 = (bf16[128,2304]{1,0:T(8,128)(2,1)}, bf16[128,2304]{1,0:T(8,128)(2,1)S(1)}, u32[]{:S(2)}, u32[]{:S(2)}) collective-permute-start(bf16[128,2304]{1,0:T(8,128)(2,1)} %get-tuple-element.24.refs_0_), channel_id=1, source_target_pairs={{0,3},{1,0},{2,1},{3,2},{4,7},{5,4},{6,5},{7,6},{8,11},{9,8},{10,9... | collective-permute-start | bytes 1769480 | tf_op jit(solution)/shard_map/ppermute | solution.py:462
  6.2 16.8 %collective-permute-start = (bf16[128,2304]{1,0:T(8,128)(2,1)}, bf16[128,2304]{1,0:T(8,128)(2,1)S(1)}, u32[]{:S(2)}, u32[]{:S(2)}) collective-permute-start(bf16[128,2304]{1,0:T(8,128)(2,1)} %get-tuple-element.24.refs_0_), channel_id=1, source_target_pairs={{0,1},{1,2},{2,3},{3,0},{4,5},{5,6},{6,7},{7,4},{8,9},{9,10},{10,1... | collective-permute-start | bytes 1769480 | tf_op jit(solution)/shard_map/ppermute | solution.py:462
  12.4 18.6 %copy-start = (bf16[128,2304]{1,0:T(8,128)(2,1)S(1)}, bf16[128,2304]{1,0:T(8,128)(2,1)}, u32[]{:S(2)}) copy-start(bf16[128,2304]{1,0:T(8,128)(2,1)} %get-tuple-element.24.refs_0_) | copy-start | bytes 1769476
  12.5 18.5 %all-to-all-start = ((bf16[16,32,512]{2,1,0:T(8,128)(2,1)}), bf16[16,32,512]{2,1,0:T(8,128)(2,1)S(1)}, u32[]{:S(2)}, u32[]{:S(2)}) async-start(bf16[16,32,512]{2,1,0:T(8,128)(2,1)} %bitcast.22), calls=%async_computation | async-start | bytes 1048576 | tf_op jit(solution)/shard_map/all_to_all | solution.py:502
  20.2 14.4 %copy-start.1 = (f32[8,128]{1,0:T(8,128)S(1)}, f32[8,128]{1,0:T(8,128)}, u32[]{:S(2)}) copy-start(f32[8,128]{1,0:T(8,128)} %get-tuple-element.29.own_ref) | copy-start | bytes 12292
  20.3 7.5 %collective-permute-start.3 = (bf16[64,2304]{1,0:T(8,128)(2,1)S(1)}, bf16[64,2304]{1,0:T(8,128)(2,1)S(1)}, u32[]{:S(2)}, u32[]{:S(2)}) collective-permute-start(bf16[64,2304]{1,0:T(8,128)(2,1)S(1)} %slice.47), channel_id=1, source_target_pairs={{0,3},{1,0},{2,1},{3,2},{4,7},{5,4},{6,5},{7,6},{8,11},{9,8},{10,9... | collective-permute-start | bytes 884744 | tf_op jit(solution)/shard_map/ppermute | solution.py:462
  23.0 8.0 %collective-permute-start.1 = (bf16[64,2304]{1,0:T(8,128)(2,1)S(1)}, bf16[64,2304]{1,0:T(8,128)(2,1)S(1)}, u32[]{:S(2)}, u32[]{:S(2)}) collective-permute-start(bf16[64,2304]{1,0:T(8,128)(2,1)S(1)} %slice.46), channel_id=1, source_target_pairs={{0,1},{1,2},{2,3},{3,0},{4,5},{5,6},{6,7},{7,4},{8,9},{9,10},{10,1... | collective-permute-start | bytes 884744 | tf_op jit(solution)/shard_map/ppermute | solution.py:462
  31.9 4.4 %collective-permute-start.4 = (bf16[128,512]{1,0:T(8,128)(2,1)S(1)}, bf16[128,512]{1,0:T(8,128)(2,1)S(1)}, u32[]{:S(2)}, u32[]{:S(2)}) collective-permute-start(bf16[128,512]{1,0:T(8,128)(2,1)S(1)} %find_values.1.own_values), channel_id=1, source_target_pairs={{0,64},{64,0},{1,65},{65,1},{2,66},{66,2},{3,67},{67,3},{4,68},{68... | collective-permute-start | bytes 393224 | tf_op jit(solution)/shard_map/ppermute | solution.py:466
  34.7 1.2 collective-permute-start.5
  37.7 21.9 %collective-permute-start.6 = (bf16[2,3584,512]{2,1,0:T(8,128)(2,1)}, bf16[2,3584,512]{2,1,0:T(8,128)(2,1)}, u32[]{:S(2)}, u32[]{:S(2)}) collective-permute-start(bf16[2,3584,512]{2,1,0:T(8,128)(2,1)} %gate_near), channel_id=1, source_target_pairs={{0,64},{64,0},{1,65},{65,1},{2,66},{66,2},{3,67},{67,3},{4,68},{68... | collective-permute-start | bytes 22020104 | tf_op jit(solution)/shard_map/ppermute | solution.py:466
  38.0 25.2 %copy-start.2 = (f32[3584]{0:T(1024)S(1)}, f32[3584]{0:T(1024)}, u32[]{:S(2)}) copy-start(f32[3584]{0:T(1024)} %param.20) | copy-start | bytes 43012
  59.8 2.6 %collective-permute-start.7 = (f32[16,1792]{1,0:T(8,128)S(1)}, f32[16,1792]{1,0:T(8,128)S(1)}, u32[]{:S(2)}, u32[]{:S(2)}) collective-permute-start(f32[16,1792]{1,0:T(8,128)S(1)} %convert_reduce_fusion), channel_id=1, source_target_pairs={{0,64},{64,0},{1,65},{65,1},{2,66},{66,2},{3,67},{67,3},{4,68},{68... | collective-permute-start | bytes 344072 | tf_op jit(solution)/shard_map/ppermute | solution.py:466
  62.5 32.1 %collective-permute-start.8 = (bf16[2,3584,512]{2,1,0:T(8,128)(2,1)}, bf16[2,3584,512]{2,1,0:T(8,128)(2,1)}, u32[]{:S(2)}, u32[]{:S(2)}) collective-permute-start(bf16[2,3584,512]{2,1,0:T(8,128)(2,1)} %up_near), channel_id=1, source_target_pairs={{0,64},{64,0},{1,65},{65,1},{2,66},{66,2},{3,67},{67,3},{4,68},{68... | collective-permute-start | bytes 22020104 | tf_op jit(solution)/shard_map/ppermute | solution.py:466
  63.0 31.6 %collective-permute-start.9 = (bf16[2,512,3584]{2,1,0:T(8,128)(2,1)}, bf16[2,512,3584]{2,1,0:T(8,128)(2,1)}, u32[]{:S(2)}, u32[]{:S(2)}) collective-permute-start(bf16[2,512,3584]{2,1,0:T(8,128)(2,1)} %down_near), channel_id=1, source_target_pairs={{0,64},{64,0},{1,65},{65,1},{2,66},{66,2},{3,67},{67,3},{4,68},{68... | collective-permute-start | bytes 22020104 | tf_op jit(solution)/shard_map/ppermute | solution.py:466
  138.3 4.5 %collective-permute-start.10 = (f32[8,3584]{1,0:T(8,128)S(1)}, f32[8,3584]{1,0:T(8,128)S(1)}, u32[]{:S(2)}, u32[]{:S(2)}) collective-permute-start(f32[8,3584]{1,0:T(8,128)S(1)} %bitcast.24), channel_id=1, source_target_pairs={{0,64},{64,0},{1,65},{65,1},{2,66},{66,2},{3,67},{67,3},{4,68},{68... | collective-permute-start | bytes 344072 | tf_op jit(solution)/shard_map/ppermute | solution.py:466

commit v4 on v3

--- a/solution.py
+++ b/solution.py
@@ -10,6 +10,7 @@
 EPSILON = 1e-06
 SIDE = 4
 CHIPS = ("z", "x", "y")
+PLANE = ("x", "z")
 SWAP = [(0, 1), (1, 0)]
 F32 = jnp.float32
 BF16 = jnp.bfloat16
@@ -77,7 +78,7 @@
     fresh = jnp.concatenate(
         [fresh_ref[...].astype(F32), jnp.zeros((seq_count, wide - entry), F32)], axis=1
     )
-    group = 8
+    group = 16
     for g in range(query_ref.shape[1] // (2 * entry) // group):
         base = 2 * entry * group * g
         evens = [
@@ -130,7 +131,9 @@
                 ],
                 axis=0,
             )
-            at = 2 * seq_count * (group * g + i)
+            head = 2 * (group * g + i)
+            across, along, within = head // SIDE**2, head // SIDE % SIDE, head % SIDE
+            at = seq_count * ((along * SIDE + across) * SIDE + within)
             out_ref[at : at + 2 * seq_count, :] = two.astype(BF16)
 
 
@@ -311,7 +314,6 @@
 def project_kernel(own_values, far_values, *refs):
     own, one, top, bottom, three, out_ref = refs
     rows = own_values.shape[0]
-    head_rows = own.shape[0]
     half = out_ref.shape[1]
     to = lax.broadcasted_iota(jnp.int32, (2 * rows, rows), 0)
     source = lax.broadcasted_iota(jnp.int32, (2 * rows, rows), 1)
@@ -321,12 +323,9 @@
     values = (dot(near, own_values[...]) + dot(far, far_values[...])).astype(BF16)
     step = 256
     for at in range(0, half, step):
-        total = jnp.zeros((2 * rows, step), F32)
         columns = slice(at, at + step)
-        two = jnp.concatenate([top[:, columns], bottom[:, columns]], axis=0)
-        for k, part in enumerate((own[:, columns], one[:, columns], two, three[:, columns])):
-            total = total + dot(values[:, k * head_rows : (k + 1) * head_rows], part)
-        out_ref[:, at : at + step] = total.astype(BF16)
+        part = jnp.concatenate([ref[:, columns] for ref in (own, one, top, bottom, three)], axis=0)
+        out_ref[:, columns] = dot(values, part).astype(BF16)
 
 
 def project(own_values, far_values, pieces, half):
@@ -344,8 +343,8 @@
 
 
 def expert_kernel(
-    rows_hbm, gate_far, up_far, down_far, gate_near, up_near, down_near, out_hbm,
-    rows_ref, out_ref, gate_buf, up_buf, down_buf, wide_ref, total_ref, sems, edge_sems,
+    rows_ref, gate_far, up_far, down_far, gate_near, up_near, down_near, out_ref,
+    gate_buf, up_buf, down_buf, wide_ref, total_ref, sems,
 ):
     core = lax.axis_index("core")
     blocks, width, block = gate_buf.shape
@@ -353,7 +352,7 @@
     count = total_ref.shape[0]
 
     def copies(i):
-        near = i < blocks // 2
+        near = i >= blocks // 2
         gate, up, down = (gate_near, up_near, down_near) if near else (gate_far, up_far, down_far)
         at = pl.ds((i % (blocks // 2)) * block, block)
         return (
@@ -363,38 +362,21 @@
         )
 
     step = 256
-    edges = range(0, half, step)
-
-    def chunk(at):
-        return slice(None), pl.ds(at, step)
-
-    arriving = [
-        pltpu.make_async_copy(rows_hbm.at[chunk(at)], rows_ref.at[chunk(at)], edge_sems.at[0, i])
-        for i, at in enumerate(edges)
-    ]
-    leaving = [
-        pltpu.make_async_copy(out_ref.at[chunk(at)], out_hbm.at[chunk(at)], edge_sems.at[1, i])
-        for i, at in enumerate(edges)
-    ]
-    for copy in arriving:
+    started = [copies(i) for i in range(blocks)]
+    for copy in started[0]:
         copy.start()
-    started = [copies(i) for i in range(blocks)]
-    started[0][0].start()
-    started[0][1].start()
 
     to = lax.broadcasted_iota(jnp.int32, (count, 2 * count), 0)
     source = lax.broadcasted_iota(jnp.int32, (count, 2 * count), 1)
     picks = [
         (source == to // 4 * 8 + to % 4 + 4 * side).astype(F32).astype(BF16) for side in range(2)
     ]
-    for i, at in enumerate(edges):
-        arriving[i].wait()
-        for side in range(2):
+    for side in range(2):
+        for at in range(0, half, step):
             wide_ref[:, side * half + at : side * half + at + step] = dot(
                 picks[side], rows_ref[:, at : at + step]
             ).astype(BF16)
 
-    started[0][2].start()
     for copy in started[1]:
         copy.start()
 
@@ -420,14 +402,11 @@
     same = source == to // 8 * 4 + to % 4
     first = ((to % 8 < 4) & same).astype(F32).astype(BF16)
     second = ((to % 8 >= 4) & same).astype(F32).astype(BF16)
-    for i, at in enumerate(edges):
+    for at in range(0, half, step):
         out_ref[:, at : at + step] = (
             dot(first, total_ref[:, at : at + step].astype(BF16))
             + dot(second, total_ref[:, half + at : half + at + step].astype(BF16))
         ).astype(BF16)
-        leaving[i].start()
-    for copy in leaving:
-        copy.wait()
 
 
 def run_expert(rows, near, far):
@@ -437,20 +416,17 @@
     return pl.pallas_call(
         expert_kernel,
         out_shape=jax.ShapeDtypeStruct(rows.shape, BF16),
-        in_specs=[HBM] * 7,
-        out_specs=HBM,
+        in_specs=[VMEM] + [HBM] * 6,
+        out_specs=VMEM,
         scratch_shapes=[
-            pltpu.VMEM(rows.shape, BF16),
-            pltpu.VMEM(rows.shape, BF16),
             pltpu.VMEM((blocks, width, block), BF16),
             pltpu.VMEM((blocks, width, block), BF16),
             pltpu.VMEM((blocks, block, width), BF16),
             pltpu.VMEM((count, width), BF16),
             pltpu.VMEM((count, width), F32),
             pltpu.SemaphoreType.DMA((3, blocks)),
-            pltpu.SemaphoreType.DMA((2, rows.shape[1] // 256)),
         ],
-        compiler_params=pltpu.CompilerParams(vmem_limit_bytes=58 * MIB),
+        compiler_params=pltpu.CompilerParams(vmem_limit_bytes=29 * MIB),
         cost_estimate=pl.CostEstimate(
             flops=7_500_000_000, bytes_accessed=26_000_000, transcendentals=300_000
         ),
@@ -499,7 +475,7 @@
 
     latent = attend(block_table, lengths, queries, new_latent, latent_cache, kv_width)
     outbound = latent.reshape(planes, SIDE * seq_count, kv_width)
-    arrived = lax.all_to_all(outbound, ("z", "x"), split_axis=0, concat_axis=0, tiled=True)
+    arrived = lax.all_to_all(outbound, PLANE, split_axis=0, concat_axis=0, tiled=True)
     arrived = arrived.reshape(planes * SIDE * seq_count, kv_width)
     placement, mixing = route(routes, far_routes, chips)
     own_values = find_values(arrived, pieces)
@@ -511,8 +487,7 @@
     partial, gate_weight = lax.optimization_barrier((partial, gate_weight))
     far_gate = other_core(gate_weight)
     partial = partial.reshape(planes, 2 * seq_count, half)
-    collected = lax.all_to_all(partial, ("z", "x"), split_axis=0, concat_axis=0, tiled=True)
-    collected, far_gate = lax.optimization_barrier((collected, far_gate))
+    collected = lax.all_to_all(partial, PLANE, split_axis=0, concat_axis=0, tiled=True)
     mine = jnp.sum(collected.astype(F32), axis=0)
     theirs = other_core(mine)
     theirs = jnp.concatenate([theirs[seq_count:], theirs[:seq_count]], axis=0)

time: 144 us -> 138 us (0.958)
  Pallas kernels: 23.7 us -> 18.9 us
  blocking collectives: 82.6 us -> 81 us
    pallas_call x1, Pallas kernels: 12.8 us -> 9.97 us  [run_expert(): pl.pallas_call(expert_kernel, out_shape=jax.ShapeDtypeStruct(rows.shape,...]
  transfers between devices with their start and end apart: 12 -> 12, of which waited for: 5 -> 6; matrix products, arithmetic and copies ran while one was open for 1% -> 1% of each run, Pallas kernels for 5% -> 4%
where the time goes in v4:
time: 138 us
  blocking collectives  81 us (59%)
  starting transfers between devices  23.6 us (17%)
  Pallas kernels  18.9 us (14%)
  waiting for transfers between devices  10.9 us (8%)
    all_to_all x1, blocking collectives, shards(): lax.all_to_all(outgoing, CHIPS, split_axis=0, concat_axis=0, tiled=True)  29.6 us
    all_to_all x1, blocking collectives, shards(): lax.all_to_all(reply.reshape(chips, 8, half), CHIPS, split_axis=0, concat...  29.3 us
    all_to_all x1, blocking collectives, shards(): lax.all_to_all(partial, PLANE, split_axis=0, concat_axis=0, tiled=True)  22 us
    pallas_call x1, Pallas kernels, run_expert(): pl.pallas_call(expert_kernel, out_shape=jax.ShapeDtypeStruct(rows.shape,...  9.97 us
    ppermute x7, starting transfers between devices, other_core(): return lax.ppermute(array, 'core', SWAP)  9.11 us
    ppermute x4, waiting for transfers between devices, along_y(): lax.ppermute(array, 'y', [(i, (i + step) % SIDE) for i in range(SIDE)])  7.88 us
    all_to_all x1, starting transfers between devices, shards(): lax.all_to_all(outbound, PLANE, split_axis=0, concat_axis=0, tiled=True)  7.74 us
    ppermute x4, starting transfers between devices, along_y(): lax.ppermute(array, 'y', [(i, (i + step) % SIDE) for i in range(SIDE)])  6.76 us
  transfers between devices with their start and end apart: 12, of which 6 were waited for; matrix products, arithmetic and copies ran while one was open for 1% of the time, Pallas kernels for 4%

profile of v4, /device:TPU:1, one launch (start us, length us, event | category | flops | bytes accessed | tf_op | source)
XLA Modules:
  0.0 138.0 jit_solution(15535810913367805271)
XLA Ops:
  0.6 1.9 %prepare.1 = (bf16[128,2304]{1,0:T(8,128)(2,1)}, f32[8,128]{1,0:T(8,128)}) custom-call(bf16[128,3584]{1,0:T(8,128)(2,1)} %out_proj.1, bf16[1,512,128]{2,1,0:T(8,128)(2,1)} %value_up.1, s32[8,8]{1,0:T(8,128)} %ids_hbm.1, f32[8,8]{1,0:T(8,128)} %affinity_hbm.1), custom_call_target="tpu_custom_call" | custom-call | bytes 1200000 | tf_op jit(solution)/shard_map/prepare/pallas_call | solution.py:194
  2.6 3.6 %collective-permute-start.2 = (bf16[128,2304]{1,0:T(8,128)(2,1)}, bf16[128,2304]{1,0:T(8,128)(2,1)S(1)}, u32[]{:S(2)}, u32[]{:S(2)}) collective-permute-start(bf16[128,2304]{1,0:T(8,128)(2,1)} %get-tuple-element.22.refs_0_), channel_id=1, source_target_pairs={{0,3},{1,0},{2,1},{3,2},{4,7},{5,4},{6,5},{7,6},{8,11},{9,8},{10,9... | collective-permute-start | bytes 1769480 | tf_op jit(solution)/shard_map/ppermute | solution.py:438
  6.2 0.0 collective-permute-start
  6.2 4.9 %attend.1 = bf16[512,512]{1,0:T(8,128)(2,1)} custom-call(s32[1,16]{1,0:T(1,128)} %table_hbm.1, s32[1,8]{1,0:T(1,128)} %length_hbm.1, bf16[8,36864]{1,0:T(8,128)(2,1)} %query_hbm.1, bf16[8,576]{1,0:T(8,128)(2,1)} %fresh_hbm.1, bf16[16,36864]{1,0:T(8,128)(2,1)} %cache_hbm.1), custom_call_target="tpu_custom_call" | custom-call | flops 1400000000 | bytes 2400000 | tf_op jit(solution)/shard_map/attend/pallas_call | solution.py:145
  11.1 0.0 copy-start
  11.1 7.7 %all-to-all-start = ((bf16[16,32,512]{2,1,0:T(8,128)(2,1)}), bf16[16,32,512]{2,1,0:T(8,128)(2,1)S(1)}, u32[]{:S(2)}, u32[]{:S(2)}) async-start(bf16[16,32,512]{2,1,0:T(8,128)(2,1)} %bitcast.22), calls=%async_computation | async-start | bytes 1048576 | tf_op jit(solution)/shard_map/all_to_all | solution.py:478
  18.8 0.0 collective-permute-done.2.refs_4_
  18.9 0.0 copy-start.1
  18.9 3.0 %collective-permute-start.3 = (bf16[64,2304]{1,0:T(8,128)(2,1)S(1)}, bf16[64,2304]{1,0:T(8,128)(2,1)S(1)}, u32[]{:S(2)}, u32[]{:S(2)}) collective-permute-start(bf16[64,2304]{1,0:T(8,128)(2,1)S(1)} %slice.47), channel_id=1, source_target_pairs={{0,3},{1,0},{2,1},{3,2},{4,7},{5,4},{6,5},{7,6},{8,11},{9,8},{10,9... | collective-permute-start | bytes 884744 | tf_op jit(solution)/shard_map/ppermute | solution.py:438
  21.9 0.0 collective-permute-done.refs_1_
  22.0 0.1 collective-permute-start.1
  22.0 4.6 %collective-permute-done.3.refs_3_ = bf16[64,2304]{1,0:T(8,128)(2,1)S(1)} collective-permute-done((bf16[64,2304]{1,0:T(8,128)(2,1)S(1)}, bf16[64,2304]{1,0:T(8,128)(2,1)S(1)}, u32[]{:S(2)}, u32[]{:S(2)}) %collective-permute-start.3) | collective-permute-done | bytes 294944 | tf_op jit(solution)/shard_map/ppermute | solution.py:438
  26.7 3.2 %collective-permute-done.1.refs_2_ = bf16[64,2304]{1,0:T(8,128)(2,1)S(1)} collective-permute-done((bf16[64,2304]{1,0:T(8,128)(2,1)S(1)}, bf16[64,2304]{1,0:T(8,128)(2,1)S(1)}, u32[]{:S(2)}, u32[]{:S(2)}) %collective-permute-start.1) | collective-permute-done | bytes 294944 | tf_op jit(solution)/shard_map/ppermute | solution.py:438
  29.9 0.0 all-to-all-done
  29.9 0.0 copy-done
  29.9 0.9 find_values.1.own_values
  30.8 2.8 %collective-permute-start.4 = (bf16[128,512]{1,0:T(8,128)(2,1)S(1)}, bf16[128,512]{1,0:T(8,128)(2,1)S(1)}, u32[]{:S(2)}, u32[]{:S(2)}) collective-permute-start(bf16[128,512]{1,0:T(8,128)(2,1)S(1)} %find_values.1.own_values), channel_id=1, source_target_pairs={{0,64},{64,0},{1,65},{65,1},{2,66},{66,2},{3,67},{67,3},{4,68},{68... | collective-permute-start | bytes 393224 | tf_op jit(solution)/shard_map/ppermute | solution.py:442
  33.6 0.0 copy-done.1
  33.6 0.1 collective-permute-start.5
  33.7 1.1 collective-permute-done.5.far_ref
  34.8 0.4 route.1
  35.2 0.0 collective-permute-done.4.far_values
  35.2 0.9 project.1
  36.1 0.0 copy-start.2
  36.1 22.0 %all_to_all.20 = bf16[16,16,1792]{2,1,0:T(8,128)(2,1)S(1)} all-to-all(bf16[16,16,1792]{2,1,0:T(8,128)(2,1)S(1)} %bitcast.19), channel_id=1, replica_groups=mesh['core'=2,'z'=4,'x'=4,'y'=4] {'x','z'}, dimensions={0} | all-to-all | bytes 1835008 | tf_op jit(solution)/shard_map/all_to_all | solution.py:490
  58.1 0.1 convert_reduce_fusion
  58.3 1.8 %collective-permute-start.6 = (f32[16,1792]{1,0:T(8,128)S(1)}, f32[16,1792]{1,0:T(8,128)S(1)}, u32[]{:S(2)}, u32[]{:S(2)}) collective-permute-start(f32[16,1792]{1,0:T(8,128)S(1)} %convert_reduce_fusion), channel_id=1, source_target_pairs={{0,64},{64,0},{1,65},{65,1},{2,66},{66,2},{3,67},{67,3},{4,68},{68... | collective-permute-start | bytes 344072 | tf_op jit(solution)/shard_map/ppermute | solution.py:442
  60.1 0.1 collective-permute-start.7
  60.2 0.9 collective-permute-done.6
  61.1 0.4 collective-permute-start.8
  61.6 0.2 collective-permute-start.9
  61.7 0.1 multiply_reduce_fusion
  61.9 0.0 copy-done.2
  61.9 0.1 multiply_convert_fusion
  62.0 0.7 fusion
  62.6 29.6 %all_to_all.21 = bf16[64,8,1792]{2,1,0:T(8,128)(2,1)S(1)} all-to-all(bf16[64,8,1792]{2,1,0:T(8,128)(2,1)S(1)} %fusion), channel_id=1, replica_groups=mesh['core'=2,'z'=4,'x'=4,'y'=4] {'z','x','y'}, dimensions={0} | all-to-all | bytes 3670016 | tf_op jit(solution)/shard_map/all_to_all | solution.py:512
  92.2 0.0 collective-permute-done.7.gate_far
  92.2 0.0 collective-permute-done.8.up_far
  92.2 0.7 collective-permute-done.9.down_far
  93.0 10.0 %expert.1 = bf16[512,1792]{1,0:T(8,128)(2,1)S(1)} custom-call(bf16[512,1792]{1,0:T(8,128)(2,1)S(1)} %bitcast.17, bf16[2,3584,512]{2,1,0:T(8,128)(2,1)S(1)} %collective-permute-done.7.gate_far, bf16[2,3584,512]{2,1,0:T(8,128)(2,1)S(1)} %collective-permute-done.8.up_far, bf16[2,512,3584]{2,1,0:T(8,128)(2,1)S(1)} %collective-permute-done.9.down_far, ...), custom_call_target="tpu_custom_call" | custom-call | flops 7500000256 | bytes 26000000 | tf_op jit(solution)/shard_map/expert/pallas_call | solution.py:416
  102.9 29.3 %all_to_all.22 = bf16[64,8,1792]{2,1,0:T(8,128)(2,1)S(1)} all-to-all(bf16[64,8,1792]{2,1,0:T(8,128)(2,1)S(1)} %bitcast.18), channel_id=1, replica_groups=mesh['core'=2,'z'=4,'x'=4,'y'=4] {'z','x','y'}, dimensions={0} | all-to-all | bytes 3670016 | tf_op jit(solution)/shard_map/all_to_all | solution.py:514
  132.3 0.4 fusion.1
  132.8 3.7 %collective-permute-start.10 = (f32[8,3584]{1,0:T(8,128)S(1)}, f32[8,3584]{1,0:T(8,128)S(1)}, u32[]{:S(2)}, u32[]{:S(2)}) collective-permute-start(f32[8,3584]{1,0:T(8,128)S(1)} %bitcast.24), channel_id=1, source_target_pairs={{0,64},{64,0},{1,65},{65,1},{2,66},{66,2},{3,67},{67,3},{4,68},{68... | collective-permute-start | bytes 344072 | tf_op jit(solution)/shard_map/ppermute | solution.py:442
  136.4 0.6 slice.50
  137.1 0.3 collective-permute-done.10
  137.4 0.6 add_convert_fusion
  (8 shorter events, 0.1 us)
Async XLA Ops:
  2.6 16.3 %collective-permute-start.2 = (bf16[128,2304]{1,0:T(8,128)(2,1)}, bf16[128,2304]{1,0:T(8,128)(2,1)S(1)}, u32[]{:S(2)}, u32[]{:S(2)}) collective-permute-start(bf16[128,2304]{1,0:T(8,128)(2,1)} %get-tuple-element.22.refs_0_), channel_id=1, source_target_pairs={{0,3},{1,0},{2,1},{3,2},{4,7},{5,4},{6,5},{7,6},{8,11},{9,8},{10,9... | collective-permute-start | bytes 1769480 | tf_op jit(solution)/shard_map/ppermute | solution.py:438
  6.2 15.7 %collective-permute-start = (bf16[128,2304]{1,0:T(8,128)(2,1)}, bf16[128,2304]{1,0:T(8,128)(2,1)S(1)}, u32[]{:S(2)}, u32[]{:S(2)}) collective-permute-start(bf16[128,2304]{1,0:T(8,128)(2,1)} %get-tuple-element.22.refs_0_), channel_id=1, source_target_pairs={{0,1},{1,2},{2,3},{3,0},{4,5},{5,6},{6,7},{7,4},{8,9},{9,10},{10,1... | collective-permute-start | bytes 1769480 | tf_op jit(solution)/shard_map/ppermute | solution.py:438
  11.1 18.8 %copy-start = (bf16[128,2304]{1,0:T(8,128)(2,1)S(1)}, bf16[128,2304]{1,0:T(8,128)(2,1)}, u32[]{:S(2)}) copy-start(bf16[128,2304]{1,0:T(8,128)(2,1)} %get-tuple-element.22.refs_0_) | copy-start | bytes 1769476
  11.1 18.8 %all-to-all-start = ((bf16[16,32,512]{2,1,0:T(8,128)(2,1)}), bf16[16,32,512]{2,1,0:T(8,128)(2,1)S(1)}, u32[]{:S(2)}, u32[]{:S(2)}) async-start(bf16[16,32,512]{2,1,0:T(8,128)(2,1)} %bitcast.22), calls=%async_computation | async-start | bytes 1048576 | tf_op jit(solution)/shard_map/all_to_all | solution.py:478
  18.9 14.8 %copy-start.1 = (f32[8,128]{1,0:T(8,128)S(1)}, f32[8,128]{1,0:T(8,128)}, u32[]{:S(2)}) copy-start(f32[8,128]{1,0:T(8,128)} %get-tuple-element.27.own_ref) | copy-start | bytes 12292
  18.9 7.8 %collective-permute-start.3 = (bf16[64,2304]{1,0:T(8,128)(2,1)S(1)}, bf16[64,2304]{1,0:T(8,128)(2,1)S(1)}, u32[]{:S(2)}, u32[]{:S(2)}) collective-permute-start(bf16[64,2304]{1,0:T(8,128)(2,1)S(1)} %slice.47), channel_id=1, source_target_pairs={{0,3},{1,0},{2,1},{3,2},{4,7},{5,4},{6,5},{7,6},{8,11},{9,8},{10,9... | collective-permute-start | bytes 884744 | tf_op jit(solution)/shard_map/ppermute | solution.py:438
  22.0 8.0 %collective-permute-start.1 = (bf16[64,2304]{1,0:T(8,128)(2,1)S(1)}, bf16[64,2304]{1,0:T(8,128)(2,1)S(1)}, u32[]{:S(2)}, u32[]{:S(2)}) collective-permute-start(bf16[64,2304]{1,0:T(8,128)(2,1)S(1)} %slice.46), channel_id=1, source_target_pairs={{0,1},{1,2},{2,3},{3,0},{4,5},{5,6},{6,7},{7,4},{8,9},{9,10},{10,1... | collective-permute-start | bytes 884744 | tf_op jit(solution)/shard_map/ppermute | solution.py:438
  30.8 4.4 %collective-permute-start.4 = (bf16[128,512]{1,0:T(8,128)(2,1)S(1)}, bf16[128,512]{1,0:T(8,128)(2,1)S(1)}, u32[]{:S(2)}, u32[]{:S(2)}) collective-permute-start(bf16[128,512]{1,0:T(8,128)(2,1)S(1)} %find_values.1.own_values), channel_id=1, source_target_pairs={{0,64},{64,0},{1,65},{65,1},{2,66},{66,2},{3,67},{67,3},{4,68},{68... | collective-permute-start | bytes 393224 | tf_op jit(solution)/shard_map/ppermute | solution.py:442
  33.6 1.2 collective-permute-start.5
  36.1 25.8 %copy-start.2 = (f32[3584]{0:T(1024)S(1)}, f32[3584]{0:T(1024)}, u32[]{:S(2)}) copy-start(f32[3584]{0:T(1024)} %param.20) | copy-start | bytes 43012
  58.3 2.8 %collective-permute-start.6 = (f32[16,1792]{1,0:T(8,128)S(1)}, f32[16,1792]{1,0:T(8,128)S(1)}, u32[]{:S(2)}, u32[]{:S(2)}) collective-permute-start(f32[16,1792]{1,0:T(8,128)S(1)} %convert_reduce_fusion), channel_id=1, source_target_pairs={{0,64},{64,0},{1,65},{65,1},{2,66},{66,2},{3,67},{67,3},{4,68},{68... | collective-permute-start | bytes 344072 | tf_op jit(solution)/shard_map/ppermute | solution.py:442
  60.1 32.1 %collective-permute-start.7 = (bf16[2,3584,512]{2,1,0:T(8,128)(2,1)}, bf16[2,3584,512]{2,1,0:T(8,128)(2,1)S(1)}, u32[]{:S(2)}, u32[]{:S(2)}) collective-permute-start(bf16[2,3584,512]{2,1,0:T(8,128)(2,1)} %gate_near), channel_id=1, source_target_pairs={{0,64},{64,0},{1,65},{65,1},{2,66},{66,2},{3,67},{67,3},{4,68},{68... | collective-permute-start | bytes 22020104 | tf_op jit(solution)/shard_map/ppermute | solution.py:442
  61.1 31.1 %collective-permute-start.8 = (bf16[2,3584,512]{2,1,0:T(8,128)(2,1)}, bf16[2,3584,512]{2,1,0:T(8,128)(2,1)S(1)}, u32[]{:S(2)}, u32[]{:S(2)}) collective-permute-start(bf16[2,3584,512]{2,1,0:T(8,128)(2,1)} %up_near), channel_id=1, source_target_pairs={{0,64},{64,0},{1,65},{65,1},{2,66},{66,2},{3,67},{67,3},{4,68},{68... | collective-permute-start | bytes 22020104 | tf_op jit(solution)/shard_map/ppermute | solution.py:442
  61.6 31.4 %collective-permute-start.9 = (bf16[2,512,3584]{2,1,0:T(8,128)(2,1)}, bf16[2,512,3584]{2,1,0:T(8,128)(2,1)S(1)}, u32[]{:S(2)}, u32[]{:S(2)}) collective-permute-start(bf16[2,512,3584]{2,1,0:T(8,128)(2,1)} %down_near), channel_id=1, source_target_pairs={{0,64},{64,0},{1,65},{65,1},{2,66},{66,2},{3,67},{67,3},{4,68},{68... | collective-permute-start | bytes 22020104 | tf_op jit(solution)/shard_map/ppermute | solution.py:442
  132.8 4.6 %collective-permute-start.10 = (f32[8,3584]{1,0:T(8,128)S(1)}, f32[8,3584]{1,0:T(8,128)S(1)}, u32[]{:S(2)}, u32[]{:S(2)}) collective-permute-start(f32[8,3584]{1,0:T(8,128)S(1)} %bitcast.24), channel_id=1, source_target_pairs={{0,64},{64,0},{1,65},{65,1},{2,66},{66,2},{3,67},{67,3},{4,68},{68... | collective-permute-start | bytes 344072 | tf_op jit(solution)/shard_map/ppermute | solution.py:442

commit v5 on v4

--- a/solution.py
+++ b/solution.py
@@ -11,6 +11,7 @@
 SIDE = 4
 CHIPS = ("z", "x", "y")
 PLANE = ("x", "z")
+ALL = ("core",) + CHIPS
 SWAP = [(0, 1), (1, 0)]
 F32 = jnp.float32
 BF16 = jnp.bfloat16
@@ -210,12 +211,11 @@
     )(out_proj, value_up, expert_ids, affinity)
 
 
-def route_kernel(own_ref, far_ref, place_ref, mix_ref):
-    core = lax.axis_index("core")
-    seq_count = own_ref.shape[0]
-    tokens, top_count = 2 * seq_count, 8
+def route_kernel(own_ref, place_ref, mix_ref):
+    own, top_count = own_ref.shape[0], 8
+    tokens = 2 * own
     columns = place_ref.shape[1]
-    routes = jnp.concatenate([own_ref[...], far_ref[...]], axis=0)
+    routes = jnp.concatenate([own_ref[...], own_ref[...]], axis=0)
     affinity = routes[:, top_count : 2 * top_count]
     share = affinity / jnp.sum(affinity, axis=1, keepdims=True) * ROUTED_SCALE
     experts = routes.shape[1]
@@ -228,45 +228,45 @@
         shares = jnp.where(hit, share[:, k : k + 1], shares)
     row = lax.broadcasted_iota(jnp.int32, (tokens, tokens), 0)
     column = lax.broadcasted_iota(jnp.int32, (tokens, tokens), 1)
-    earlier = ((column < row) & (column // seq_count == row // seq_count)).astype(F32)
+    earlier = ((column < row) & (column // own == row // own)).astype(F32)
     rank = dot(earlier.astype(BF16), chosen.astype(BF16))
-    token = lax.broadcasted_iota(jnp.int32, (tokens, experts), 0)
-    slot = (rank + jnp.where(token < seq_count, 1.0, 3.0)) * chosen
+    slot = (rank + 1.0) * chosen
     named = lax.broadcasted_iota(jnp.int32, (experts, columns), 0)
     at = lax.broadcasted_iota(jnp.int32, (experts, columns), 1)
-    spread = (named == at // 8 * 2 + core).astype(F32).astype(BF16)
+    each = columns // 2
+    spread = (named == at % each // 8 * 2 + at // each).astype(F32).astype(BF16)
     high = shares.astype(BF16)
     low = (shares - high.astype(F32)).astype(BF16)
     at = lax.broadcasted_iota(jnp.int32, (tokens, columns), 1)
-    filled = dot(slot.astype(BF16), spread) == (at % 4 + 1).astype(F32)
+    filled = dot(slot.astype(BF16), spread) == (at % 2 + 1).astype(F32)
     high = jnp.where(filled, dot(high, spread), 0.0)
     low = jnp.where(filled, dot(low, spread), 0.0)
     placed = filled.astype(F32)
-    first = at % 8 < 4
-
-    def by_half(table):
-        return [jnp.where(first, table, 0.0), jnp.where(first, 0.0, table)]
-
-    place_ref[...] = jnp.concatenate(by_half(placed), axis=0).astype(BF16)
-    mix_ref[...] = jnp.concatenate(by_half(high) + by_half(low), axis=0).astype(BF16)
-
-
-def route(own, far, chips):
-    tokens = 2 * own.shape[0]
+    quarter = at % 8 // 2
+
+    def by_quarter(table):
+        return [jnp.where(quarter == q, table, 0.0)[:own] for q in range(4)]
+
+    place_ref[...] = jnp.concatenate(by_quarter(placed), axis=0).astype(BF16)
+    mix_ref[...] = jnp.concatenate(by_quarter(high) + by_quarter(low), axis=0).astype(BF16)
+
+
+def route(own, devices):
+    rows = 4 * own.shape[0]
     return pl.pallas_call(
         route_kernel,
         out_shape=(
-            jax.ShapeDtypeStruct((2 * tokens, chips * 8), BF16),
-            jax.ShapeDtypeStruct((4 * tokens, chips * 8), BF16),
-        ),
-        in_specs=[VMEM] * 2,
+            jax.ShapeDtypeStruct((rows, devices * 8), BF16),
+            jax.ShapeDtypeStruct((2 * rows, devices * 8), BF16),
+        ),
+        in_specs=[VMEM],
         out_specs=(VMEM, VMEM),
         compiler_params=pltpu.CompilerParams(vmem_limit_bytes=8 * MIB),
         cost_estimate=pl.CostEstimate(
-            flops=20_000_000, bytes_accessed=120_000, transcendentals=0
+            flops=20_000_000, bytes_accessed=220_000, transcendentals=0
         ),
         name="route",
-    )(own, far)
+    )(own)
 
 
 def value_kernel(arrived_ref, *refs):
@@ -311,16 +311,13 @@
     )(arrived, *pieces)
 
 
-def project_kernel(own_values, far_values, *refs):
-    own, one, top, bottom, three, out_ref = refs
-    rows = own_values.shape[0]
-    half = out_ref.shape[1]
-    to = lax.broadcasted_iota(jnp.int32, (2 * rows, rows), 0)
-    source = lax.broadcasted_iota(jnp.int32, (2 * rows, rows), 1)
-    same = source == to // 16 * 8 + to % 8
-    near = (same & (to % 16 < 8)).astype(F32).astype(BF16)
-    far = (same & (to % 16 >= 8)).astype(F32).astype(BF16)
-    values = (dot(near, own_values[...]) + dot(far, far_values[...])).astype(BF16)
+def project_kernel(own_values, far_values, own, one, top, bottom, three, out_ref):
+    core = lax.axis_index("core")
+    rows, half = own_values.shape[0], out_ref.shape[1]
+    mine, theirs = own_values[...].astype(F32), far_values[...].astype(F32)
+    values = jnp.concatenate(
+        [jnp.where(core == 0, mine, theirs), jnp.where(core == 0, theirs, mine)], axis=0
+    ).astype(BF16)
     step = 256
     for at in range(0, half, step):
         columns = slice(at, at + step)
@@ -348,7 +345,7 @@
 ):
     core = lax.axis_index("core")
     blocks, width, block = gate_buf.shape
-    half = width // 2
+    quarter = width // 4
     count = total_ref.shape[0]
 
     def copies(i):
@@ -366,16 +363,16 @@
     for copy in started[0]:
         copy.start()
 
-    to = lax.broadcasted_iota(jnp.int32, (count, 2 * count), 0)
-    source = lax.broadcasted_iota(jnp.int32, (count, 2 * count), 1)
-    picks = [
-        (source == to // 4 * 8 + to % 4 + 4 * side).astype(F32).astype(BF16) for side in range(2)
-    ]
-    for side in range(2):
-        for at in range(0, half, step):
-            wide_ref[:, side * half + at : side * half + at + step] = dot(
-                picks[side], rows_ref[:, at : at + step]
-            ).astype(BF16)
+    sent = lax.broadcasted_iota(jnp.int32, (256, 256), 1)
+    whole = lax.broadcasted_iota(jnp.int32, (256, 256), 0)
+    gather = sent == whole % 64 // 2 * 8 + whole // 64 * 2 + whole % 2
+    gather = gather.astype(F32).astype(BF16)
+    for g in range(count // 64):
+        held = dot(gather, rows_ref[g * 256 : (g + 1) * 256, :]).astype(BF16)
+        for q in range(4):
+            wide_ref[g * 64 : (g + 1) * 64, q * quarter : (q + 1) * quarter] = held[
+                q * 64 : (q + 1) * 64
+            ]
 
     for copy in started[1]:
         copy.start()
@@ -397,21 +394,23 @@
             else:
                 total_ref[:, at : at + 2 * step] += part
 
-    to = lax.broadcasted_iota(jnp.int32, (2 * count, count), 0)
-    source = lax.broadcasted_iota(jnp.int32, (2 * count, count), 1)
-    same = source == to // 8 * 4 + to % 4
-    first = ((to % 8 < 4) & same).astype(F32).astype(BF16)
-    second = ((to % 8 >= 4) & same).astype(F32).astype(BF16)
-    for at in range(0, half, step):
-        out_ref[:, at : at + step] = (
-            dot(first, total_ref[:, at : at + step].astype(BF16))
-            + dot(second, total_ref[:, half + at : half + at + step].astype(BF16))
+    sent = lax.broadcasted_iota(jnp.int32, (256, 256), 0)
+    whole = lax.broadcasted_iota(jnp.int32, (256, 256), 1)
+    scatter = sent == whole % 64 // 2 * 8 + whole // 64 * 2 + whole % 2
+    scatter = scatter.astype(F32).astype(BF16)
+    for g in range(count // 64):
+        held = [
+            total_ref[g * 64 : (g + 1) * 64, q * quarter : (q + 1) * quarter].astype(BF16)
+            for q in range(4)
+        ]
+        out_ref[g * 256 : (g + 1) * 256, :] = dot(
+            scatter, jnp.concatenate(held, axis=0)
         ).astype(BF16)
 
 
 def run_expert(rows, near, far):
     _, hidden, width = near[2].shape
-    count, block = rows.shape[0] // 2, 256
+    count, block = rows.shape[0] // 4, 256
     blocks = 2 * hidden // block
     return pl.pallas_call(
         expert_kernel,
@@ -463,7 +462,8 @@
     half = model_width // 2
     core = lax.axis_index("core")
     planes = SIDE * SIDE
-    chips = SIDE**3
+    devices = 2 * SIDE**3
+    quarter = model_width // 4
 
     piece, routes = prepare(out_proj, value_up, expert_ids, affinity)
     one, three = along_y(piece, 1), along_y(piece, -1)
@@ -471,13 +471,12 @@
     two_top, two_bottom = along_y(one[:middle], 1), along_y(three[middle:], -1)
     pieces = (piece, one, two_top, two_bottom, three)
     routes, pieces = lax.optimization_barrier((routes, pieces))
-    far_routes = other_core(routes)
 
     latent = attend(block_table, lengths, queries, new_latent, latent_cache, kv_width)
     outbound = latent.reshape(planes, SIDE * seq_count, kv_width)
     arrived = lax.all_to_all(outbound, PLANE, split_axis=0, concat_axis=0, tiled=True)
     arrived = arrived.reshape(planes * SIDE * seq_count, kv_width)
-    placement, mixing = route(routes, far_routes, chips)
+    placement, mixing = route(routes, devices)
     own_values = find_values(arrived, pieces)
     far_values, placement, mixing = lax.optimization_barrier(
         (other_core(own_values), placement, mixing)
@@ -486,39 +485,33 @@
 
     partial, gate_weight = lax.optimization_barrier((partial, gate_weight))
     far_gate = other_core(gate_weight)
-    partial = partial.reshape(planes, 2 * seq_count, half)
-    collected = lax.all_to_all(partial, PLANE, split_axis=0, concat_axis=0, tiled=True)
-    mine = jnp.sum(collected.astype(F32), axis=0)
-    theirs = other_core(mine)
-    theirs = jnp.concatenate([theirs[seq_count:], theirs[:seq_count]], axis=0)
-    attn_out = jnp.where(
-        core == 0,
-        jnp.concatenate([mine, theirs], axis=1),
-        jnp.concatenate([theirs, mine], axis=1),
-    )
+    partial = partial.reshape(2 * planes, seq_count, half)
+    collected = lax.all_to_all(partial, ("core",) + PLANE, split_axis=0, concat_axis=0, tiled=True)
+    halves = jnp.sum(collected.astype(F32).reshape(2, planes, seq_count, half), axis=1)
+    attn_out = jnp.concatenate([halves[0], halves[1]], axis=1)
     attn_out, up_weight, down_weight = lax.optimization_barrier(
         (attn_out, up_weight, down_weight)
     )
     weights = (gate_weight, up_weight, down_weight)
     far_weights = (far_gate, other_core(up_weight), other_core(down_weight))
     mean_square = jnp.mean(attn_out * attn_out, axis=1, keepdims=True)
-    both = (attn_out * lax.rsqrt(mean_square + EPSILON) * norm_gain).astype(BF16)
-    normed = both[:seq_count]
-    both = jnp.concatenate([both[:, :half], both[:, half:]], axis=0)
+    normed = (attn_out * lax.rsqrt(mean_square + EPSILON) * norm_gain).astype(BF16)
+    parts = jnp.concatenate(
+        [normed[:, at : at + quarter] for at in range(0, model_width, quarter)], axis=0
+    )
     outgoing = lax.dot_general(
-        placement, both, (((0,), (0,)), ((), ())), preferred_element_type=F32
-    )
-    outgoing = outgoing.astype(BF16).reshape(chips, 8, half)
-    received = lax.all_to_all(outgoing, CHIPS, split_axis=0, concat_axis=0, tiled=True)
-    reply = run_expert(received.reshape(chips * 8, half), weights, far_weights)
+        placement, parts, (((0,), (0,)), ((), ())), preferred_element_type=F32
+    )
+    outgoing = outgoing.astype(BF16).reshape(devices, 8, quarter)
+    received = lax.all_to_all(outgoing, ALL, split_axis=0, concat_axis=0, tiled=True)
+    reply = run_expert(received.reshape(devices * 8, quarter), weights, far_weights)
     returned = lax.all_to_all(
-        reply.reshape(chips, 8, half), CHIPS, split_axis=0, concat_axis=0, tiled=True
-    )
-    mixed = dot(mixing, returned.reshape(chips * 8, half))
+        reply.reshape(devices, 8, quarter), ALL, split_axis=0, concat_axis=0, tiled=True
+    )
+    mixed = dot(mixing, returned.reshape(devices * 8, quarter))
     mixed = mixed[: 4 * seq_count] + mixed[4 * seq_count :]
-    mixed = mixed.reshape(2, 2, seq_count, half)
-    mixed = jnp.transpose(mixed, (1, 2, 0, 3)).reshape(2, seq_count, model_width)
-    expert_out = (mixed[0] + other_core(mixed[1])).astype(BF16)
+    mixed = jnp.transpose(mixed.reshape(4, seq_count, quarter), (1, 0, 2))
+    expert_out = mixed.reshape(seq_count, model_width).astype(BF16)
     return (normed, expert_out)
 
 

time: 138 us -> 134 us (0.971)
  blocking collectives: 81 us -> 60.8 us
  waiting for transfers between devices: 10.9 us -> 23.3 us
  starting transfers between devices: 23.6 us -> 27.4 us
    all_to_all x3 -> x2, blocking collectives: 81 us -> 60.8 us  [the longest x1 31.9 us: shards(): lax.all_to_all(reply.reshape(devices, 8, quarter), ALL, split_axis=0, con...]
    all_to_all x0 -> x1, waiting for transfers between devices: none -> 14.8 us  [shards(): lax.all_to_all(partial, ('core',) + PLANE, split_axis=0, concat_axis=0, t...]
    all_to_all x0 -> x1, starting transfers between devices: none -> 8.43 us  [shards(): lax.all_to_all(partial, ('core',) + PLANE, split_axis=0, concat_axis=0, t...]
    ppermute x7 -> x4, starting transfers between devices: 9.11 us -> 4.44 us  [other_core(): return lax.ppermute(array, 'core', SWAP)]
    ppermute x7 -> x4, waiting for transfers between devices: 3.03 us -> 0.58 us  [other_core(): return lax.ppermute(array, 'core', SWAP)]
  transfers between devices with their start and end apart: 12 -> 10, of which waited for: 6 -> 4; matrix products, arithmetic and copies ran while one was open for 1% -> 1% of each run, Pallas kernels for 4% -> 4%
where the time goes in v5:
time: 134 us; the launch traced here: 133 us
  blocking collectives  60.8 us (45%)
  starting transfers between devices  27.4 us (20%)
  waiting for transfers between devices  23.3 us (17%)
  Pallas kernels  18.9 us (14%)
    all_to_all x1, blocking collectives, shards(): lax.all_to_all(reply.reshape(devices, 8, quarter), ALL, split_axis=0, con...  31.9 us
    all_to_all x1, blocking collectives, shards(): lax.all_to_all(outgoing, ALL, split_axis=0, concat_axis=0, tiled=True)  28.8 us
    all_to_all x1, waiting for transfers between devices, shards(): lax.all_to_all(partial, ('core',) + PLANE, split_axis=0, concat_axis=0, t...  14.8 us
    pallas_call x1, Pallas kernels, run_expert(): pl.pallas_call(expert_kernel, out_shape=jax.ShapeDtypeStruct(rows.shape,...  9.21 us
    all_to_all x1, starting transfers between devices, shards(): lax.all_to_all(partial, ('core',) + PLANE, split_axis=0, concat_axis=0, t...  8.43 us
    ppermute x4, waiting for transfers between devices, along_y(): lax.ppermute(array, 'y', [(i, (i + step) % SIDE) for i in range(SIDE)])  7.88 us
    all_to_all x1, starting transfers between devices, shards(): lax.all_to_all(outbound, PLANE, split_axis=0, concat_axis=0, tiled=True)  7.75 us
    ppermute x4, starting transfers between devices, along_y(): lax.ppermute(array, 'y', [(i, (i + step) % SIDE) for i in range(SIDE)])  6.74 us
  transfers between devices with their start and end apart: 10, of which 4 were waited for; matrix products, arithmetic and copies ran while one was open for 1% of the time, Pallas kernels for 4%

profile of v5, /device:TPU:1, one launch (start us, length us, event | category | flops | bytes accessed | tf_op | source)
XLA Modules:
  0.0 133.3 jit_solution(5447145556189899713)
XLA Ops:
  0.6 1.9 %prepare.1 = (bf16[128,2304]{1,0:T(8,128)(2,1)}, f32[8,128]{1,0:T(8,128)}) custom-call(bf16[128,3584]{1,0:T(8,128)(2,1)} %out_proj.1, bf16[1,512,128]{2,1,0:T(8,128)(2,1)} %value_up.1, s32[8,8]{1,0:T(8,128)} %ids_hbm.1, f32[8,8]{1,0:T(8,128)} %affinity_hbm.1), custom_call_target="tpu_custom_call" | custom-call | bytes 1200000 | tf_op jit(solution)/shard_map/prepare/pallas_call | solution.py:195
  2.6 3.6 %collective-permute-start.2 = (bf16[128,2304]{1,0:T(8,128)(2,1)}, bf16[128,2304]{1,0:T(8,128)(2,1)S(1)}, u32[]{:S(2)}, u32[]{:S(2)}) collective-permute-start(bf16[128,2304]{1,0:T(8,128)(2,1)} %get-tuple-element.22.refs_0_.own), channel_id=1, source_target_pairs={{0,3},{1,0},{2,1},{3,2},{4,7},{5,4},{6,5},{7,6},{8,11},{9,8},{10,9... | collective-permute-start | bytes 1769480 | tf_op jit(solution)/shard_map/ppermute | solution.py:437
  6.2 0.0 collective-permute-start
  6.2 4.9 %attend.1 = bf16[512,512]{1,0:T(8,128)(2,1)} custom-call(s32[1,16]{1,0:T(1,128)} %table_hbm.1, s32[1,8]{1,0:T(1,128)} %length_hbm.1, bf16[8,36864]{1,0:T(8,128)(2,1)} %query_hbm.1, bf16[8,576]{1,0:T(8,128)(2,1)} %fresh_hbm.1, bf16[16,36864]{1,0:T(8,128)(2,1)} %cache_hbm.1), custom_call_target="tpu_custom_call" | custom-call | flops 1400000000 | bytes 2400000 | tf_op jit(solution)/shard_map/attend/pallas_call | solution.py:146
  11.1 0.0 copy-start
  11.1 7.8 %all-to-all-start = ((bf16[16,32,512]{2,1,0:T(8,128)(2,1)}), bf16[16,32,512]{2,1,0:T(8,128)(2,1)S(1)}, u32[]{:S(2)}, u32[]{:S(2)}) async-start(bf16[16,32,512]{2,1,0:T(8,128)(2,1)} %bitcast.27), calls=%async_computation | async-start | bytes 1048576 | tf_op jit(solution)/shard_map/all_to_all | solution.py:477
  18.9 0.0 collective-permute-done.2.refs_4_.three
  18.9 0.0 copy-start.1
  18.9 3.0 %collective-permute-start.3 = (bf16[64,2304]{1,0:T(8,128)(2,1)S(1)}, bf16[64,2304]{1,0:T(8,128)(2,1)S(1)}, u32[]{:S(2)}, u32[]{:S(2)}) collective-permute-start(bf16[64,2304]{1,0:T(8,128)(2,1)S(1)} %slice.41), channel_id=1, source_target_pairs={{0,3},{1,0},{2,1},{3,2},{4,7},{5,4},{6,5},{7,6},{8,11},{9,8},{10,9... | collective-permute-start | bytes 884744 | tf_op jit(solution)/shard_map/ppermute | solution.py:437
  21.9 0.0 collective-permute-done.refs_1_.one
  22.0 0.1 collective-permute-start.1
  22.0 4.6 %collective-permute-done.3.refs_3_.bottom = bf16[64,2304]{1,0:T(8,128)(2,1)S(1)} collective-permute-done((bf16[64,2304]{1,0:T(8,128)(2,1)S(1)}, bf16[64,2304]{1,0:T(8,128)(2,1)S(1)}, u32[]{:S(2)}, u32[]{:S(2)}) %collective-permute-start.3) | collective-permute-done | bytes 294944 | tf_op jit(solution)/shard_map/ppermute | solution.py:437
  26.7 3.2 %collective-permute-done.1.refs_2_.top = bf16[64,2304]{1,0:T(8,128)(2,1)S(1)} collective-permute-done((bf16[64,2304]{1,0:T(8,128)(2,1)S(1)}, bf16[64,2304]{1,0:T(8,128)(2,1)S(1)}, u32[]{:S(2)}, u32[]{:S(2)}) %collective-permute-start.1) | collective-permute-done | bytes 294944 | tf_op jit(solution)/shard_map/ppermute | solution.py:437
  29.9 0.0 all-to-all-done
  29.9 0.0 copy-done
  29.9 0.9 find_values.1.own_values
  30.8 2.8 %collective-permute-start.4 = (bf16[128,512]{1,0:T(8,128)(2,1)S(1)}, bf16[128,512]{1,0:T(8,128)(2,1)S(1)}, u32[]{:S(2)}, u32[]{:S(2)}) collective-permute-start(bf16[128,512]{1,0:T(8,128)(2,1)S(1)} %find_values.1.own_values), channel_id=1, source_target_pairs={{0,64},{64,0},{1,65},{65,1},{2,66},{66,2},{3,67},{67,3},{4,68},{68... | collective-permute-start | bytes 393224 | tf_op jit(solution)/shard_map/ppermute | solution.py:441
  33.6 0.0 copy-done.1
  33.6 0.4 route.1
  34.0 0.6 collective-permute-done.4.far_values
  34.6 1.6 %project.1 = bf16[256,1792]{1,0:T(8,128)(2,1)} custom-call(bf16[128,512]{1,0:T(8,128)(2,1)S(1)} %find_values.1.own_values, bf16[128,512]{1,0:T(8,128)(2,1)S(1)} %collective-permute-done.4.far_values, bf16[128,2304]{1,0:T(8,128)(2,1)S(1)} %copy-done, bf16[128,2304]{1,0:T(8,128)(2,1)S(1)} %collective-permute-done.refs_1_.one, ...), custom_call_target="tpu_custom_call" | custom-call | flops 600000000 | bytes 3000000 | tf_op jit(solution)/shard_map/project/pallas_call | solution.py:329
  36.2 0.0 copy-start.3
  36.2 8.4 %all-to-all-start.1 = ((bf16[32,8,1792]{2,1,0:T(8,128)(2,1)}), bf16[32,8,1792]{2,1,0:T(8,128)(2,1)S(1)}, u32[]{:S(2)}, u32[]{:S(2)}) async-start(bf16[32,8,1792]{2,1,0:T(8,128)(2,1)} %bitcast.2), calls=%async_computation.1 | async-start | bytes 1835008 | tf_op jit(solution)/shard_map/all_to_all | solution.py:489
  44.7 0.3 collective-permute-start.5
  45.0 14.8 %all-to-all-done.1 = bf16[32,8,1792]{2,1,0:T(8,128)(2,1)S(1)} async-done(((bf16[32,8,1792]{2,1,0:T(8,128)(2,1)}), bf16[32,8,1792]{2,1,0:T(8,128)(2,1)S(1)}, u32[]{:S(2)}, u32[]{:S(2)}) %all-to-all-start.1) | async-done | bytes 917536 | tf_op jit(solution)/shard_map/all_to_all | solution.py:489
  59.8 0.1 convert_reduce_fusion
  60.0 1.2 collective-permute-start.6
  61.2 0.1 collective-permute-start.7
  61.3 0.1 multiply_reduce_fusion
  61.4 0.0 copy-done.3
  61.4 0.1 multiply_convert_fusion
  61.5 0.0 copy-start.2
  61.6 0.7 convert_bitcast_fusion
  62.2 28.8 %all_to_all.20 = bf16[128,8,896]{2,1,0:T(8,128)(2,1)S(1)} all-to-all(bf16[128,8,896]{2,1,0:T(8,128)(2,1)S(1)} %convert_bitcast_fusion), channel_id=1, replica_groups=mesh['core'=2,'z'=4,'x'=4,'y'=4] {'core','z','x','y'}, dimensions={0} | all-to-all | bytes 3670016 | tf_op jit(solution)/shard_map/all_to_all | solution.py:506
  91.1 0.0 copy-done.2
  91.1 0.0 collective-permute-done.5.gate_far
  91.1 0.0 collective-permute-done.6.up_far
  91.1 0.0 collective-permute-done.7.down_far
  91.1 9.2 %expert.1 = bf16[1024,896]{1,0:T(8,128)(2,1)S(1)} custom-call(bf16[1024,896]{1,0:T(8,128)(2,1)S(1)} %bitcast.24, bf16[2,3584,512]{2,1,0:T(8,128)(2,1)} %collective-permute-done.5.gate_far, bf16[2,3584,512]{2,1,0:T(8,128)(2,1)S(1)} %collective-permute-done.6.up_far, bf16[2,512,3584]{2,1,0:T(8,128)(2,1)S(1)} %collective-permute-done.7.down_far, ...), custom_call_target="tpu_custom_call" | custom-call | flops 7500000256 | bytes 26000000 | tf_op jit(solution)/shard_map/expert/pallas_call | solution.py:415
  100.3 31.9 %all_to_all.21 = bf16[128,8,896]{2,1,0:T(8,128)(2,1)S(1)} all-to-all(bf16[128,8,896]{2,1,0:T(8,128)(2,1)S(1)} %bitcast.25), channel_id=1, replica_groups=mesh['core'=2,'z'=4,'x'=4,'y'=4] {'core','z','x','y'}, dimensions={0} | all-to-all | bytes 3670016 | tf_op jit(solution)/shard_map/all_to_all | solution.py:508
  132.2 0.4 fusion
  132.7 0.6 fusion.2
  (6 shorter events, 0.1 us)
Async XLA Ops:
  2.6 16.3 %collective-permute-start.2 = (bf16[128,2304]{1,0:T(8,128)(2,1)}, bf16[128,2304]{1,0:T(8,128)(2,1)S(1)}, u32[]{:S(2)}, u32[]{:S(2)}) collective-permute-start(bf16[128,2304]{1,0:T(8,128)(2,1)} %get-tuple-element.22.refs_0_.own), channel_id=1, source_target_pairs={{0,3},{1,0},{2,1},{3,2},{4,7},{5,4},{6,5},{7,6},{8,11},{9,8},{10,9... | collective-permute-start | bytes 1769480 | tf_op jit(solution)/shard_map/ppermute | solution.py:437
  6.2 15.7 %collective-permute-start = (bf16[128,2304]{1,0:T(8,128)(2,1)}, bf16[128,2304]{1,0:T(8,128)(2,1)S(1)}, u32[]{:S(2)}, u32[]{:S(2)}) collective-permute-start(bf16[128,2304]{1,0:T(8,128)(2,1)} %get-tuple-element.22.refs_0_.own), channel_id=1, source_target_pairs={{0,1},{1,2},{2,3},{3,0},{4,5},{5,6},{6,7},{7,4},{8,9},{9,10},{10,1... | collective-permute-start | bytes 1769480 | tf_op jit(solution)/shard_map/ppermute | solution.py:437
  11.1 18.8 %copy-start = (bf16[128,2304]{1,0:T(8,128)(2,1)S(1)}, bf16[128,2304]{1,0:T(8,128)(2,1)}, u32[]{:S(2)}) copy-start(bf16[128,2304]{1,0:T(8,128)(2,1)} %get-tuple-element.22.refs_0_.own) | copy-start | bytes 1769476
  11.1 18.8 %all-to-all-start = ((bf16[16,32,512]{2,1,0:T(8,128)(2,1)}), bf16[16,32,512]{2,1,0:T(8,128)(2,1)S(1)}, u32[]{:S(2)}, u32[]{:S(2)}) async-start(bf16[16,32,512]{2,1,0:T(8,128)(2,1)} %bitcast.27), calls=%async_computation | async-start | bytes 1048576 | tf_op jit(solution)/shard_map/all_to_all | solution.py:477
  18.9 14.7 %copy-start.1 = (f32[8,128]{1,0:T(8,128)S(1)}, f32[8,128]{1,0:T(8,128)}, u32[]{:S(2)}) copy-start(f32[8,128]{1,0:T(8,128)} %get-tuple-element.27.own_ref) | copy-start | bytes 12292
  18.9 7.8 %collective-permute-start.3 = (bf16[64,2304]{1,0:T(8,128)(2,1)S(1)}, bf16[64,2304]{1,0:T(8,128)(2,1)S(1)}, u32[]{:S(2)}, u32[]{:S(2)}) collective-permute-start(bf16[64,2304]{1,0:T(8,128)(2,1)S(1)} %slice.41), channel_id=1, source_target_pairs={{0,3},{1,0},{2,1},{3,2},{4,7},{5,4},{6,5},{7,6},{8,11},{9,8},{10,9... | collective-permute-start | bytes 884744 | tf_op jit(solution)/shard_map/ppermute | solution.py:437
  22.0 8.0 %collective-permute-start.1 = (bf16[64,2304]{1,0:T(8,128)(2,1)S(1)}, bf16[64,2304]{1,0:T(8,128)(2,1)S(1)}, u32[]{:S(2)}, u32[]{:S(2)}) collective-permute-start(bf16[64,2304]{1,0:T(8,128)(2,1)S(1)} %slice.40), channel_id=1, source_target_pairs={{0,1},{1,2},{2,3},{3,0},{4,5},{5,6},{6,7},{7,4},{8,9},{9,10},{10,1... | collective-permute-start | bytes 884744 | tf_op jit(solution)/shard_map/ppermute | solution.py:437
  30.8 3.8 %collective-permute-start.4 = (bf16[128,512]{1,0:T(8,128)(2,1)S(1)}, bf16[128,512]{1,0:T(8,128)(2,1)S(1)}, u32[]{:S(2)}, u32[]{:S(2)}) collective-permute-start(bf16[128,512]{1,0:T(8,128)(2,1)S(1)} %find_values.1.own_values), channel_id=1, source_target_pairs={{0,64},{64,0},{1,65},{65,1},{2,66},{66,2},{3,67},{67,3},{4,68},{68... | collective-permute-start | bytes 393224 | tf_op jit(solution)/shard_map/ppermute | solution.py:441
  36.2 25.2 %copy-start.3 = (f32[3584]{0:T(1024)S(1)}, f32[3584]{0:T(1024)}, u32[]{:S(2)}) copy-start(f32[3584]{0:T(1024)} %param.20) | copy-start | bytes 43012
  36.2 23.6 %all-to-all-start.1 = ((bf16[32,8,1792]{2,1,0:T(8,128)(2,1)}), bf16[32,8,1792]{2,1,0:T(8,128)(2,1)S(1)}, u32[]{:S(2)}, u32[]{:S(2)}) async-start(bf16[32,8,1792]{2,1,0:T(8,128)(2,1)} %bitcast.2), calls=%async_computation.1 | async-start | bytes 1835008 | tf_op jit(solution)/shard_map/all_to_all | solution.py:489
  44.7 46.4 %collective-permute-start.5 = (bf16[2,3584,512]{2,1,0:T(8,128)(2,1)}, bf16[2,3584,512]{2,1,0:T(8,128)(2,1)}, u32[]{:S(2)}, u32[]{:S(2)}) collective-permute-start(bf16[2,3584,512]{2,1,0:T(8,128)(2,1)} %gate_near), channel_id=1, source_target_pairs={{0,64},{64,0},{1,65},{65,1},{2,66},{66,2},{3,67},{67,3},{4,68},{68... | collective-permute-start | bytes 22020104 | tf_op jit(solution)/shard_map/ppermute | solution.py:441
  60.0 31.1 %collective-permute-start.6 = (bf16[2,3584,512]{2,1,0:T(8,128)(2,1)}, bf16[2,3584,512]{2,1,0:T(8,128)(2,1)S(1)}, u32[]{:S(2)}, u32[]{:S(2)}) collective-permute-start(bf16[2,3584,512]{2,1,0:T(8,128)(2,1)} %up_near), channel_id=1, source_target_pairs={{0,64},{64,0},{1,65},{65,1},{2,66},{66,2},{3,67},{67,3},{4,68},{68... | collective-permute-start | bytes 22020104 | tf_op jit(solution)/shard_map/ppermute | solution.py:441
  61.2 29.9 %collective-permute-start.7 = (bf16[2,512,3584]{2,1,0:T(8,128)(2,1)}, bf16[2,512,3584]{2,1,0:T(8,128)(2,1)S(1)}, u32[]{:S(2)}, u32[]{:S(2)}) collective-permute-start(bf16[2,512,3584]{2,1,0:T(8,128)(2,1)} %down_near), channel_id=1, source_target_pairs={{0,64},{64,0},{1,65},{65,1},{2,66},{66,2},{3,67},{67,3},{4,68},{68... | collective-permute-start | bytes 22020104 | tf_op jit(solution)/shard_map/ppermute | solution.py:441
  61.5 29.5 %copy-start.2 = (bf16[8,3584]{1,0:T(8,128)(2,1)}, bf16[8,3584]{1,0:T(8,128)(2,1)S(1)}, u32[]{:S(2)}) copy-start(bf16[8,3584]{1,0:T(8,128)(2,1)S(1)} %multiply_convert_fusion) | copy-start | bytes 172036

commit v6 on v5

--- a/solution.py
+++ b/solution.py
@@ -483,17 +483,13 @@
     )
     partial = project(own_values, far_values, pieces, half)
 
-    partial, gate_weight = lax.optimization_barrier((partial, gate_weight))
-    far_gate = other_core(gate_weight)
     partial = partial.reshape(2 * planes, seq_count, half)
     collected = lax.all_to_all(partial, ("core",) + PLANE, split_axis=0, concat_axis=0, tiled=True)
     halves = jnp.sum(collected.astype(F32).reshape(2, planes, seq_count, half), axis=1)
     attn_out = jnp.concatenate([halves[0], halves[1]], axis=1)
-    attn_out, up_weight, down_weight = lax.optimization_barrier(
-        (attn_out, up_weight, down_weight)
-    )
     weights = (gate_weight, up_weight, down_weight)
-    far_weights = (far_gate, other_core(up_weight), other_core(down_weight))
+    attn_out, weights = lax.optimization_barrier((attn_out, weights))
+    far_weights = [other_core(w) for w in weights]
     mean_square = jnp.mean(attn_out * attn_out, axis=1, keepdims=True)
     normed = (attn_out * lax.rsqrt(mean_square + EPSILON) * norm_gain).astype(BF16)
     parts = jnp.concatenate(

time: 134 us -> 133 us (level)
  blocking collectives: 60.8 us -> 81.2 us
  waiting for transfers between devices: 23.3 us -> 11 us
  starting transfers between devices: 27.4 us -> 19 us
    all_to_all x0 -> x1, blocking collectives: none -> 23.2 us  [shards(): lax.all_to_all(partial, ('core',) + PLANE, split_axis=0, concat_axis=0, t...]
    all_to_all x1 -> x0, waiting for transfers between devices: 14.8 us -> none  [shards(): lax.all_to_all(partial, ('core',) + PLANE, split_axis=0, concat_axis=0, t...]
    all_to_all x1 -> x0, starting transfers between devices: 8.43 us -> none  [shards(): lax.all_to_all(partial, ('core',) + PLANE, split_axis=0, concat_axis=0, t...]
    ppermute x4, waiting for transfers between devices: 0.58 us -> 3.1 us  [other_core(): return lax.ppermute(array, 'core', SWAP)]
    all_to_all x1, blocking collectives: 31.9 us -> 29.4 us  [shards(): lax.all_to_all(reply.reshape(devices, 8, quarter), ALL, split_axis=0, con...]
  transfers between devices with their start and end apart: 10 -> 9, of which waited for: 4 -> 4; matrix products, arithmetic and copies ran while one was open for 1% -> 1% of each run, Pallas kernels for 4% -> 4%
where the time goes in v6:
time: 133 us; the launch traced here: 132 us
  blocking collectives  81.2 us (61%)
  starting transfers between devices  19 us (14%)
  Pallas kernels  17.8 us (13%)
  waiting for transfers between devices  11 us (8%)
    all_to_all x1, blocking collectives, shards(): lax.all_to_all(reply.reshape(devices, 8, quarter), ALL, split_axis=0, con...  29.4 us
    all_to_all x1, blocking collectives, shards(): lax.all_to_all(outgoing, ALL, split_axis=0, concat_axis=0, tiled=True)  28.5 us
    all_to_all x1, blocking collectives, shards(): lax.all_to_all(partial, ('core',) + PLANE, split_axis=0, concat_axis=0, t...  23.2 us
    pallas_call x1, Pallas kernels, run_expert(): pl.pallas_call(expert_kernel, out_shape=jax.ShapeDtypeStruct(rows.shape,...  9.13 us
    ppermute x4, waiting for transfers between devices, along_y(): lax.ppermute(array, 'y', [(i, (i + step) % SIDE) for i in range(SIDE)])  7.88 us
    all_to_all x1, starting transfers between devices, shards(): lax.all_to_all(outbound, PLANE, split_axis=0, concat_axis=0, tiled=True)  7.75 us
    ppermute x4, starting transfers between devices, along_y(): lax.ppermute(array, 'y', [(i, (i + step) % SIDE) for i in range(SIDE)])  6.74 us
    pallas_call x1, Pallas kernels, attend(): pl.pallas_call(attend_kernel, out_shape=jax.ShapeDtypeStruct((head_count...  4.86 us
  transfers between devices with their start and end apart: 9, of which 4 were waited for; matrix products, arithmetic and copies ran while one was open for 1% of the time, Pallas kernels for 4%

profile of v6, /device:TPU:1, one launch (start us, length us, event | category | flops | bytes accessed | tf_op | source)
XLA Modules:
  0.0 132.1 jit_solution(2315322626496686063)
XLA Ops:
  0.6 1.9 %prepare.1 = (bf16[128,2304]{1,0:T(8,128)(2,1)}, f32[8,128]{1,0:T(8,128)}) custom-call(bf16[128,3584]{1,0:T(8,128)(2,1)} %out_proj.1, bf16[1,512,128]{2,1,0:T(8,128)(2,1)} %value_up.1, s32[8,8]{1,0:T(8,128)} %ids_hbm.1, f32[8,8]{1,0:T(8,128)} %affinity_hbm.1), custom_call_target="tpu_custom_call" | custom-call | bytes 1200000 | tf_op jit(solution)/shard_map/prepare/pallas_call | solution.py:195
  2.6 3.6 %collective-permute-start.2 = (bf16[128,2304]{1,0:T(8,128)(2,1)}, bf16[128,2304]{1,0:T(8,128)(2,1)S(1)}, u32[]{:S(2)}, u32[]{:S(2)}) collective-permute-start(bf16[128,2304]{1,0:T(8,128)(2,1)} %get-tuple-element.21.refs_0_.own), channel_id=1, source_target_pairs={{0,3},{1,0},{2,1},{3,2},{4,7},{5,4},{6,5},{7,6},{8,11},{9,8},{10,9... | collective-permute-start | bytes 1769480 | tf_op jit(solution)/shard_map/ppermute | solution.py:437
  6.2 0.0 collective-permute-start
  6.2 4.9 %attend.1 = bf16[512,512]{1,0:T(8,128)(2,1)} custom-call(s32[1,16]{1,0:T(1,128)} %table_hbm.1, s32[1,8]{1,0:T(1,128)} %length_hbm.1, bf16[8,36864]{1,0:T(8,128)(2,1)} %query_hbm.1, bf16[8,576]{1,0:T(8,128)(2,1)} %fresh_hbm.1, bf16[16,36864]{1,0:T(8,128)(2,1)} %cache_hbm.1), custom_call_target="tpu_custom_call" | custom-call | flops 1400000000 | bytes 2400000 | tf_op jit(solution)/shard_map/attend/pallas_call | solution.py:146
  11.1 0.0 copy-start
  11.1 7.8 %all-to-all-start = ((bf16[16,32,512]{2,1,0:T(8,128)(2,1)}), bf16[16,32,512]{2,1,0:T(8,128)(2,1)S(1)}, u32[]{:S(2)}, u32[]{:S(2)}) async-start(bf16[16,32,512]{2,1,0:T(8,128)(2,1)} %bitcast.28), calls=%async_computation | async-start | bytes 1048576 | tf_op jit(solution)/shard_map/all_to_all | solution.py:477
  18.9 0.0 collective-permute-done.2.refs_4_.three
  18.9 0.0 copy-start.1
  18.9 3.0 %collective-permute-start.3 = (bf16[64,2304]{1,0:T(8,128)(2,1)S(1)}, bf16[64,2304]{1,0:T(8,128)(2,1)S(1)}, u32[]{:S(2)}, u32[]{:S(2)}) collective-permute-start(bf16[64,2304]{1,0:T(8,128)(2,1)S(1)} %slice.41), channel_id=1, source_target_pairs={{0,3},{1,0},{2,1},{3,2},{4,7},{5,4},{6,5},{7,6},{8,11},{9,8},{10,9... | collective-permute-start | bytes 884744 | tf_op jit(solution)/shard_map/ppermute | solution.py:437
  21.9 0.0 collective-permute-done.refs_1_.one
  22.0 0.1 collective-permute-start.1
  22.0 4.6 %collective-permute-done.3.refs_3_.bottom = bf16[64,2304]{1,0:T(8,128)(2,1)S(1)} collective-permute-done((bf16[64,2304]{1,0:T(8,128)(2,1)S(1)}, bf16[64,2304]{1,0:T(8,128)(2,1)S(1)}, u32[]{:S(2)}, u32[]{:S(2)}) %collective-permute-start.3) | collective-permute-done | bytes 294944 | tf_op jit(solution)/shard_map/ppermute | solution.py:437
  26.7 3.2 %collective-permute-done.1.refs_2_.top = bf16[64,2304]{1,0:T(8,128)(2,1)S(1)} collective-permute-done((bf16[64,2304]{1,0:T(8,128)(2,1)S(1)}, bf16[64,2304]{1,0:T(8,128)(2,1)S(1)}, u32[]{:S(2)}, u32[]{:S(2)}) %collective-permute-start.1) | collective-permute-done | bytes 294944 | tf_op jit(solution)/shard_map/ppermute | solution.py:437
  29.9 0.0 all-to-all-done
  29.9 0.0 copy-done
  29.9 0.9 find_values.1.own_values
  30.8 2.8 %collective-permute-start.4 = (bf16[128,512]{1,0:T(8,128)(2,1)S(1)}, bf16[128,512]{1,0:T(8,128)(2,1)S(1)}, u32[]{:S(2)}, u32[]{:S(2)}) collective-permute-start(bf16[128,512]{1,0:T(8,128)(2,1)S(1)} %find_values.1.own_values), channel_id=1, source_target_pairs={{0,64},{64,0},{1,65},{65,1},{2,66},{66,2},{3,67},{67,3},{4,68},{68... | collective-permute-start | bytes 393224 | tf_op jit(solution)/shard_map/ppermute | solution.py:441
  33.6 0.0 copy-done.1
  33.6 0.4 route.1
  34.0 0.6 collective-permute-done.4.far_values
  34.6 0.6 project.1
  35.3 0.0 copy-start.3
  35.3 23.2 %all_to_all.20 = bf16[32,8,1792]{2,1,0:T(8,128)(2,1)S(1)} all-to-all(bf16[32,8,1792]{2,1,0:T(8,128)(2,1)S(1)} %bitcast.26), channel_id=1, replica_groups=mesh['core'=2,'z'=4,'x'=4,'y'=4] {'core','x','z'}, dimensions={0} | all-to-all | bytes 1835008 | tf_op jit(solution)/shard_map/all_to_all | solution.py:487
  58.5 0.1 convert_reduce_fusion
  58.7 1.2 collective-permute-start.5
  59.9 0.1 collective-permute-start.6
  60.0 0.4 collective-permute-start.7
  60.4 0.1 multiply_reduce_fusion
  60.6 0.0 copy-done.3
  60.6 0.1 multiply_convert_fusion
  60.6 0.0 copy-start.2
  60.7 0.7 convert_bitcast_fusion
  61.3 28.5 %all_to_all.21 = bf16[128,8,896]{2,1,0:T(8,128)(2,1)S(1)} all-to-all(bf16[128,8,896]{2,1,0:T(8,128)(2,1)S(1)} %convert_bitcast_fusion), channel_id=1, replica_groups=mesh['core'=2,'z'=4,'x'=4,'y'=4] {'core','z','x','y'}, dimensions={0} | all-to-all | bytes 3670016 | tf_op jit(solution)/shard_map/all_to_all | solution.py:502
  89.9 0.0 copy-done.2
  89.9 0.0 collective-permute-done.5.gate_far
  89.9 0.0 collective-permute-done.6.up_far
  89.9 2.5 %collective-permute-done.7.down_far = bf16[2,512,3584]{2,1,0:T(8,128)(2,1)S(1)} collective-permute-done((bf16[2,512,3584]{2,1,0:T(8,128)(2,1)}, bf16[2,512,3584]{2,1,0:T(8,128)(2,1)S(1)}, u32[]{:S(2)}, u32[]{:S(2)}) %collective-permute-start.7) | collective-permute-done | bytes 7340064 | tf_op jit(solution)/shard_map/ppermute | solution.py:441
  92.4 9.1 %expert.1 = bf16[1024,896]{1,0:T(8,128)(2,1)S(1)} custom-call(bf16[1024,896]{1,0:T(8,128)(2,1)S(1)} %bitcast.24, bf16[2,3584,512]{2,1,0:T(8,128)(2,1)S(1)} %collective-permute-done.5.gate_far, bf16[2,3584,512]{2,1,0:T(8,128)(2,1)S(1)} %collective-permute-done.6.up_far, bf16[2,512,3584]{2,1,0:T(8,128)(2,1)S(1)} %collective-permute-done.7.down_far, ...), custom_call_target="tpu_custom_call" | custom-call | flops 7500000256 | bytes 26000000 | tf_op jit(solution)/shard_map/expert/pallas_call | solution.py:415
  101.5 29.4 %all_to_all.22 = bf16[128,8,896]{2,1,0:T(8,128)(2,1)S(1)} all-to-all(bf16[128,8,896]{2,1,0:T(8,128)(2,1)S(1)} %bitcast.25), channel_id=1, replica_groups=mesh['core'=2,'z'=4,'x'=4,'y'=4] {'core','z','x','y'}, dimensions={0} | all-to-all | bytes 3670016 | tf_op jit(solution)/shard_map/all_to_all | solution.py:504
  131.0 0.4 fusion
  131.4 0.6 fusion.2
  (6 shorter events, 0.1 us)
Async XLA Ops:
  2.6 16.3 %collective-permute-start.2 = (bf16[128,2304]{1,0:T(8,128)(2,1)}, bf16[128,2304]{1,0:T(8,128)(2,1)S(1)}, u32[]{:S(2)}, u32[]{:S(2)}) collective-permute-start(bf16[128,2304]{1,0:T(8,128)(2,1)} %get-tuple-element.21.refs_0_.own), channel_id=1, source_target_pairs={{0,3},{1,0},{2,1},{3,2},{4,7},{5,4},{6,5},{7,6},{8,11},{9,8},{10,9... | collective-permute-start | bytes 1769480 | tf_op jit(solution)/shard_map/ppermute | solution.py:437
  6.2 15.7 %collective-permute-start = (bf16[128,2304]{1,0:T(8,128)(2,1)}, bf16[128,2304]{1,0:T(8,128)(2,1)S(1)}, u32[]{:S(2)}, u32[]{:S(2)}) collective-permute-start(bf16[128,2304]{1,0:T(8,128)(2,1)} %get-tuple-element.21.refs_0_.own), channel_id=1, source_target_pairs={{0,1},{1,2},{2,3},{3,0},{4,5},{5,6},{6,7},{7,4},{8,9},{9,10},{10,1... | collective-permute-start | bytes 1769480 | tf_op jit(solution)/shard_map/ppermute | solution.py:437
  11.1 18.8 %copy-start = (bf16[128,2304]{1,0:T(8,128)(2,1)S(1)}, bf16[128,2304]{1,0:T(8,128)(2,1)}, u32[]{:S(2)}) copy-start(bf16[128,2304]{1,0:T(8,128)(2,1)} %get-tuple-element.21.refs_0_.own) | copy-start | bytes 1769476
  11.1 18.8 %all-to-all-start = ((bf16[16,32,512]{2,1,0:T(8,128)(2,1)}), bf16[16,32,512]{2,1,0:T(8,128)(2,1)S(1)}, u32[]{:S(2)}, u32[]{:S(2)}) async-start(bf16[16,32,512]{2,1,0:T(8,128)(2,1)} %bitcast.28), calls=%async_computation | async-start | bytes 1048576 | tf_op jit(solution)/shard_map/all_to_all | solution.py:477
  18.9 14.7 %copy-start.1 = (f32[8,128]{1,0:T(8,128)S(1)}, f32[8,128]{1,0:T(8,128)}, u32[]{:S(2)}) copy-start(f32[8,128]{1,0:T(8,128)} %get-tuple-element.26.own_ref) | copy-start | bytes 12292
  18.9 7.8 %collective-permute-start.3 = (bf16[64,2304]{1,0:T(8,128)(2,1)S(1)}, bf16[64,2304]{1,0:T(8,128)(2,1)S(1)}, u32[]{:S(2)}, u32[]{:S(2)}) collective-permute-start(bf16[64,2304]{1,0:T(8,128)(2,1)S(1)} %slice.41), channel_id=1, source_target_pairs={{0,3},{1,0},{2,1},{3,2},{4,7},{5,4},{6,5},{7,6},{8,11},{9,8},{10,9... | collective-permute-start | bytes 884744 | tf_op jit(solution)/shard_map/ppermute | solution.py:437
  22.0 8.0 %collective-permute-start.1 = (bf16[64,2304]{1,0:T(8,128)(2,1)S(1)}, bf16[64,2304]{1,0:T(8,128)(2,1)S(1)}, u32[]{:S(2)}, u32[]{:S(2)}) collective-permute-start(bf16[64,2304]{1,0:T(8,128)(2,1)S(1)} %slice.40), channel_id=1, source_target_pairs={{0,1},{1,2},{2,3},{3,0},{4,5},{5,6},{6,7},{7,4},{8,9},{9,10},{10,1... | collective-permute-start | bytes 884744 | tf_op jit(solution)/shard_map/ppermute | solution.py:437
  30.8 3.8 %collective-permute-start.4 = (bf16[128,512]{1,0:T(8,128)(2,1)S(1)}, bf16[128,512]{1,0:T(8,128)(2,1)S(1)}, u32[]{:S(2)}, u32[]{:S(2)}) collective-permute-start(bf16[128,512]{1,0:T(8,128)(2,1)S(1)} %find_values.1.own_values), channel_id=1, source_target_pairs={{0,64},{64,0},{1,65},{65,1},{2,66},{66,2},{3,67},{67,3},{4,68},{68... | collective-permute-start | bytes 393224 | tf_op jit(solution)/shard_map/ppermute | solution.py:441
  35.3 25.3 %copy-start.3 = (f32[3584]{0:T(1024)S(1)}, f32[3584]{0:T(1024)}, u32[]{:S(2)}) copy-start(f32[3584]{0:T(1024)} %param.20) | copy-start | bytes 43012
  58.7 31.2 %collective-permute-start.5 = (bf16[2,3584,512]{2,1,0:T(8,128)(2,1)}, bf16[2,3584,512]{2,1,0:T(8,128)(2,1)S(1)}, u32[]{:S(2)}, u32[]{:S(2)}) collective-permute-start(bf16[2,3584,512]{2,1,0:T(8,128)(2,1)} %gate_near), channel_id=1, source_target_pairs={{0,64},{64,0},{1,65},{65,1},{2,66},{66,2},{3,67},{67,3},{4,68},{68... | collective-permute-start | bytes 22020104 | tf_op jit(solution)/shard_map/ppermute | solution.py:441
  59.9 30.0 %collective-permute-start.6 = (bf16[2,3584,512]{2,1,0:T(8,128)(2,1)}, bf16[2,3584,512]{2,1,0:T(8,128)(2,1)S(1)}, u32[]{:S(2)}, u32[]{:S(2)}) collective-permute-start(bf16[2,3584,512]{2,1,0:T(8,128)(2,1)} %up_near), channel_id=1, source_target_pairs={{0,64},{64,0},{1,65},{65,1},{2,66},{66,2},{3,67},{67,3},{4,68},{68... | collective-permute-start | bytes 22020104 | tf_op jit(solution)/shard_map/ppermute | solution.py:441
  60.0 32.4 %collective-permute-start.7 = (bf16[2,512,3584]{2,1,0:T(8,128)(2,1)}, bf16[2,512,3584]{2,1,0:T(8,128)(2,1)S(1)}, u32[]{:S(2)}, u32[]{:S(2)}) collective-permute-start(bf16[2,512,3584]{2,1,0:T(8,128)(2,1)} %down_near), channel_id=1, source_target_pairs={{0,64},{64,0},{1,65},{65,1},{2,66},{66,2},{3,67},{67,3},{4,68},{68... | collective-permute-start | bytes 22020104 | tf_op jit(solution)/shard_map/ppermute | solution.py:441
  60.6 29.2 %copy-start.2 = (bf16[8,3584]{1,0:T(8,128)(2,1)}, bf16[8,3584]{1,0:T(8,128)(2,1)S(1)}, u32[]{:S(2)}) copy-start(bf16[8,3584]{1,0:T(8,128)(2,1)S(1)} %multiply_convert_fusion) | copy-start | bytes 172036

commit v7 on v6

--- a/solution.py
+++ b/solution.py
@@ -285,14 +285,14 @@
         head = lax.rem(place_y - k + SIDE, SIDE)
         pick = (source == plane * (SIDE * 8) + head * 8 + seq).astype(F32)
         latent = dot(pick.astype(BF16), arrived).astype(BF16)
-        total = jnp.zeros((tokens, head_rows), F32)
-        for at in range(0, kv_width, head_rows):
-            columns = slice(half + at, half + at + head_rows)
+        blocks = []
+        for at in range(half, half + kv_width, head_rows):
+            columns = slice(at, at + head_rows)
             if k == 2:
-                up = jnp.concatenate([top[:, columns], bottom[:, columns]], axis=0)
+                blocks += [top[:, columns], bottom[:, columns]]
             else:
-                up = (own, one, None, three)[k][:, columns]
-            total = total + dot(latent[:, at : at + head_rows], up)
+                blocks.append((own, one, None, three)[k][:, columns])
+        total = dot(latent, jnp.concatenate(blocks, axis=0))
         out_ref[:, k * head_rows : (k + 1) * head_rows] = total.astype(BF16)
 
 

time: 133 us -> 133 us (level)
  no operation moved by 1% of the time
where the time goes in v7:
time: 133 us; the launch traced here: 132 us
  blocking collectives  81.2 us (61%)
  starting transfers between devices  19 us (14%)
  Pallas kernels  18 us (14%)
  waiting for transfers between devices  11 us (8%)
    all_to_all x1, blocking collectives, shards(): lax.all_to_all(reply.reshape(devices, 8, quarter), ALL, split_axis=0, con...  29.4 us
    all_to_all x1, blocking collectives, shards(): lax.all_to_all(outgoing, ALL, split_axis=0, concat_axis=0, tiled=True)  28.5 us
    all_to_all x1, blocking collectives, shards(): lax.all_to_all(partial, ('core',) + PLANE, split_axis=0, concat_axis=0, t...  23.3 us
    pallas_call x1, Pallas kernels, run_expert(): pl.pallas_call(expert_kernel, out_shape=jax.ShapeDtypeStruct(rows.shape,...  9.13 us
    ppermute x4, waiting for transfers between devices, along_y(): lax.ppermute(array, 'y', [(i, (i + step) % SIDE) for i in range(SIDE)])  7.88 us
    all_to_all x1, starting transfers between devices, shards(): lax.all_to_all(outbound, PLANE, split_axis=0, concat_axis=0, tiled=True)  7.75 us
    ppermute x4, starting transfers between devices, along_y(): lax.ppermute(array, 'y', [(i, (i + step) % SIDE) for i in range(SIDE)])  6.74 us
    pallas_call x1, Pallas kernels, attend(): pl.pallas_call(attend_kernel, out_shape=jax.ShapeDtypeStruct((head_count...  4.86 us
  transfers between devices with their start and end apart: 9, of which 4 were waited for; matrix products, arithmetic and copies ran while one was open for 1% of the time, Pallas kernels for 4%

profile of v7, /device:TPU:1, one launch (start us, length us, event | category | flops | bytes accessed | tf_op | source)
XLA Modules:
  0.0 132.2 jit_solution(1564594674233390740)
XLA Ops:
  0.6 1.9 %prepare.1 = (bf16[128,2304]{1,0:T(8,128)(2,1)}, f32[8,128]{1,0:T(8,128)}) custom-call(bf16[128,3584]{1,0:T(8,128)(2,1)} %out_proj.1, bf16[1,512,128]{2,1,0:T(8,128)(2,1)} %value_up.1, s32[8,8]{1,0:T(8,128)} %ids_hbm.1, f32[8,8]{1,0:T(8,128)} %affinity_hbm.1), custom_call_target="tpu_custom_call" | custom-call | bytes 1200000 | tf_op jit(solution)/shard_map/prepare/pallas_call | solution.py:195
  2.6 3.6 %collective-permute-start.2 = (bf16[128,2304]{1,0:T(8,128)(2,1)}, bf16[128,2304]{1,0:T(8,128)(2,1)S(1)}, u32[]{:S(2)}, u32[]{:S(2)}) collective-permute-start(bf16[128,2304]{1,0:T(8,128)(2,1)} %get-tuple-element.21.refs_0_.own), channel_id=1, source_target_pairs={{0,3},{1,0},{2,1},{3,2},{4,7},{5,4},{6,5},{7,6},{8,11},{9,8},{10,9... | collective-permute-start | bytes 1769480 | tf_op jit(solution)/shard_map/ppermute | solution.py:437
  6.2 0.0 collective-permute-start
  6.2 4.9 %attend.1 = bf16[512,512]{1,0:T(8,128)(2,1)} custom-call(s32[1,16]{1,0:T(1,128)} %table_hbm.1, s32[1,8]{1,0:T(1,128)} %length_hbm.1, bf16[8,36864]{1,0:T(8,128)(2,1)} %query_hbm.1, bf16[8,576]{1,0:T(8,128)(2,1)} %fresh_hbm.1, bf16[16,36864]{1,0:T(8,128)(2,1)} %cache_hbm.1), custom_call_target="tpu_custom_call" | custom-call | flops 1400000000 | bytes 2400000 | tf_op jit(solution)/shard_map/attend/pallas_call | solution.py:146
  11.1 0.0 copy-start
  11.1 7.8 %all-to-all-start = ((bf16[16,32,512]{2,1,0:T(8,128)(2,1)}), bf16[16,32,512]{2,1,0:T(8,128)(2,1)S(1)}, u32[]{:S(2)}, u32[]{:S(2)}) async-start(bf16[16,32,512]{2,1,0:T(8,128)(2,1)} %bitcast.28), calls=%async_computation | async-start | bytes 1048576 | tf_op jit(solution)/shard_map/all_to_all | solution.py:477
  18.9 0.0 collective-permute-done.2.refs_4_.three
  18.9 0.0 copy-start.1
  18.9 3.0 %collective-permute-start.3 = (bf16[64,2304]{1,0:T(8,128)(2,1)S(1)}, bf16[64,2304]{1,0:T(8,128)(2,1)S(1)}, u32[]{:S(2)}, u32[]{:S(2)}) collective-permute-start(bf16[64,2304]{1,0:T(8,128)(2,1)S(1)} %slice.41), channel_id=1, source_target_pairs={{0,3},{1,0},{2,1},{3,2},{4,7},{5,4},{6,5},{7,6},{8,11},{9,8},{10,9... | collective-permute-start | bytes 884744 | tf_op jit(solution)/shard_map/ppermute | solution.py:437
  21.9 0.0 collective-permute-done.refs_1_.one
  22.0 0.1 collective-permute-start.1
  22.0 4.6 %collective-permute-done.3.refs_3_.bottom = bf16[64,2304]{1,0:T(8,128)(2,1)S(1)} collective-permute-done((bf16[64,2304]{1,0:T(8,128)(2,1)S(1)}, bf16[64,2304]{1,0:T(8,128)(2,1)S(1)}, u32[]{:S(2)}, u32[]{:S(2)}) %collective-permute-start.3) | collective-permute-done | bytes 294944 | tf_op jit(solution)/shard_map/ppermute | solution.py:437
  26.7 3.2 %collective-permute-done.1.refs_2_.top = bf16[64,2304]{1,0:T(8,128)(2,1)S(1)} collective-permute-done((bf16[64,2304]{1,0:T(8,128)(2,1)S(1)}, bf16[64,2304]{1,0:T(8,128)(2,1)S(1)}, u32[]{:S(2)}, u32[]{:S(2)}) %collective-permute-start.1) | collective-permute-done | bytes 294944 | tf_op jit(solution)/shard_map/ppermute | solution.py:437
  29.9 0.0 all-to-all-done
  29.9 0.0 copy-done
  29.9 1.0 find_values.1.own_values
  30.9 2.8 %collective-permute-start.4 = (bf16[128,512]{1,0:T(8,128)(2,1)S(1)}, bf16[128,512]{1,0:T(8,128)(2,1)S(1)}, u32[]{:S(2)}, u32[]{:S(2)}) collective-permute-start(bf16[128,512]{1,0:T(8,128)(2,1)S(1)} %find_values.1.own_values), channel_id=1, source_target_pairs={{0,64},{64,0},{1,65},{65,1},{2,66},{66,2},{3,67},{67,3},{4,68},{68... | collective-permute-start | bytes 393224 | tf_op jit(solution)/shard_map/ppermute | solution.py:441
  33.8 0.0 copy-done.1
  33.8 0.4 route.1
  34.2 0.6 collective-permute-done.4.far_values
  34.7 0.6 project.1
  35.4 0.0 copy-start.3
  35.4 23.3 %all_to_all.20 = bf16[32,8,1792]{2,1,0:T(8,128)(2,1)S(1)} all-to-all(bf16[32,8,1792]{2,1,0:T(8,128)(2,1)S(1)} %bitcast.26), channel_id=1, replica_groups=mesh['core'=2,'z'=4,'x'=4,'y'=4] {'core','x','z'}, dimensions={0} | all-to-all | bytes 1835008 | tf_op jit(solution)/shard_map/all_to_all | solution.py:487
  58.7 0.1 convert_reduce_fusion
  58.8 1.2 collective-permute-start.5
  60.0 0.1 collective-permute-start.6
  60.1 0.4 collective-permute-start.7
  60.5 0.1 multiply_reduce_fusion
  60.7 0.0 copy-done.3
  60.7 0.1 multiply_convert_fusion
  60.8 0.0 copy-start.2
  60.8 0.7 convert_bitcast_fusion
  61.5 28.5 %all_to_all.21 = bf16[128,8,896]{2,1,0:T(8,128)(2,1)S(1)} all-to-all(bf16[128,8,896]{2,1,0:T(8,128)(2,1)S(1)} %convert_bitcast_fusion), channel_id=1, replica_groups=mesh['core'=2,'z'=4,'x'=4,'y'=4] {'core','z','x','y'}, dimensions={0} | all-to-all | bytes 3670016 | tf_op jit(solution)/shard_map/all_to_all | solution.py:502
  90.0 0.0 copy-done.2
  90.0 0.0 collective-permute-done.5.gate_far
  90.0 0.0 collective-permute-done.6.up_far
  90.0 2.5 %collective-permute-done.7.down_far = bf16[2,512,3584]{2,1,0:T(8,128)(2,1)S(1)} collective-permute-done((bf16[2,512,3584]{2,1,0:T(8,128)(2,1)}, bf16[2,512,3584]{2,1,0:T(8,128)(2,1)S(1)}, u32[]{:S(2)}, u32[]{:S(2)}) %collective-permute-start.7) | collective-permute-done | bytes 7340064 | tf_op jit(solution)/shard_map/ppermute | solution.py:441
  92.5 9.1 %expert.1 = bf16[1024,896]{1,0:T(8,128)(2,1)S(1)} custom-call(bf16[1024,896]{1,0:T(8,128)(2,1)S(1)} %bitcast.24, bf16[2,3584,512]{2,1,0:T(8,128)(2,1)S(1)} %collective-permute-done.5.gate_far, bf16[2,3584,512]{2,1,0:T(8,128)(2,1)S(1)} %collective-permute-done.6.up_far, bf16[2,512,3584]{2,1,0:T(8,128)(2,1)S(1)} %collective-permute-done.7.down_far, ...), custom_call_target="tpu_custom_call" | custom-call | flops 7500000256 | bytes 26000000 | tf_op jit(solution)/shard_map/expert/pallas_call | solution.py:415
  101.7 29.4 %all_to_all.22 = bf16[128,8,896]{2,1,0:T(8,128)(2,1)S(1)} all-to-all(bf16[128,8,896]{2,1,0:T(8,128)(2,1)S(1)} %bitcast.25), channel_id=1, replica_groups=mesh['core'=2,'z'=4,'x'=4,'y'=4] {'core','z','x','y'}, dimensions={0} | all-to-all | bytes 3670016 | tf_op jit(solution)/shard_map/all_to_all | solution.py:504
  131.1 0.4 fusion
  131.6 0.6 fusion.2
  (6 shorter events, 0.1 us)
Async XLA Ops:
  2.6 16.3 %collective-permute-start.2 = (bf16[128,2304]{1,0:T(8,128)(2,1)}, bf16[128,2304]{1,0:T(8,128)(2,1)S(1)}, u32[]{:S(2)}, u32[]{:S(2)}) collective-permute-start(bf16[128,2304]{1,0:T(8,128)(2,1)} %get-tuple-element.21.refs_0_.own), channel_id=1, source_target_pairs={{0,3},{1,0},{2,1},{3,2},{4,7},{5,4},{6,5},{7,6},{8,11},{9,8},{10,9... | collective-permute-start | bytes 1769480 | tf_op jit(solution)/shard_map/ppermute | solution.py:437
  6.2 15.7 %collective-permute-start = (bf16[128,2304]{1,0:T(8,128)(2,1)}, bf16[128,2304]{1,0:T(8,128)(2,1)S(1)}, u32[]{:S(2)}, u32[]{:S(2)}) collective-permute-start(bf16[128,2304]{1,0:T(8,128)(2,1)} %get-tuple-element.21.refs_0_.own), channel_id=1, source_target_pairs={{0,1},{1,2},{2,3},{3,0},{4,5},{5,6},{6,7},{7,4},{8,9},{9,10},{10,1... | collective-permute-start | bytes 1769480 | tf_op jit(solution)/shard_map/ppermute | solution.py:437
  11.1 18.8 %copy-start = (bf16[128,2304]{1,0:T(8,128)(2,1)S(1)}, bf16[128,2304]{1,0:T(8,128)(2,1)}, u32[]{:S(2)}) copy-start(bf16[128,2304]{1,0:T(8,128)(2,1)} %get-tuple-element.21.refs_0_.own) | copy-start | bytes 1769476
  11.1 18.8 %all-to-all-start = ((bf16[16,32,512]{2,1,0:T(8,128)(2,1)}), bf16[16,32,512]{2,1,0:T(8,128)(2,1)S(1)}, u32[]{:S(2)}, u32[]{:S(2)}) async-start(bf16[16,32,512]{2,1,0:T(8,128)(2,1)} %bitcast.28), calls=%async_computation | async-start | bytes 1048576 | tf_op jit(solution)/shard_map/all_to_all | solution.py:477
  18.9 14.9 %copy-start.1 = (f32[8,128]{1,0:T(8,128)S(1)}, f32[8,128]{1,0:T(8,128)}, u32[]{:S(2)}) copy-start(f32[8,128]{1,0:T(8,128)} %get-tuple-element.26.own_ref) | copy-start | bytes 12292
  18.9 7.8 %collective-permute-start.3 = (bf16[64,2304]{1,0:T(8,128)(2,1)S(1)}, bf16[64,2304]{1,0:T(8,128)(2,1)S(1)}, u32[]{:S(2)}, u32[]{:S(2)}) collective-permute-start(bf16[64,2304]{1,0:T(8,128)(2,1)S(1)} %slice.41), channel_id=1, source_target_pairs={{0,3},{1,0},{2,1},{3,2},{4,7},{5,4},{6,5},{7,6},{8,11},{9,8},{10,9... | collective-permute-start | bytes 884744 | tf_op jit(solution)/shard_map/ppermute | solution.py:437
  22.0 8.0 %collective-permute-start.1 = (bf16[64,2304]{1,0:T(8,128)(2,1)S(1)}, bf16[64,2304]{1,0:T(8,128)(2,1)S(1)}, u32[]{:S(2)}, u32[]{:S(2)}) collective-permute-start(bf16[64,2304]{1,0:T(8,128)(2,1)S(1)} %slice.40), channel_id=1, source_target_pairs={{0,1},{1,2},{2,3},{3,0},{4,5},{5,6},{6,7},{7,4},{8,9},{9,10},{10,1... | collective-permute-start | bytes 884744 | tf_op jit(solution)/shard_map/ppermute | solution.py:437
  30.9 3.8 %collective-permute-start.4 = (bf16[128,512]{1,0:T(8,128)(2,1)S(1)}, bf16[128,512]{1,0:T(8,128)(2,1)S(1)}, u32[]{:S(2)}, u32[]{:S(2)}) collective-permute-start(bf16[128,512]{1,0:T(8,128)(2,1)S(1)} %find_values.1.own_values), channel_id=1, source_target_pairs={{0,64},{64,0},{1,65},{65,1},{2,66},{66,2},{3,67},{67,3},{4,68},{68... | collective-permute-start | bytes 393224 | tf_op jit(solution)/shard_map/ppermute | solution.py:441
  35.4 25.3 %copy-start.3 = (f32[3584]{0:T(1024)S(1)}, f32[3584]{0:T(1024)}, u32[]{:S(2)}) copy-start(f32[3584]{0:T(1024)} %param.20) | copy-start | bytes 43012
  58.8 31.2 %collective-permute-start.5 = (bf16[2,3584,512]{2,1,0:T(8,128)(2,1)}, bf16[2,3584,512]{2,1,0:T(8,128)(2,1)S(1)}, u32[]{:S(2)}, u32[]{:S(2)}) collective-permute-start(bf16[2,3584,512]{2,1,0:T(8,128)(2,1)} %gate_near), channel_id=1, source_target_pairs={{0,64},{64,0},{1,65},{65,1},{2,66},{66,2},{3,67},{67,3},{4,68},{68... | collective-permute-start | bytes 22020104 | tf_op jit(solution)/shard_map/ppermute | solution.py:441
  60.0 30.0 %collective-permute-start.6 = (bf16[2,3584,512]{2,1,0:T(8,128)(2,1)}, bf16[2,3584,512]{2,1,0:T(8,128)(2,1)S(1)}, u32[]{:S(2)}, u32[]{:S(2)}) collective-permute-start(bf16[2,3584,512]{2,1,0:T(8,128)(2,1)} %up_near), channel_id=1, source_target_pairs={{0,64},{64,0},{1,65},{65,1},{2,66},{66,2},{3,67},{67,3},{4,68},{68... | collective-permute-start | bytes 22020104 | tf_op jit(solution)/shard_map/ppermute | solution.py:441
  60.1 32.4 %collective-permute-start.7 = (bf16[2,512,3584]{2,1,0:T(8,128)(2,1)}, bf16[2,512,3584]{2,1,0:T(8,128)(2,1)S(1)}, u32[]{:S(2)}, u32[]{:S(2)}) collective-permute-start(bf16[2,512,3584]{2,1,0:T(8,128)(2,1)} %down_near), channel_id=1, source_target_pairs={{0,64},{64,0},{1,65},{65,1},{2,66},{66,2},{3,67},{67,3},{4,68},{68... | collective-permute-start | bytes 22020104 | tf_op jit(solution)/shard_map/ppermute | solution.py:441
  60.8 29.2 %copy-start.2 = (bf16[8,3584]{1,0:T(8,128)(2,1)}, bf16[8,3584]{1,0:T(8,128)(2,1)S(1)}, u32[]{:S(2)}) copy-start(bf16[8,3584]{1,0:T(8,128)(2,1)S(1)} %multiply_convert_fusion) | copy-start | bytes 172036
